TPU v7x, 32 devices: a whole 2x2x4 slice. The times are simulated.
32 devices in a mesh: group: 2 (over y), hid: 4 (over z), wid: 4 (over x, core).
Axes of the slice: x: 2, y: 2, z: 4, core: 2. Of those that a mesh axis runs over, the one named last changes fastest.
Arguments:
- tokens: bfloat16 [256, 8192], P(('group', 'hid'), 'wid'), parts along dimension 0, may hold values from -6 to 6
- gate_weight: bfloat16 [8192, 26624], P('wid', 'hid'), may hold values from -0.0625 to 0.0625
- up_weight: bfloat16 [8192, 26624], P('wid', 'hid'), may hold values from -0.0625 to 0.0625
- down_weight: bfloat16 [26624, 8192], P('hid', 'wid'), may hold values from -0.0390625 to 0.0390625
Outputs:
- mixed: bfloat16 [256, 8192], P(('group', 'hid'), 'wid'), parts along dimension 0
There are 2 independent parts, one for each index of `group`. A program takes and returns all parts, laid end to end along the dimension named above; an argument that names none is the same for every part. Nothing has to cross between parts.
All inputs are finite; a program needn't handle non-finite values.
Results may differ from a plain program's by a relative error of at most 0.005.
Values may be sent and summed in bfloat16 or wider, within the bound.
No kernel may reach another device: no remote copies, remote signals or barrier semaphores. Data moves between devices by JAX's collectives and lax.ppermute only.
A program may use at most 192 MiB of HBM per device.

v0:
```python
import jax
import jax.numpy as jnp
from jax import lax
from jax.sharding import PartitionSpec as P


def body(tokens, gate_weight, up_weight, down_weight):
    gathered = lax.all_gather(tokens, "hid", axis=0, tiled=True)
    gate_part = jnp.dot(gathered, gate_weight, preferred_element_type=jnp.float32)
    up_part = jnp.dot(gathered, up_weight, preferred_element_type=jnp.float32)
    gate, upward = lax.psum((gate_part, up_part), "wid")
    hidden = (jax.nn.silu(gate) * upward).astype(jnp.bfloat16)
    summed = lax.psum_scatter(
        jnp.dot(hidden, down_weight, preferred_element_type=jnp.float32),
        "hid",
        scatter_dimension=0,
        tiled=True,
    )
    return summed.astype(jnp.bfloat16)


def solution(mesh):
    placed = (P(("group", "hid"), "wid"), P("wid", "hid"), P("wid", "hid"), P("hid", "wid"))
    return jax.shard_map(
        body, mesh=mesh, in_specs=placed, out_specs=P(("group", "hid"), "wid"), check_vma=False
    )
```

profile of v0, /device:TPU:0, one launch (start us, length us, event | category | flops | bytes accessed | tf_op | source)
XLA Modules:
  0.0 234.5 jit_solution(2388682358263931335)
XLA Ops:
  6.5 0.0 all-reduce.3.cloned.1.call-start
  6.5 17.6 %all_gather.3 = bf16[128,2048]{1,0:T(8,128)(2,1)S(1)} all-gather(bf16[32,2048]{1,0:T(8,128)(2,1)} %param.4), channel_id=1, replica_groups=mesh['group'=2,'hid'=4,'wid'=4] {'hid'}, dimensions={0}, use_global_device_ids=true | all-gather | bytes 655360 | tf_op jit(solution)/shard_map/all_gather | solution.py:8
  24.1 14.3 %fusion.4 = f32[128,6656]{1,0:T(8,128)} fusion(bf16[128,2048]{1,0:T(8,128)(2,1)S(1)} %all_gather.3, bf16[2048,6656]{1,0:T(8,128)(2,1)} %param.6), kind=kOutput, calls=%fused_computation.5 | convolution fusion | flops 3489660928 | bytes 31195136 | tf_op jit(solution)/shard_map/dot_general | solution.py:10
  38.4 14.3 %fusion.3 = f32[128,6656]{1,0:T(8,128)} fusion(bf16[128,2048]{1,0:T(8,128)(2,1)S(1)} %all_gather.3, bf16[2048,6656]{1,0:T(8,128)(2,1)} %param.5), kind=kOutput, calls=%fused_computation.4 | convolution fusion | flops 3489660928 | bytes 31195136 | tf_op jit(solution)/shard_map/dot_general | solution.py:9
  52.7 0.0 all-reduce.3.cloned.1.call-update
  52.7 0.0 reduce-scatter.2.cloned.1.call-start
  52.7 130.2 %all-reduce.3.cloned.1.call-done = (f32[128,6656]{1,0:T(8,128)}, f32[128,6656]{1,0:T(8,128)}) async-done(((f32[128,6656]{1,0:T(8,128)}, f32[128,6656]{1,0:T(8,128)}), (f32[128,6656]{1,0:T(8,128)}, f32[128,6656]{1,0:T(8,128)})) %all-reduce.3.cloned.1.call-update) | async-done | bytes 6815760 | tf_op jit(solution)/shard_map/psum | solution.py:11
  182.9 15.6 %fusion = f32[128,2048]{1,0:T(8,128)} fusion(bf16[6656,2048]{1,0:T(8,128)(2,1)} %param.7, f32[128,6656]{1,0:T(8,128)} %get-tuple-element.5, f32[128,6656]{1,0:T(8,128)} %get-tuple-element.6), kind=kOutput, calls=%fused_computation.1 | convolution fusion | flops 3494772736 | bytes 35127296 | tf_op jit(solution)/shard_map/dot_general | solution.py:14
  198.5 0.0 reduce-scatter.2.cloned.1.call-update
  198.6 27.5 %reduce-scatter.2.cloned.1.call-done = f32[32,2048]{1,0:T(8,128)} async-done(((f32[128,2048]{1,0:T(8,128)}), f32[32,2048]{1,0:T(8,128)}) %reduce-scatter.2.cloned.1.call-update) | async-done | bytes 262160 | tf_op jit(solution)/shard_map/reduce_scatter | solution.py:13
  226.1 1.6 convert_element_type.7
Async XLA Ops:
  6.5 176.4 %all-reduce.3.cloned.1.call-start = ((), (), s32[]{:S(2)}) async-start(), calls=%async_computation.2 | async-start | bytes 13631488 | tf_op jit(solution)/shard_map/psum | solution.py:11
  52.7 173.4 %reduce-scatter.2.cloned.1.call-start = ((), (), s32[]{:S(2)}) async-start(), calls=%async_computation.1 | async-start | bytes 1310720 | tf_op jit(solution)/shard_map/reduce_scatter | solution.py:13
Sparse Core Ops, SparseCore 0:
  52.8 130.0 all-reduce.2
  198.7 27.3 reduce-scatter.1
where the time goes:
time: 235 us
  waiting for transfers between devices  158 us (67%)
  matrix products  44.2 us (19%)
  blocking collectives  17.6 us (7%)
  between operations  13.4 us (6%)
    psum x1, waiting for transfers between devices, body(): gate, upward = lax.psum((gate_part, up_part), 'wid')  130 us
    reduce_scatter x1, waiting for transfers between devices, body(): lax.psum_scatter(jnp.dot(hidden, down_weight, preferred_element_type=jnp....  27.5 us
    all_gather x1, blocking collectives, body(): gathered = lax.all_gather(tokens, 'hid', axis=0, tiled=True)  17.6 us
    dot_general x1, matrix products, body(): jnp.dot(hidden, down_weight, preferred_element_type=jnp.float32)  15.6 us
    dot_general x1, matrix products, body(): jnp.dot(gathered, gate_weight, preferred_element_type=jnp.float32)  14.3 us
    dot_general x1, matrix products, body(): up_part = jnp.dot(gathered, up_weight, preferred_element_type=jnp.float32)  14.3 us
  transfers between devices with their start and end apart: 2, of which 2 were waited for; matrix products, arithmetic and copies ran while one was open for 0% of the time, Pallas kernels for 0%

commit v1 on v0

v1 whole, which is shorter than its diff:
```python
import functools

import jax
import jax.numpy as jnp
from jax import lax
from jax.experimental import pallas as pl
from jax.experimental.pallas import tpu as pltpu
from jax.sharding import PartitionSpec as P

MIB = 1 << 20
WHOLE = pl.BlockSpec(memory_space=pltpu.VMEM)
STAY = pl.BlockSpec(memory_space=pl.ANY)


def largest(total, options):
    return next(o for o in options if total % o == 0)


def call(kernel, ins, outs, scratch, flops, moved, limit):
    return pl.pallas_call(
        kernel,
        in_specs=ins,
        out_specs=[WHOLE] * len(outs),
        out_shape=outs,
        scratch_shapes=scratch,
        compiler_params=pltpu.CompilerParams(vmem_limit_bytes=limit),
        cost_estimate=pl.CostEstimate(flops=flops, bytes_accessed=moved, transcendentals=0),
    )


def gate_up_kernel(start, width, depth, slots, blocks, *refs):
    parts, (gate_ref, up_ref, send_ref, keep_ref, left, held, sems) = refs[:blocks], refs[blocks:]
    steps = left.shape[1] // depth
    total = 2 * steps

    def copy(i):
        source = (gate_ref, up_ref)[i % 2]
        slot = i % slots
        return pltpu.make_async_copy(
            source.at[pl.ds(i // 2 * depth, depth), pl.ds(start, width)], held.at[slot], sems.at[slot]
        )

    for i in range(min(slots, total)):
        copy(i).start()
    rows = parts[0].shape[0]
    half = left.shape[0] // 2
    other = 1 - lax.rem(lax.axis_index("wid"), 2)
    for j, part in enumerate(parts):
        at = lax.rem(j * rows + other * half, 2 * half)
        left[pl.ds(pl.multiple_of(at, rows), rows), :] = part[...]
    sums = [None, None]
    for i in range(total):
        copy(i).wait()
        product = jnp.dot(
            left[:, pl.ds(i // 2 * depth, depth)], held[i % slots], preferred_element_type=jnp.float32
        )
        sums[i % 2] = product if i < 2 else sums[i % 2] + product
        if i + slots < total:
            copy(i + slots).start()
    for which in range(2):
        send_ref[which] = sums[which][:half].astype(jnp.bfloat16)
        keep_ref[which] = sums[which][half:]


def chip_sum_kernel(count, keep_ref, came_ref, own_ref, *send_refs):
    rows = own_ref.shape[1]
    me = lax.axis_index("wid") // 2
    for j in range(count):
        at = pl.ds(pl.multiple_of(lax.rem(me + j, count) * rows, rows), rows)
        for which in range(2):
            value = keep_ref[which, at, :] + came_ref[which, at, :].astype(jnp.float32)
            if j == 0:
                own_ref[which] = value
            else:
                send_refs[j - 1][which] = value.astype(jnp.bfloat16)


def hidden_kernel(own_ref, *refs):
    came_refs, hidden_ref = refs[:-1], refs[-1]
    gate, up = own_ref[0], own_ref[1]
    for came in came_refs:
        gate = gate + came[0].astype(jnp.float32)
        up = up + came[1].astype(jnp.float32)
    hidden_ref[...] = (gate / (1.0 + jnp.exp(-gate)) * up).astype(jnp.bfloat16)


def down_kernel(start, depth, slots, count, first, last, *refs):
    pieces, refs = refs[: 2 * count], refs[2 * count :]
    if not first:
        before_ref, refs = refs[0], refs[1:]
    down_ref, refs = refs[0], refs[1:]
    outs, (left, held, sems) = refs[:-3], refs[-3:]
    total = left.shape[1] // depth

    def copy(i):
        slot = i % slots
        return pltpu.make_async_copy(down_ref.at[pl.ds(start + i * depth, depth), :], held.at[slot], sems.at[slot])

    for i in range(min(slots, total)):
        copy(i).start()
    rows = pieces[0].shape[0]
    half = left.shape[0] // 2
    x, core = lax.axis_index("wid") // 2, lax.rem(lax.axis_index("wid"), 2)
    for side in range(2):
        for j in range(count):
            base = (core if side == 0 else 1 - core) * half
            at = base + lax.rem(x - j + count, count) * rows
            left[pl.ds(pl.multiple_of(at, rows), rows), :] = pieces[side * count + j][...]
    value = None if first else before_ref[...]
    for i in range(total):
        copy(i).wait()
        product = jnp.dot(left[:, pl.ds(i * depth, depth)], held[i % slots], preferred_element_type=jnp.float32)
        value = product if value is None else value + product
        if i + slots < total:
            copy(i + slots).start()
    if not last:
        outs[0][...] = value
    else:
        rows = outs[0].shape[0]
        for j, out in enumerate(outs):
            out[...] = value[j * rows : (j + 1) * rows].astype(out.dtype)


def final_kernel(own_ref, *refs):
    value = own_ref[...]
    for came in refs[:-1]:
        value = value + came[...].astype(jnp.float32)
    refs[-1][...] = value.astype(refs[-1].dtype)


def body(groups, wide, tokens, gate_weight, up_weight, down_weight):
    chips = wide // 2
    f32, bf16 = jnp.float32, jnp.bfloat16
    shape = jax.ShapeDtypeStruct
    part, width = tokens.shape
    units = gate_weight.shape[1]
    rows = part * groups
    own_rows = rows // wide

    other_core = [(w, w ^ 1) for w in range(wide)]

    def along_x(value, j):
        return lax.ppermute(value, "wid", [(w, (w // 2 + j) % chips * 2 + w % 2) for w in range(wide)])

    def along_z(value, j):
        return lax.ppermute(value, "hid", [(z, (z + j) % groups) for z in range(groups)])

    step = units // 26 if units // 26 % 128 == 0 else units // 13
    count = units // step
    cuts = [0, count * 6 // 26, count * 16 // 26, count]
    chunks = [(a * step, (b - a) * step) for a, b in zip(cuts[:-1], cuts[1:])]

    parts = [tokens] + [along_z(tokens, groups - j) for j in range(1, groups)]

    summed = []
    for start, size in chunks:
        depth = largest(width, (512, 256))
        slots = 6
        send, keep = call(
            functools.partial(gate_up_kernel, start, size, depth, slots, groups),
            [WHOLE] * groups + [STAY] * 2,
            [shape((2, rows // 2, size), bf16), shape((2, rows // 2, size), f32)],
            [pltpu.VMEM((rows, width), bf16), pltpu.VMEM((slots, depth, size), bf16), pltpu.SemaphoreType.DMA((slots,))],
            4 * rows * width * size,
            4 * width * size,
            34 * MIB,
        )(*parts, gate_weight, up_weight)
        came = lax.ppermute(send, "wid", other_core)
        summed.append((keep, came))

    hidden = []
    for (keep, came), (start, size) in zip(summed, chunks):
        own, *sends = call(
            functools.partial(chip_sum_kernel, chips),
            [WHOLE] * 2,
            [shape((2, own_rows, size), f32)] + [shape((2, own_rows, size), bf16)] * (chips - 1),
            [],
            rows * size,
            4 * rows * size,
            24 * MIB,
        )(keep, came)
        arrived = [along_x(sends[j - 1], j) for j in range(1, chips)]
        (mine,) = call(
            hidden_kernel, [WHOLE] * chips, [shape((own_rows, size), bf16)], [], own_rows * size * 8, 8 * own_rows * size, 24 * MIB
        )(own, *arrived)
        near = [mine] + [along_x(mine, j) for j in range(1, chips)]
        far = [lax.ppermute(v, "wid", other_core) for v in near]
        hidden.append(near + far)

    value = []
    for n, (pieces, (start, size)) in enumerate(zip(hidden, chunks)):
        first, last = n == 0, n == len(chunks) - 1
        depth = largest(size, (512, 256, 128))
        slots = 5
        outs = [shape((part, width), f32)] + [shape((part, width), bf16)] * (groups - 1) if last else [shape((rows, width), f32)]
        value = call(
            functools.partial(down_kernel, start, depth, slots, chips, first, last),
            [WHOLE] * (len(pieces) + len(value)) + [STAY],
            outs,
            [pltpu.VMEM((rows, size), bf16), pltpu.VMEM((slots, depth, width), bf16), pltpu.SemaphoreType.DMA((slots,))],
            2 * rows * width * size,
            2 * width * size,
            28 * MIB,
        )(*pieces, *value, down_weight)

    arrived = [along_z(value[j], j) for j in range(1, groups)]
    (mixed,) = call(final_kernel, [WHOLE] * groups, [shape((part, width), bf16)], [], groups * part * width, 4 * groups * part * width, 16 * MIB)(
        value[0], *arrived
    )
    return mixed


def solution(mesh):
    placed = (P(("group", "hid"), "wid"), P("wid", "hid"), P("wid", "hid"), P("hid", "wid"))
    return jax.shard_map(
        functools.partial(body, mesh.shape["hid"], mesh.shape["wid"]),
        mesh=mesh,
        in_specs=placed,
        out_specs=P(("group", "hid"), "wid"),
        check_vma=False,
    )
```

time: 235 us -> 96.8 us (0.41)
  waiting for transfers between devices: 158 us -> 39.8 us
  matrix products: 44.2 us -> 0 us
  Pallas kernels: 0 us -> 35 us
  starting transfers between devices: 0.04 us -> 20.8 us
  blocking collectives: 17.6 us -> 0 us
  between operations: 13.4 us -> 0.13 us
    psum x1 -> x0, waiting for transfers between devices: 130 us -> none  [body(): gate, upward = lax.psum((gate_part, up_part), 'wid')]
    dot_general x3 -> x0, matrix products: 44.2 us -> none  [the longest x1 15.6 us: body(): jnp.dot(hidden, down_weight, preferred_element_type=jnp.float32)]
    ppermute x0 -> x21, waiting for transfers between devices: none -> 39.8 us  [the longest x6 21.5 us: along_x(): lax.ppermute(value, 'wid', [(w, (w // 2 + j) % chips * 2 + w % 2) for w i...]
    pallas_call x0 -> x13, Pallas kernels: none -> 35 us  [the longest x3 21.2 us: body(): call(functools.partial(gate_up_kernel, start, size, depth, slots, groups)...]
    reduce_scatter x1 -> x0, waiting for transfers between devices: 27.5 us -> none  [body(): lax.psum_scatter(jnp.dot(hidden, down_weight, preferred_element_type=jnp....]
    ppermute x0 -> x21, starting transfers between devices: none -> 20.8 us  [the longest x6 11.7 us: along_z(): lax.ppermute(value, 'hid', [(z, (z + j) % groups) for z in range(groups)])]
    all_gather x1 -> x0, blocking collectives: 17.6 us -> none  [body(): gathered = lax.all_gather(tokens, 'hid', axis=0, tiled=True)]
  transfers between devices with their start and end apart: 2 -> 21, of which waited for: 2 -> 8; matrix products, arithmetic and copies ran while one was open for 0% -> 0% of each run, Pallas kernels for 0% -> 23%
where the time goes in v1:
time: 96.8 us; the launch traced here: 96.7 us
  waiting for transfers between devices  39.8 us (41%)
  Pallas kernels  35 us (36%)
  starting transfers between devices  20.8 us (21%)
    ppermute x6, waiting for transfers between devices, along_x(): lax.ppermute(value, 'wid', [(w, (w // 2 + j) % chips * 2 + w % 2) for w i...  21.5 us
    pallas_call x3, Pallas kernels, body(): call(functools.partial(gate_up_kernel, start, size, depth, slots, groups)...  21.2 us
    ppermute x6, waiting for transfers between devices, along_z(): lax.ppermute(value, 'hid', [(z, (z + j) % groups) for z in range(groups)])  18.3 us
    pallas_call x3, Pallas kernels, body(): call(functools.partial(down_kernel, start, depth, slots, chips, first, la...  12.5 us
    ppermute x6, starting transfers between devices, along_z(): lax.ppermute(value, 'hid', [(z, (z + j) % groups) for z in range(groups)])  11.7 us
    ppermute x6, starting transfers between devices, along_x(): lax.ppermute(value, 'wid', [(w, (w // 2 + j) % chips * 2 + w % 2) for w i...  7.44 us
  transfers between devices with their start and end apart: 21, of which 8 were waited for; matrix products, arithmetic and copies ran while one was open for 0% of the time, Pallas kernels for 23%

profile of v1, /device:TPU:0, one launch (start us, length us, event | category | flops | bytes accessed | tf_op | source)
XLA Modules:
  0.0 96.7 jit_solution(11750821446817172225)
XLA Ops:
  0.0 5.0 %collective-permute-start = (bf16[32,2048]{1,0:T(8,128)(2,1)}, bf16[32,2048]{1,0:T(8,128)(2,1)S(1)}, u32[]{:S(2)}, u32[]{:S(2)}) collective-permute-start(bf16[32,2048]{1,0:T(8,128)(2,1)} %refs_0_.5), channel_id=1, source_target_pairs={{0,12},{4,0},{8,4},{12,8},{1,13},{5,1},{9,5},{13,9},{2,14},{6,2},{... | collective-permute-start | bytes 393224 | tf_op jit(solution)/shard_map/ppermute | solution.py:146
  5.1 1.0 %collective-permute-start.2 = (bf16[32,2048]{1,0:T(8,128)(2,1)}, bf16[32,2048]{1,0:T(8,128)(2,1)S(1)}, u32[]{:S(2)}, u32[]{:S(2)}) collective-permute-start(bf16[32,2048]{1,0:T(8,128)(2,1)} %refs_0_.5), channel_id=1, source_target_pairs={{0,4},{4,8},{8,12},{12,0},{1,5},{5,9},{9,13},{13,1},{2,6},{6,10},{... | collective-permute-start | bytes 393224 | tf_op jit(solution)/shard_map/ppermute | solution.py:146
  6.1 3.2 %collective-permute-done.refs_1_ = bf16[32,2048]{1,0:T(8,128)(2,1)S(1)} collective-permute-done((bf16[32,2048]{1,0:T(8,128)(2,1)}, bf16[32,2048]{1,0:T(8,128)(2,1)S(1)}, u32[]{:S(2)}, u32[]{:S(2)}) %collective-permute-start) | collective-permute-done | bytes 131104 | tf_op jit(solution)/shard_map/ppermute | solution.py:146
  9.3 7.2 %collective-permute-done.1.refs_2_ = bf16[32,2048]{1,0:T(8,128)(2,1)S(1)} collective-permute-done((bf16[32,2048]{1,0:T(8,128)(2,1)}, bf16[32,2048]{1,0:T(8,128)(2,1)S(1)}, u32[]{:S(2)}, u32[]{:S(2)}) %collective-permute-start.1) | collective-permute-done | bytes 131104 | tf_op jit(solution)/shard_map/ppermute | solution.py:146
  16.5 0.9 copy-done
  17.4 7.9 %shard_map.49 = (bf16[2,64,2560]{2,1,0:T(8,128)(2,1)S(1)}, f32[2,64,2560]{2,1,0:T(8,128)S(1)}) custom-call(bf16[32,2048]{1,0:T(8,128)(2,1)S(1)} %copy-done, bf16[32,2048]{1,0:T(8,128)(2,1)S(1)} %collective-permute-done.refs_1_, bf16[32,2048]{1,0:T(8,128)(2,1)S(1)} %collective-permute-done.1.refs_2_, bf16[32,2048]{1,0:T(8,128)(2,1)S(1)} %collective-permute-done.2.refs_3_, ...), custom_call_target="tpu_custom_call" | custom-call | flops 2684354560 | bytes 20971520 | tf_op jit(solution)/shard_map/pallas_call | solution.py:159
  25.4 7.9 %shard_map.46 = (bf16[2,64,2560]{2,1,0:T(8,128)(2,1)S(1)}, f32[2,64,2560]{2,1,0:T(8,128)S(1)}) custom-call(bf16[32,2048]{1,0:T(8,128)(2,1)S(1)} %copy-done, bf16[32,2048]{1,0:T(8,128)(2,1)S(1)} %collective-permute-done.refs_1_, bf16[32,2048]{1,0:T(8,128)(2,1)S(1)} %collective-permute-done.1.refs_2_, bf16[32,2048]{1,0:T(8,128)(2,1)S(1)} %collective-permute-done.2.refs_3_, ...), custom_call_target="tpu_custom_call" | custom-call | flops 2684354560 | bytes 20971520 | tf_op jit(solution)/shard_map/pallas_call | solution.py:159
  33.3 0.6 collective-permute-start.3
  33.8 5.3 %shard_map.52 = (bf16[2,64,1536]{2,1,0:T(8,128)(2,1)S(1)}, f32[2,64,1536]{2,1,0:T(8,128)S(1)}) custom-call(bf16[32,2048]{1,0:T(8,128)(2,1)S(1)} %copy-done, bf16[32,2048]{1,0:T(8,128)(2,1)S(1)} %collective-permute-done.refs_1_, bf16[32,2048]{1,0:T(8,128)(2,1)S(1)} %collective-permute-done.1.refs_2_, bf16[32,2048]{1,0:T(8,128)(2,1)S(1)} %collective-permute-done.2.refs_3_, ...), custom_call_target="tpu_custom_call" | custom-call | flops 1610612736 | bytes 12582912 | tf_op jit(solution)/shard_map/pallas_call | solution.py:159
  39.4 1.6 %collective-permute-start.9 = (bf16[2,32,2560]{2,1,0:T(8,128)(2,1)S(1)}, bf16[2,32,2560]{2,1,0:T(8,128)(2,1)S(1)}, u32[]{:S(2)}, u32[]{:S(2)}) collective-permute-start(bf16[2,32,2560]{2,1,0:T(8,128)(2,1)S(1)} %get-tuple-element.28), channel_id=1, source_target_pairs={{0,2},{1,3},{2,0},{3,1},{4,6},{5,7},{6,4},{7,5},{8,10},{9,11},{10,... | collective-permute-start | bytes 983048 | tf_op jit(solution)/shard_map/ppermute | solution.py:143
  41.1 0.6 collective-permute-start.4
  41.8 1.6 %collective-permute-start.14 = (bf16[2,32,1536]{2,1,0:T(8,128)(2,1)S(1)}, bf16[2,32,1536]{2,1,0:T(8,128)(2,1)S(1)}, u32[]{:S(2)}, u32[]{:S(2)}) collective-permute-start(bf16[2,32,1536]{2,1,0:T(8,128)(2,1)S(1)} %get-tuple-element.32), channel_id=1, source_target_pairs={{0,2},{1,3},{2,0},{3,1},{4,6},{5,7},{6,4},{7,5},{8,10},{9,11},{10,... | collective-permute-start | bytes 589832 | tf_op jit(solution)/shard_map/ppermute | solution.py:143
  43.3 6.7 %collective-permute-done.9.refs_0_ = bf16[2,32,2560]{2,1,0:T(8,128)(2,1)S(1)} collective-permute-done((bf16[2,32,2560]{2,1,0:T(8,128)(2,1)S(1)}, bf16[2,32,2560]{2,1,0:T(8,128)(2,1)S(1)}, u32[]{:S(2)}, u32[]{:S(2)}) %collective-permute-start.9) | collective-permute-done | bytes 327712 | tf_op jit(solution)/shard_map/ppermute | solution.py:143
  50.0 0.1 shard_map.51.refs_0_
  50.1 1.6 %collective-permute-start.10 = (bf16[32,2560]{1,0:T(8,128)(2,1)S(1)}, bf16[32,2560]{1,0:T(8,128)(2,1)S(1)}, u32[]{:S(2)}, u32[]{:S(2)}) collective-permute-start(bf16[32,2560]{1,0:T(8,128)(2,1)S(1)} %shard_map.51.refs_0_), channel_id=1, source_target_pairs={{0,2},{1,3},{2,0},{3,1},{4,6},{5,7},{6,4},{7,5},{8,10},{9,11},{10,... | collective-permute-start | bytes 491528 | tf_op jit(solution)/shard_map/ppermute | solution.py:143
  51.7 9.5 %collective-permute-done.14.refs_0_ = bf16[2,32,1536]{2,1,0:T(8,128)(2,1)S(1)} collective-permute-done((bf16[2,32,1536]{2,1,0:T(8,128)(2,1)S(1)}, bf16[2,32,1536]{2,1,0:T(8,128)(2,1)S(1)}, u32[]{:S(2)}, u32[]{:S(2)}) %collective-permute-start.14) | collective-permute-done | bytes 196640 | tf_op jit(solution)/shard_map/ppermute | solution.py:143
  61.3 1.6 %collective-permute-start.15 = (bf16[32,1536]{1,0:T(8,128)(2,1)S(1)}, bf16[32,1536]{1,0:T(8,128)(2,1)S(1)}, u32[]{:S(2)}, u32[]{:S(2)}) collective-permute-start(bf16[32,1536]{1,0:T(8,128)(2,1)S(1)} %shard_map.54.refs_0_), channel_id=1, source_target_pairs={{0,2},{1,3},{2,0},{3,1},{4,6},{5,7},{6,4},{7,5},{8,10},{9,11},{10,... | collective-permute-start | bytes 294920 | tf_op jit(solution)/shard_map/ppermute | solution.py:143
  62.9 0.1 shard_map.48.refs_0_
  63.0 0.6 collective-permute-start.5
  63.6 3.5 %collective-permute-done.15.refs_1_ = bf16[32,1536]{1,0:T(8,128)(2,1)S(1)} collective-permute-done((bf16[32,1536]{1,0:T(8,128)(2,1)S(1)}, bf16[32,1536]{1,0:T(8,128)(2,1)S(1)}, u32[]{:S(2)}, u32[]{:S(2)}) %collective-permute-start.15) | collective-permute-done | bytes 98336 | tf_op jit(solution)/shard_map/ppermute | solution.py:143
  67.1 0.5 collective-permute-start.11
  67.6 0.5 collective-permute-start.6
  68.1 1.8 %collective-permute-done.5.refs_1_ = bf16[32,2560]{1,0:T(8,128)(2,1)S(1)} collective-permute-done((bf16[32,2560]{1,0:T(8,128)(2,1)S(1)}, bf16[32,2560]{1,0:T(8,128)(2,1)S(1)}, u32[]{:S(2)}, u32[]{:S(2)}) %collective-permute-start.5) | collective-permute-done | bytes 163872 | tf_op jit(solution)/shard_map/ppermute | solution.py:143
  69.9 3.4 %shard_map.55.refs_4_ = f32[128,2048]{1,0:T(8,128)S(1)} custom-call(bf16[32,1536]{1,0:T(8,128)(2,1)S(1)} %shard_map.54.refs_0_, bf16[32,1536]{1,0:T(8,128)(2,1)S(1)} %collective-permute-done.15.refs_1_, bf16[32,1536]{1,0:T(8,128)(2,1)S(1)} %collective-permute-done.16.refs_2_, bf16[32,1536]{1,0:T(8,128)(2,1)S(1)} %collective-permute-done.17.refs_3_, ...), custom_call_target="tpu_custom_call" | custom-call | flops 805306368 | bytes 6291456 | tf_op jit(solution)/shard_map/pallas_call | solution.py:196
  73.3 4.6 %shard_map.56.refs_4_ = f32[128,2048]{1,0:T(8,128)S(1)} custom-call(bf16[32,2560]{1,0:T(8,128)(2,1)S(1)} %shard_map.51.refs_0_, bf16[32,2560]{1,0:T(8,128)(2,1)S(1)} %collective-permute-done.10.refs_1_, bf16[32,2560]{1,0:T(8,128)(2,1)S(1)} %collective-permute-done.11.refs_2_, bf16[32,2560]{1,0:T(8,128)(2,1)S(1)} %collective-permute-done.12.refs_3_, ...), custom_call_target="tpu_custom_call" | custom-call | flops 1342177280 | bytes 10485760 | tf_op jit(solution)/shard_map/pallas_call | solution.py:196
  77.9 4.6 %shard_map.57 = (f32[32,2048]{1,0:T(8,128)S(1)}, bf16[32,2048]{1,0:T(8,128)(2,1)S(1)}, bf16[32,2048]{1,0:T(8,128)(2,1)S(1)}, bf16[32,2048]{1,0:T(8,128)(2,1)S(1)}) custom-call(bf16[32,2560]{1,0:T(8,128)(2,1)S(1)} %shard_map.48.refs_0_, bf16[32,2560]{1,0:T(8,128)(2,1)S(1)} %collective-permute-done.5.refs_1_, ...), custom_call_target="tpu_custom_call" | custom-call | flops 1342177280 | bytes 10485760 | tf_op jit(solution)/shard_map/pallas_call | solution.py:196
  82.5 0.9 collective-permute-start.18
  83.4 1.9 %collective-permute-start.19 = (bf16[32,2048]{1,0:T(8,128)(2,1)S(1)}, bf16[32,2048]{1,0:T(8,128)(2,1)S(1)}, u32[]{:S(2)}, u32[]{:S(2)}) collective-permute-start(bf16[32,2048]{1,0:T(8,128)(2,1)S(1)} %get-tuple-element.35), channel_id=1, source_target_pairs={{0,8},{4,12},{8,0},{12,4},{1,9},{5,13},{9,1},{13,5},{2,10},{6,14},... | collective-permute-start | bytes 393224 | tf_op jit(solution)/shard_map/ppermute | solution.py:146
  85.3 2.8 %collective-permute-start.20 = (bf16[32,2048]{1,0:T(8,128)(2,1)S(1)}, bf16[32,2048]{1,0:T(8,128)(2,1)S(1)}, u32[]{:S(2)}, u32[]{:S(2)}) collective-permute-start(bf16[32,2048]{1,0:T(8,128)(2,1)S(1)} %get-tuple-element.36), channel_id=1, source_target_pairs={{0,12},{4,0},{8,4},{12,8},{1,13},{5,1},{9,5},{13,9},{2,14},{6,2},{... | collective-permute-start | bytes 393224 | tf_op jit(solution)/shard_map/ppermute | solution.py:146
  88.1 2.7 %collective-permute-done.18.refs_0_ = bf16[32,2048]{1,0:T(8,128)(2,1)S(1)} collective-permute-done((bf16[32,2048]{1,0:T(8,128)(2,1)S(1)}, bf16[32,2048]{1,0:T(8,128)(2,1)S(1)}, u32[]{:S(2)}, u32[]{:S(2)}) %collective-permute-start.18) | collective-permute-done | bytes 131104 | tf_op jit(solution)/shard_map/ppermute | solution.py:146
  90.8 5.2 %collective-permute-done.19.refs_1_ = bf16[32,2048]{1,0:T(8,128)(2,1)S(1)} collective-permute-done((bf16[32,2048]{1,0:T(8,128)(2,1)S(1)}, bf16[32,2048]{1,0:T(8,128)(2,1)S(1)}, u32[]{:S(2)}, u32[]{:S(2)}) %collective-permute-start.19) | collective-permute-done | bytes 131104 | tf_op jit(solution)/shard_map/ppermute | solution.py:146
  96.0 0.7 shard_map.58
  (25 shorter events, 0.6 us)
Async XLA Ops:
  0.0 9.3 %collective-permute-start = (bf16[32,2048]{1,0:T(8,128)(2,1)}, bf16[32,2048]{1,0:T(8,128)(2,1)S(1)}, u32[]{:S(2)}, u32[]{:S(2)}) collective-permute-start(bf16[32,2048]{1,0:T(8,128)(2,1)} %refs_0_.5), channel_id=1, source_target_pairs={{0,12},{4,0},{8,4},{12,8},{1,13},{5,1},{9,5},{13,9},{2,14},{6,2},{... | collective-permute-start | bytes 393224 | tf_op jit(solution)/shard_map/ppermute | solution.py:146
  5.0 11.4 %collective-permute-start.1 = (bf16[32,2048]{1,0:T(8,128)(2,1)}, bf16[32,2048]{1,0:T(8,128)(2,1)S(1)}, u32[]{:S(2)}, u32[]{:S(2)}) collective-permute-start(bf16[32,2048]{1,0:T(8,128)(2,1)} %refs_0_.5), channel_id=1, source_target_pairs={{0,8},{4,12},{8,0},{12,4},{1,9},{5,13},{9,1},{13,5},{2,10},{6,14},... | collective-permute-start | bytes 393224 | tf_op jit(solution)/shard_map/ppermute | solution.py:146
  5.1 11.4 %collective-permute-start.2 = (bf16[32,2048]{1,0:T(8,128)(2,1)}, bf16[32,2048]{1,0:T(8,128)(2,1)S(1)}, u32[]{:S(2)}, u32[]{:S(2)}) collective-permute-start(bf16[32,2048]{1,0:T(8,128)(2,1)} %refs_0_.5), channel_id=1, source_target_pairs={{0,4},{4,8},{8,12},{12,0},{1,5},{5,9},{9,13},{13,1},{2,6},{6,10},{... | collective-permute-start | bytes 393224 | tf_op jit(solution)/shard_map/ppermute | solution.py:146
  16.5 0.9 copy-start
  25.3 14.0 %collective-permute-start.8 = (bf16[2,64,2560]{2,1,0:T(8,128)(2,1)S(1)}, bf16[2,64,2560]{2,1,0:T(8,128)(2,1)S(1)}, u32[]{:S(2)}, u32[]{:S(2)}) collective-permute-start(bf16[2,64,2560]{2,1,0:T(8,128)(2,1)S(1)} %get-tuple-element.26), channel_id=1, source_target_pairs={{0,1},{1,0},{2,3},{3,2},{4,5},{5,4},{6,7},{7,6},{8,9},{9,8},{10,11... | collective-permute-start | bytes 1966088 | tf_op jit(solution)/shard_map/ppermute | solution.py:168
  33.3 7.7 %collective-permute-start.3 = (bf16[2,64,2560]{2,1,0:T(8,128)(2,1)S(1)}, bf16[2,64,2560]{2,1,0:T(8,128)(2,1)S(1)}, u32[]{:S(2)}, u32[]{:S(2)}) collective-permute-start(bf16[2,64,2560]{2,1,0:T(8,128)(2,1)S(1)} %get-tuple-element.22), channel_id=1, source_target_pairs={{0,1},{1,0},{2,3},{3,2},{4,5},{5,4},{6,7},{7,6},{8,9},{9,8},{10,11... | collective-permute-start | bytes 1966088 | tf_op jit(solution)/shard_map/ppermute | solution.py:168
  39.2 2.5 %collective-permute-start.13 = (bf16[2,64,1536]{2,1,0:T(8,128)(2,1)S(1)}, bf16[2,64,1536]{2,1,0:T(8,128)(2,1)S(1)}, u32[]{:S(2)}, u32[]{:S(2)}) collective-permute-start(bf16[2,64,1536]{2,1,0:T(8,128)(2,1)S(1)} %get-tuple-element.30), channel_id=1, source_target_pairs={{0,1},{1,0},{2,3},{3,2},{4,5},{5,4},{6,7},{7,6},{8,9},{9,8},{10,11... | collective-permute-start | bytes 1179656 | tf_op jit(solution)/shard_map/ppermute | solution.py:168
  39.4 10.6 %collective-permute-start.9 = (bf16[2,32,2560]{2,1,0:T(8,128)(2,1)S(1)}, bf16[2,32,2560]{2,1,0:T(8,128)(2,1)S(1)}, u32[]{:S(2)}, u32[]{:S(2)}) collective-permute-start(bf16[2,32,2560]{2,1,0:T(8,128)(2,1)S(1)} %get-tuple-element.28), channel_id=1, source_target_pairs={{0,2},{1,3},{2,0},{3,1},{4,6},{5,7},{6,4},{7,5},{8,10},{9,11},{10,... | collective-permute-start | bytes 983048 | tf_op jit(solution)/shard_map/ppermute | solution.py:143
  41.1 21.8 %collective-permute-start.4 = (bf16[2,32,2560]{2,1,0:T(8,128)(2,1)S(1)}, bf16[2,32,2560]{2,1,0:T(8,128)(2,1)S(1)}, u32[]{:S(2)}, u32[]{:S(2)}) collective-permute-start(bf16[2,32,2560]{2,1,0:T(8,128)(2,1)S(1)} %get-tuple-element.24), channel_id=1, source_target_pairs={{0,2},{1,3},{2,0},{3,1},{4,6},{5,7},{6,4},{7,5},{8,10},{9,11},{10,... | collective-permute-start | bytes 983048 | tf_op jit(solution)/shard_map/ppermute | solution.py:143
  41.8 19.5 %collective-permute-start.14 = (bf16[2,32,1536]{2,1,0:T(8,128)(2,1)S(1)}, bf16[2,32,1536]{2,1,0:T(8,128)(2,1)S(1)}, u32[]{:S(2)}, u32[]{:S(2)}) collective-permute-start(bf16[2,32,1536]{2,1,0:T(8,128)(2,1)S(1)} %get-tuple-element.32), channel_id=1, source_target_pairs={{0,2},{1,3},{2,0},{3,1},{4,6},{5,7},{6,4},{7,5},{8,10},{9,11},{10,... | collective-permute-start | bytes 589832 | tf_op jit(solution)/shard_map/ppermute | solution.py:143
  50.1 17.5 %collective-permute-start.10 = (bf16[32,2560]{1,0:T(8,128)(2,1)S(1)}, bf16[32,2560]{1,0:T(8,128)(2,1)S(1)}, u32[]{:S(2)}, u32[]{:S(2)}) collective-permute-start(bf16[32,2560]{1,0:T(8,128)(2,1)S(1)} %shard_map.51.refs_0_), channel_id=1, source_target_pairs={{0,2},{1,3},{2,0},{3,1},{4,6},{5,7},{6,4},{7,5},{8,10},{9,11},{10,... | collective-permute-start | bytes 491528 | tf_op jit(solution)/shard_map/ppermute | solution.py:143
  61.3 5.8 %collective-permute-start.15 = (bf16[32,1536]{1,0:T(8,128)(2,1)S(1)}, bf16[32,1536]{1,0:T(8,128)(2,1)S(1)}, u32[]{:S(2)}, u32[]{:S(2)}) collective-permute-start(bf16[32,1536]{1,0:T(8,128)(2,1)S(1)} %shard_map.54.refs_0_), channel_id=1, source_target_pairs={{0,2},{1,3},{2,0},{3,1},{4,6},{5,7},{6,4},{7,5},{8,10},{9,11},{10,... | collective-permute-start | bytes 294920 | tf_op jit(solution)/shard_map/ppermute | solution.py:143
  63.0 6.9 %collective-permute-start.5 = (bf16[32,2560]{1,0:T(8,128)(2,1)S(1)}, bf16[32,2560]{1,0:T(8,128)(2,1)S(1)}, u32[]{:S(2)}, u32[]{:S(2)}) collective-permute-start(bf16[32,2560]{1,0:T(8,128)(2,1)S(1)} %shard_map.48.refs_0_), channel_id=1, source_target_pairs={{0,2},{1,3},{2,0},{3,1},{4,6},{5,7},{6,4},{7,5},{8,10},{9,11},{10,... | collective-permute-start | bytes 491528 | tf_op jit(solution)/shard_map/ppermute | solution.py:143
  63.6 4.0 %collective-permute-start.16 = (bf16[32,1536]{1,0:T(8,128)(2,1)S(1)}, bf16[32,1536]{1,0:T(8,128)(2,1)S(1)}, u32[]{:S(2)}, u32[]{:S(2)}) collective-permute-start(bf16[32,1536]{1,0:T(8,128)(2,1)S(1)} %shard_map.54.refs_0_), channel_id=1, source_target_pairs={{0,1},{1,0},{2,3},{3,2},{4,5},{5,4},{6,7},{7,6},{8,9},{9,8},{10,11... | collective-permute-start | bytes 294920 | tf_op jit(solution)/shard_map/ppermute | solution.py:187
  67.1 2.8 %collective-permute-start.17 = (bf16[32,1536]{1,0:T(8,128)(2,1)S(1)}, bf16[32,1536]{1,0:T(8,128)(2,1)S(1)}, u32[]{:S(2)}, u32[]{:S(2)}) collective-permute-start(bf16[32,1536]{1,0:T(8,128)(2,1)S(1)} %collective-permute-done.15.refs_1_), channel_id=1, source_target_pairs={{0,1},{1,0},{2,3},{3,2},{4,5},{5,4},{6,7},{7,6},{8,9},{9,8},{10,11... | collective-permute-start | bytes 294920 | tf_op jit(solution)/shard_map/ppermute | solution.py:187
  67.1 6.2 %collective-permute-start.11 = (bf16[32,2560]{1,0:T(8,128)(2,1)S(1)}, bf16[32,2560]{1,0:T(8,128)(2,1)S(1)}, u32[]{:S(2)}, u32[]{:S(2)}) collective-permute-start(bf16[32,2560]{1,0:T(8,128)(2,1)S(1)} %shard_map.51.refs_0_), channel_id=1, source_target_pairs={{0,1},{1,0},{2,3},{3,2},{4,5},{5,4},{6,7},{7,6},{8,9},{9,8},{10,11... | collective-permute-start | bytes 491528 | tf_op jit(solution)/shard_map/ppermute | solution.py:187
  67.6 5.7 %collective-permute-start.12 = (bf16[32,2560]{1,0:T(8,128)(2,1)S(1)}, bf16[32,2560]{1,0:T(8,128)(2,1)S(1)}, u32[]{:S(2)}, u32[]{:S(2)}) collective-permute-start(bf16[32,2560]{1,0:T(8,128)(2,1)S(1)} %collective-permute-done.10.refs_1_), channel_id=1, source_target_pairs={{0,1},{1,0},{2,3},{3,2},{4,5},{5,4},{6,7},{7,6},{8,9},{9,8},{10,11... | collective-permute-start | bytes 491528 | tf_op jit(solution)/shard_map/ppermute | solution.py:187
  67.6 10.3 %collective-permute-start.6 = (bf16[32,2560]{1,0:T(8,128)(2,1)S(1)}, bf16[32,2560]{1,0:T(8,128)(2,1)S(1)}, u32[]{:S(2)}, u32[]{:S(2)}) collective-permute-start(bf16[32,2560]{1,0:T(8,128)(2,1)S(1)} %shard_map.48.refs_0_), channel_id=1, source_target_pairs={{0,1},{1,0},{2,3},{3,2},{4,5},{5,4},{6,7},{7,6},{8,9},{9,8},{10,11... | collective-permute-start | bytes 491528 | tf_op jit(solution)/shard_map/ppermute | solution.py:187
  69.9 8.0 %collective-permute-start.7 = (bf16[32,2560]{1,0:T(8,128)(2,1)S(1)}, bf16[32,2560]{1,0:T(8,128)(2,1)S(1)}, u32[]{:S(2)}, u32[]{:S(2)}) collective-permute-start(bf16[32,2560]{1,0:T(8,128)(2,1)S(1)} %collective-permute-done.5.refs_1_), channel_id=1, source_target_pairs={{0,1},{1,0},{2,3},{3,2},{4,5},{5,4},{6,7},{7,6},{8,9},{9,8},{10,11... | collective-permute-start | bytes 491528 | tf_op jit(solution)/shard_map/ppermute | solution.py:187
  82.5 8.3 %collective-permute-start.18 = (bf16[32,2048]{1,0:T(8,128)(2,1)S(1)}, bf16[32,2048]{1,0:T(8,128)(2,1)S(1)}, u32[]{:S(2)}, u32[]{:S(2)}) collective-permute-start(bf16[32,2048]{1,0:T(8,128)(2,1)S(1)} %get-tuple-element.34), channel_id=1, source_target_pairs={{0,4},{4,8},{8,12},{12,0},{1,5},{5,9},{9,13},{13,1},{2,6},{6,10},{... | collective-permute-start | bytes 393224 | tf_op jit(solution)/shard_map/ppermute | solution.py:146
  83.4 12.6 %collective-permute-start.19 = (bf16[32,2048]{1,0:T(8,128)(2,1)S(1)}, bf16[32,2048]{1,0:T(8,128)(2,1)S(1)}, u32[]{:S(2)}, u32[]{:S(2)}) collective-permute-start(bf16[32,2048]{1,0:T(8,128)(2,1)S(1)} %get-tuple-element.35), channel_id=1, source_target_pairs={{0,8},{4,12},{8,0},{12,4},{1,9},{5,13},{9,1},{13,5},{2,10},{6,14},... | collective-permute-start | bytes 393224 | tf_op jit(solution)/shard_map/ppermute | solution.py:146
  85.3 10.7 %collective-permute-start.20 = (bf16[32,2048]{1,0:T(8,128)(2,1)S(1)}, bf16[32,2048]{1,0:T(8,128)(2,1)S(1)}, u32[]{:S(2)}, u32[]{:S(2)}) collective-permute-start(bf16[32,2048]{1,0:T(8,128)(2,1)S(1)} %get-tuple-element.36), channel_id=1, source_target_pairs={{0,12},{4,0},{8,4},{12,8},{1,13},{5,1},{9,5},{13,9},{2,14},{6,2},{... | collective-permute-start | bytes 393224 | tf_op jit(solution)/shard_map/ppermute | solution.py:146

commit v2 on v0

v2 whole, which is shorter than its diff:
```python
import functools

import jax
import jax.numpy as jnp
from jax import lax
from jax.experimental import pallas as pl
from jax.experimental.pallas import tpu as pltpu
from jax.sharding import PartitionSpec as P

MIB = 1 << 20
F32, BF16 = jnp.float32, jnp.bfloat16
WHOLE = pl.BlockSpec(memory_space=pltpu.VMEM)
FAR = pl.BlockSpec(memory_space=pltpu.HBM)
STAY = pl.BlockSpec(memory_space=pl.ANY)
NEAR_ROWS, FAR_ROWS = 0, 1


def largest(total, options):
    return next(o for o in options if total % o == 0)


def fetch_start(copies):
    for copy in copies:
        copy.start()


def fetch_wait(copies):
    for copy in copies:
        copy.wait()


def column_copies(start, sources, targets, sems):
    pieces = sems.shape[0] // 2
    depth = targets[0].shape[0] // pieces
    copies = []
    for i in range(2 * pieces):
        at = pl.ds(i // 2 * depth, depth)
        source, target = sources[i % 2], targets[i % 2]
        copies.append(
            pltpu.make_async_copy(source.at[at, pl.ds(start, target.shape[1])], target.at[at, :], sems.at[i])
        )
    return copies


def fetch_kernel(start, gate_ref, up_ref, gate_out, up_out, sems):
    copies = column_copies(start, (gate_ref, up_ref), (gate_out, up_out), sems)
    fetch_start(copies)
    fetch_wait(copies)


def order_rows(parts, left):
    rows = parts[0][0].shape[0]
    half = len(parts[0]) * rows
    other = 1 - lax.rem(lax.axis_index("wid"), 2)
    for h, blocks in enumerate(parts):
        for j, block in enumerate(blocks):
            at = h * half + lax.rem(j * rows + other * (half // 2), half)
            left[pl.ds(pl.multiple_of(at, rows), rows), :] = block[...]


def put_sums(sums, halves, send_refs, keep_ref):
    for which, value in enumerate(sums):
        quarter = value.shape[0] // (2 * halves)
        for h in range(halves):
            at = 2 * h * quarter
            send_refs[h % len(send_refs)][h // len(send_refs), which] = value[at : at + quarter].astype(BF16)
            keep_ref[h, which] = value[at + quarter : at + 2 * quarter]


def split_parts(refs, halves, blocks):
    return [refs[h * blocks : (h + 1) * blocks] for h in range(halves)], refs[halves * blocks :]


def held_gate_up_kernel(halves, blocks, *refs):
    parts, (gate_ref, up_ref, *send_refs, keep_ref, left) = split_parts(refs, halves, blocks)
    order_rows(parts, left)
    sums = [jnp.dot(left[...], w[...], preferred_element_type=F32) for w in (gate_ref, up_ref)]
    put_sums(sums, halves, send_refs, keep_ref)


def gate_up_kernel(start, width, depth, slots, halves, blocks, *refs):
    parts, (gate_ref, up_ref, *send_refs, keep_ref, left, held, sems) = split_parts(refs, halves, blocks)
    total = 2 * (left.shape[1] // depth)

    def copy(i):
        source = (gate_ref, up_ref)[i % 2]
        slot = i % slots
        return pltpu.make_async_copy(
            source.at[pl.ds(i // 2 * depth, depth), pl.ds(start, width)], held.at[slot], sems.at[slot]
        )

    for i in range(min(slots, total)):
        copy(i).start()
    order_rows(parts, left)
    sums = [None, None]
    for i in range(total):
        copy(i).wait()
        product = jnp.dot(left[:, pl.ds(i // 2 * depth, depth)], held[i % slots], preferred_element_type=F32)
        sums[i % 2] = product if i < 2 else sums[i % 2] + product
        if i + slots < total:
            copy(i + slots).start()
    put_sums(sums, halves, send_refs, keep_ref)


def chip_sum_kernel(chips, halves, keep, *refs):
    came, outs = refs[:-chips], refs[-chips:]
    rows = outs[0].shape[2]
    me = lax.axis_index("wid") // 2
    for j in range(chips):
        at = pl.ds(pl.multiple_of(lax.rem(me + j, chips) * rows, rows), rows)
        for h in range(halves):
            for which in range(2):
                other = came[h % len(came)][h // len(came), which, at, :]
                outs[j][h, which] = (keep[h, which, at, :] + other.astype(F32)).astype(outs[j].dtype)


def hidden_kernel(own_ref, *refs):
    came_refs, hidden_ref = refs[:-1], refs[-1]
    for h in range(own_ref.shape[0]):
        gate, up = own_ref[h, 0], own_ref[h, 1]
        for came in came_refs:
            gate = gate + came[h, 0].astype(F32)
            up = up + came[h, 1].astype(F32)
        hidden_ref[h] = (gate / (1.0 + jnp.exp(-gate)) * up).astype(BF16)


def pack_kernel(*refs):
    for j, ref in enumerate(refs[:-1]):
        refs[-1][j] = ref[...]


def fetch_rows_kernel(start, down_ref, out_ref, sems):
    pieces = sems.shape[0]
    rows = out_ref.shape[0] // pieces
    copies = [
        pltpu.make_async_copy(
            down_ref.at[pl.ds(start + p * rows, rows), :], out_ref.at[pl.ds(p * rows, rows), :], sems.at[p]
        )
        for p in range(pieces)
    ]
    fetch_start(copies)
    fetch_wait(copies)


def place_hidden(pairs, left):
    x, core = lax.axis_index("wid") // 2, lax.rem(lax.axis_index("wid"), 2)
    for side, ref in enumerate(pairs):
        chips, halves, rows, _ = ref.shape
        quarter = left.shape[0] // (2 * halves)
        for h in range(halves):
            for j in range(chips):
                base = (2 * h + (core if side == 0 else 1 - core)) * quarter
                at = base + lax.rem(x - j + chips, chips) * rows
                left[pl.ds(pl.multiple_of(at, rows), rows), :] = ref[j, h]


def down_kernel(first, last, near_ref, far_ref, *refs):
    if not first:
        before_ref, refs = refs[0], refs[1:]
    down_ref, outs, left = refs[0], refs[1:-1], refs[-1]
    place_hidden((near_ref, far_ref), left)
    value = jnp.dot(left[...], down_ref[...], preferred_element_type=F32)
    if not first:
        value = value + before_ref[...]
    rows = outs[0].shape[0]
    for j, out in enumerate(outs):
        out[...] = value[j * rows : (j + 1) * rows].astype(out.dtype)


def final_kernel(own_ref, *refs):
    value = own_ref[...]
    for came in refs[:-1]:
        value = value + came[...].astype(F32)
    refs[-1][...] = value.astype(refs[-1].dtype)


class Body:
    def __init__(self, groups, wide):
        self.groups, self.wide, self.chips = groups, wide, wide // 2
        self.last = None

    def call(self, kernel, ins, outs, scratch, flops, moved, limit, args):
        after = [] if self.last is None else [self.last]

        def run(*refs):
            kernel(*refs[len(after) :])

        got = pl.pallas_call(
            run,
            name=kernel.func.__name__ if isinstance(kernel, functools.partial) else kernel.__name__,
            in_specs=[STAY] * len(after) + ins,
            out_specs=[WHOLE] * len(outs),
            out_shape=outs,
            scratch_shapes=scratch,
            compiler_params=pltpu.CompilerParams(vmem_limit_bytes=limit),
            cost_estimate=pl.CostEstimate(flops=flops, bytes_accessed=moved, transcendentals=0),
        )(*after, *args)
        self.last = got[0]
        return got

    def other_core(self, value):
        return lax.ppermute(value, "wid", [(w, w ^ 1) for w in range(self.wide)])

    def along_x(self, value, j):
        return lax.ppermute(value, "wid", [(w, (w // 2 + j) % self.chips * 2 + w % 2) for w in range(self.wide)])

    def along_z(self, value, j):
        return lax.ppermute(value, "hid", [(z, z ^ j) for z in range(self.groups)])

    def gate_up(self, start, size, halves, weights, sends=1):
        width = self.width
        parts = [p for h in halves for p in self.parts[h]]
        rows = len(parts) * self.part
        quarter = rows // (2 * len(halves))
        outs = [jax.ShapeDtypeStruct((len(halves) // sends, 2, quarter, size), BF16)] * sends
        outs.append(jax.ShapeDtypeStruct((len(halves), 2, quarter, size), F32))
        left = pltpu.VMEM((rows, width), BF16)
        count = (len(halves), self.groups // 2)
        if weights is not None:
            got = self.call(
                functools.partial(held_gate_up_kernel, *count),
                [WHOLE] * (len(parts) + 2),
                outs,
                [left],
                4 * rows * width * size,
                rows * width,
                6 * MIB,
                (*parts, *weights),
            )
        else:
            depth, slots = largest(width, (512, 256)), 4
            got = self.call(
                functools.partial(gate_up_kernel, start, size, depth, slots, *count),
                [WHOLE] * len(parts) + [FAR] * 2,
                outs,
                [left, pltpu.VMEM((slots, depth, size), BF16), pltpu.SemaphoreType.DMA((slots,))],
                4 * rows * width * size,
                4 * width * size,
                16 * MIB,
                (*parts, self.gate_weight, self.up_weight),
            )
        return got[-1], *(self.other_core(v) for v in got[:-1])

    def fetch(self, start, size):
        return self.call(
            functools.partial(fetch_kernel, start),
            [FAR] * 2,
            [jax.ShapeDtypeStruct((self.width, size), BF16)] * 2,
            [pltpu.SemaphoreType.DMA((8,))],
            0,
            4 * self.width * size,
            2 * MIB,
            (self.gate_weight, self.up_weight),
        )

    def chip_sum(self, halves, args):
        size = args[0].shape[3]
        block = (len(halves), 2, self.block, size)
        own, *sends = self.call(
            functools.partial(chip_sum_kernel, self.chips, len(halves)),
            [WHOLE] * len(args),
            [jax.ShapeDtypeStruct(block, F32)] + [jax.ShapeDtypeStruct(block, BF16)] * (self.chips - 1),
            [],
            size * 256,
            size * 1024,
            4 * MIB,
            args,
        )
        return own, [self.along_x(v, j + 1) for j, v in enumerate(sends)]

    def hidden(self, summed):
        own, came = summed
        n, _, rows, size = own.shape
        (mine,) = self.call(
            hidden_kernel,
            [WHOLE] * (1 + len(came)),
            [jax.ShapeDtypeStruct((n, rows, size), BF16)],
            [],
            size * 256,
            size * 1024,
            4 * MIB,
            (own, *came),
        )
        return [mine] + [self.along_x(mine, j) for j in range(1, self.chips)]

    def pack(self, near):
        shape = jax.ShapeDtypeStruct((len(near),) + near[0].shape, BF16)
        (packed,) = self.call(pack_kernel, [WHOLE] * len(near), [shape], [], 256, 1024, 4 * MIB, near)
        return packed, self.other_core(packed)

    def fetch_rows(self, start, size):
        (rows,) = self.call(
            functools.partial(fetch_rows_kernel, start),
            [FAR],
            [jax.ShapeDtypeStruct((size, self.width), BF16)],
            [pltpu.SemaphoreType.DMA((4,))],
            0,
            2 * self.width * size,
            2 * MIB,
            (self.down_weight,),
        )
        return rows

    def down(self, packed, before, weights, last):
        size = weights.shape[0]
        width, rows = self.width, 2 * self.half
        if last:
            outs = [jax.ShapeDtypeStruct((self.part, width), t) for t in [F32] + [BF16] * (self.groups - 1)]
        else:
            outs = [jax.ShapeDtypeStruct((rows, width), F32)]
        return self.call(
            functools.partial(down_kernel, not before, last),
            [WHOLE] * (3 + len(before)),
            outs,
            [pltpu.VMEM((rows, size), BF16)],
            2 * rows * width * size,
            rows * size,
            6 * MIB,
            (*packed, *before, weights),
        )

    def __call__(self, tokens, gate_weight, up_weight, down_weight):
        self.gate_weight, self.up_weight, self.down_weight = (
            pltpu.with_memory_space_constraint(w, pltpu.HBM) for w in (gate_weight, up_weight, down_weight)
        )
        self.part, self.width = tokens.shape
        groups = self.groups
        self.half = self.part * groups // 2
        self.block = self.half // self.wide
        units = gate_weight.shape[1]
        step = units // 26 if units // 26 % 128 == 0 else units // 13
        count = units // step
        cuts = [count * c // 26 * step for c in (0, 9, 17, 26)]
        (s0, n0), (s1, n1), (s2, n2) = [(a, b - a) for a, b in zip(cuts[:-1], cuts[1:])]
        both = (NEAR_ROWS, FAR_ROWS)

        blocks = [tokens] + [self.along_z(tokens, j) for j in range(1, groups)]
        self.parts = (blocks[: groups // 2], blocks[groups // 2 :])

        w0 = self.fetch(s0, n0)
        w1 = self.fetch(s1, n1)
        a0 = self.gate_up(s0, n0, both, w0)
        a1 = self.gate_up(s1, n1, both, w1)
        b0 = self.chip_sum(both, a0)
        b1 = self.chip_sum(both, a1)
        a2 = self.gate_up(s2, n2, both, None, 2)
        h0 = self.hidden(b0)
        b2 = self.chip_sum(both, a2)
        d0 = self.fetch_rows(s0, n0)
        h1 = self.hidden(b1)
        d1 = self.fetch_rows(s1, n1)
        p0 = self.pack(h0)
        d2 = self.fetch_rows(s2, n2)
        h2 = self.hidden(b2)
        p1 = self.pack(h1)
        value = self.down(p0, [], d0, False)
        p2 = self.pack(h2)
        value = self.down(p1, value, d1, False)
        own, *late = self.down(p2, value, d2, True)
        arrived = [self.along_z(late[j - 1], j) for j in range(groups - 1, 0, -1)]
        (mixed,) = self.call(
            final_kernel,
            [WHOLE] * groups,
            [jax.ShapeDtypeStruct((self.part, self.width), BF16)],
            [],
            groups * self.part * self.width,
            4 * groups * self.part * self.width,
            4 * MIB,
            (own, *arrived),
        )
        return mixed


def solution(mesh):
    placed = (P(("group", "hid"), "wid"), P("wid", "hid"), P("wid", "hid"), P("hid", "wid"))

    def run(*arrays):
        return Body(mesh.shape["hid"], mesh.shape["wid"])(*arrays)

    return jax.shard_map(run, mesh=mesh, in_specs=placed, out_specs=P(("group", "hid"), "wid"), check_vma=False)
```

time: 235 us -> 76.7 us (0.33)
  waiting for transfers between devices: 158 us -> 15.3 us
  matrix products: 44.2 us -> 0 us
  Pallas kernels: 0 us -> 41.5 us
  starting transfers between devices: 0.04 us -> 19.6 us
  blocking collectives: 17.6 us -> 0 us
  between operations: 13.4 us -> 0.23 us
    psum x1 -> x0, waiting for transfers between devices: 130 us -> none  [body(): gate, upward = lax.psum((gate_part, up_part), 'wid')]
    dot_general x3 -> x0, matrix products: 44.2 us -> none  [the longest x1 15.6 us: body(): jnp.dot(hidden, down_weight, preferred_element_type=jnp.float32)]
    pallas_call x0 -> x21, Pallas kernels: none -> 41.5 us  [call(): pl.pallas_call(run, name=kernel.func.__name__ if isinstance(kernel, funct...]
    reduce_scatter x1 -> x0, waiting for transfers between devices: 27.5 us -> none  [body(): lax.psum_scatter(jnp.dot(hidden, down_weight, preferred_element_type=jnp....]
    ppermute x0 -> x19, starting transfers between devices: none -> 19.6 us  [the longest x6 10.1 us: along_z(): return lax.ppermute(value, 'hid', [(z, z ^ j) for z in range(self.groups)])]
    all_gather x1 -> x0, blocking collectives: 17.6 us -> none  [body(): gathered = lax.all_gather(tokens, 'hid', axis=0, tiled=True)]
    ppermute x0 -> x19, waiting for transfers between devices: none -> 15.3 us  [the longest x6 10.4 us: along_z(): return lax.ppermute(value, 'hid', [(z, z ^ j) for z in range(self.groups)])]
  transfers between devices with their start and end apart: 2 -> 19, of which waited for: 2 -> 7; matrix products, arithmetic and copies ran while one was open for 0% -> 0% of each run, Pallas kernels for 0% -> 48%
where the time goes in v2:
time: 76.7 us; the launch traced here: 76.6 us
  Pallas kernels  41.5 us (54%)
  starting transfers between devices  19.6 us (26%)
  waiting for transfers between devices  15.3 us (20%)
    pallas_call x21, Pallas kernels, call(): pl.pallas_call(run, name=kernel.func.__name__ if isinstance(kernel, funct...  41.5 us
    ppermute x6, waiting for transfers between devices, along_z(): return lax.ppermute(value, 'hid', [(z, z ^ j) for z in range(self.groups)])  10.4 us
    ppermute x6, starting transfers between devices, along_z(): return lax.ppermute(value, 'hid', [(z, z ^ j) for z in range(self.groups)])  10.1 us
    ppermute x6, starting transfers between devices, along_x(): lax.ppermute(value, 'wid', [(w, (w // 2 + j) % self.chips * 2 + w % 2) fo...  8.09 us
    ppermute x6, waiting for transfers between devices, along_x(): lax.ppermute(value, 'wid', [(w, (w // 2 + j) % self.chips * 2 + w % 2) fo...  4.66 us
  transfers between devices with their start and end apart: 19, of which 7 were waited for; matrix products, arithmetic and copies ran while one was open for 0% of the time, Pallas kernels for 48%

profile of v2, /device:TPU:0, one launch (start us, length us, event | category | flops | bytes accessed | tf_op | source)
XLA Modules:
  0.0 76.6 jit_solution(15186803065931331853)
XLA Ops:
  0.0 5.0 %collective-permute-start.2 = (bf16[32,2048]{1,0:T(8,128)(2,1)}, bf16[32,2048]{1,0:T(8,128)(2,1)S(1)}, u32[]{:S(2)}, u32[]{:S(2)}) collective-permute-start(bf16[32,2048]{1,0:T(8,128)(2,1)} %refs_1_.12), channel_id=1, source_target_pairs={{0,12},{4,8},{8,4},{12,0},{1,13},{5,9},{9,5},{13,1},{2,14},{6,10},... | collective-permute-start | bytes 393224 | tf_op jit(solution)/shard_map/ppermute | solution.py:208
  5.1 0.6 collective-permute-start
  5.6 6.6 %fetch_kernel.2 = (bf16[2048,2304]{1,0:T(8,128)(2,1)S(1)}, bf16[2048,2304]{1,0:T(8,128)(2,1)S(1)}) custom-call(bf16[2048,6656]{1,0:T(8,128)(2,1)} %refs_5_.1, bf16[2048,6656]{1,0:T(8,128)(2,1)} %refs_6_.1), custom_call_target="tpu_custom_call" | custom-call | bytes 18874368 | tf_op jit(solution)/shard_map/fetch_kernel/pallas_call | solution.py:188
  12.2 6.0 %fetch_kernel.3 = (bf16[2048,2048]{1,0:T(8,128)(2,1)S(1)}, bf16[2048,2048]{1,0:T(8,128)(2,1)S(1)}) custom-call(bf16[2048,2304]{1,0:T(8,128)(2,1)S(1)} %get-tuple-element.26.refs_0_.refs_5_, bf16[2048,6656]{1,0:T(8,128)(2,1)} %refs_5_.1, bf16[2048,6656]{1,0:T(8,128)(2,1)} %refs_6_.1), custom_call_target="tpu_custom_call" | custom-call | bytes 16777216 | tf_op jit(solution)/shard_map/fetch_kernel/pallas_call | solution.py:188
  18.2 2.6 %held_gate_up_kernel.2 = (bf16[2,2,32,2304]{3,2,1,0:T(8,128)(2,1)S(1)}, f32[2,2,32,2304]{3,2,1,0:T(8,128)S(1)}) custom-call(bf16[2048,2048]{1,0:T(8,128)(2,1)S(1)} %get-tuple-element.27.refs_0_.refs_5_, bf16[32,2048]{1,0:T(8,128)(2,1)S(1)} %copy-done, bf16[32,2048]{1,0:T(8,128)(2,1)S(1)} %collective-permute-done.refs_2_, ...), custom_call_target="tpu_custom_call" | custom-call | flops 2415919104 | bytes 262144 | tf_op jit(solution)/shard_map/held_gate_up_kernel/pallas_call | solution.py:188
  20.9 2.4 %held_gate_up_kernel.3 = (bf16[2,2,32,2048]{3,2,1,0:T(8,128)(2,1)S(1)}, f32[2,2,32,2048]{3,2,1,0:T(8,128)S(1)}) custom-call(bf16[2,2,32,2304]{3,2,1,0:T(8,128)(2,1)S(1)} %get-tuple-element.29.refs_0_, bf16[32,2048]{1,0:T(8,128)(2,1)S(1)} %copy-done, bf16[32,2048]{1,0:T(8,128)(2,1)S(1)} %collective-permute-done.refs_2_, ...), custom_call_target="tpu_custom_call" | custom-call | flops 2147483648 | bytes 262144 | tf_op jit(solution)/shard_map/held_gate_up_kernel/pallas_call | solution.py:188
  23.3 0.5 collective-permute-start.4
  24.0 1.8 %collective-permute-start.5 = (bf16[2,2,16,2304]{3,2,1,0:T(8,128)(2,1)S(1)}, bf16[2,2,16,2304]{3,2,1,0:T(8,128)(2,1)S(1)}, u32[]{:S(2)}, u32[]{:S(2)}) collective-permute-start(bf16[2,2,16,2304]{3,2,1,0:T(8,128)(2,1)S(1)} %get-tuple-element.37), channel_id=1, source_target_pairs={{0,2},{1,3},{2,0},{3,1},{4,6},{5,7},{6,4},{7,5},{8,10},{9,11},{10,... | collective-permute-start | bytes 884744 | tf_op jit(solution)/shard_map/ppermute | solution.py:205
  25.9 7.3 %gate_up_kernel.1 = (bf16[1,2,32,2304]{3,2,1,0:T(8,128)(2,1)S(1)}, bf16[1,2,32,2304]{3,2,1,0:T(8,128)(2,1)S(1)}, f32[2,2,32,2304]{3,2,1,0:T(8,128)S(1)}) custom-call(f32[2,2,16,2048]{3,2,1,0:T(8,128)S(1)} %get-tuple-element.35.refs_0_.refs_1_, bf16[32,2048]{1,0:T(8,128)(2,1)S(1)} %copy-done, bf16[32,2048]{1,0:T(8,128)(2,1)S(1)} %collective-permute-done.refs_2_, ...), custom_call_target="tpu_custom_call" | custom-call | flops 2415919104 | bytes 18874368 | tf_op jit(solution)/shard_map/gate_up_kernel/pallas_call | solution.py:188
  33.2 0.5 collective-permute-start.6
  33.7 1.4 %collective-permute-start.8 = (bf16[2,2,16,2048]{3,2,1,0:T(8,128)(2,1)S(1)}, bf16[2,2,16,2048]{3,2,1,0:T(8,128)(2,1)S(1)}, u32[]{:S(2)}, u32[]{:S(2)}) collective-permute-start(bf16[2,2,16,2048]{3,2,1,0:T(8,128)(2,1)S(1)} %get-tuple-element.41), channel_id=1, source_target_pairs={{0,2},{1,3},{2,0},{3,1},{4,6},{5,7},{6,4},{7,5},{8,10},{9,11},{10,... | collective-permute-start | bytes 786440 | tf_op jit(solution)/shard_map/ppermute | solution.py:205
  35.1 0.1 hidden_kernel.3.refs_0_.refs_1_
  35.2 0.7 collective-permute-start.9
  36.1 1.4 %collective-permute-start.10 = (bf16[2,2,16,2304]{3,2,1,0:T(8,128)(2,1)S(1)}, bf16[2,2,16,2304]{3,2,1,0:T(8,128)(2,1)S(1)}, u32[]{:S(2)}, u32[]{:S(2)}) collective-permute-start(bf16[2,2,16,2304]{3,2,1,0:T(8,128)(2,1)S(1)} %get-tuple-element.42), channel_id=1, source_target_pairs={{0,2},{1,3},{2,0},{3,1},{4,6},{5,7},{6,4},{7,5},{8,10},{9,11},{10,... | collective-permute-start | bytes 884744 | tf_op jit(solution)/shard_map/ppermute | solution.py:205
  37.5 3.8 %fetch_rows_kernel.3.refs_0_.refs_3_ = bf16[2304,2048]{1,0:T(8,128)(2,1)S(1)} custom-call(f32[2,2,16,2304]{3,2,1,0:T(8,128)S(1)} %get-tuple-element.40.refs_0_.refs_1_, bf16[6656,2048]{1,0:T(8,128)(2,1)} %refs_1_.15), custom_call_target="tpu_custom_call" | custom-call | bytes 9437184 | tf_op jit(solution)/shard_map/fetch_rows_kernel/pallas_call | solution.py:188
  41.3 1.6 %collective-permute-done.8.refs_2_ = bf16[2,2,16,2048]{3,2,1,0:T(8,128)(2,1)S(1)} collective-permute-done((bf16[2,2,16,2048]{3,2,1,0:T(8,128)(2,1)S(1)}, bf16[2,2,16,2048]{3,2,1,0:T(8,128)(2,1)S(1)}, u32[]{:S(2)}, u32[]{:S(2)}) %collective-permute-start.8) | collective-permute-done | bytes 262176 | tf_op jit(solution)/shard_map/ppermute | solution.py:205
  43.0 3.5 %fetch_rows_kernel.4.refs_0_.refs_4_ = bf16[2048,2048]{1,0:T(8,128)(2,1)S(1)} custom-call(bf16[2,16,2048]{2,1,0:T(8,128)(2,1)S(1)} %hidden_kernel.4.refs_0_.refs_1_, bf16[6656,2048]{1,0:T(8,128)(2,1)} %refs_1_.15), custom_call_target="tpu_custom_call" | custom-call | bytes 8388608 | tf_op jit(solution)/shard_map/fetch_rows_kernel/pallas_call | solution.py:188
  46.6 1.4 %collective-permute-start.11 = (bf16[2,16,2048]{2,1,0:T(8,128)(2,1)S(1)}, bf16[2,16,2048]{2,1,0:T(8,128)(2,1)S(1)}, u32[]{:S(2)}, u32[]{:S(2)}) collective-permute-start(bf16[2,16,2048]{2,1,0:T(8,128)(2,1)S(1)} %hidden_kernel.4.refs_0_.refs_1_), channel_id=1, source_target_pairs={{0,2},{1,3},{2,0},{3,1},{4,6},{5,7},{6,4},{7,5},{8,10},{9,11},{10,... | collective-permute-start | bytes 393224 | tf_op jit(solution)/shard_map/ppermute | solution.py:205
  48.0 3.8 %fetch_rows_kernel.5.refs_0_.refs_4_ = bf16[2304,2048]{1,0:T(8,128)(2,1)S(1)} custom-call(bf16[2,2,16,2304]{3,2,1,0:T(8,128)(2,1)S(1)} %pack_kernel.3.refs_0_.refs_1_, bf16[6656,2048]{1,0:T(8,128)(2,1)} %refs_1_.15), custom_call_target="tpu_custom_call" | custom-call | bytes 9437184 | tf_op jit(solution)/shard_map/fetch_rows_kernel/pallas_call | solution.py:188
  51.8 0.5 collective-permute-done.10.refs_2_
  52.5 1.4 %collective-permute-start.13 = (bf16[2,16,2304]{2,1,0:T(8,128)(2,1)S(1)}, bf16[2,16,2304]{2,1,0:T(8,128)(2,1)S(1)}, u32[]{:S(2)}, u32[]{:S(2)}) collective-permute-start(bf16[2,16,2304]{2,1,0:T(8,128)(2,1)S(1)} %hidden_kernel.5.refs_0_.refs_1_), channel_id=1, source_target_pairs={{0,2},{1,3},{2,0},{3,1},{4,6},{5,7},{6,4},{7,5},{8,10},{9,11},{10,... | collective-permute-start | bytes 442376 | tf_op jit(solution)/shard_map/ppermute | solution.py:205
  53.9 0.4 collective-permute-done.11.refs_2_
  54.4 1.4 %down_kernel.3.refs_0_.refs_3_ = f32[128,2048]{1,0:T(8,128)S(1)} custom-call(bf16[2,2,16,2048]{3,2,1,0:T(8,128)(2,1)S(1)} %pack_kernel.4.refs_0_.refs_1_, bf16[2,2,16,2304]{3,2,1,0:T(8,128)(2,1)S(1)} %pack_kernel.3.refs_0_.refs_1_, bf16[2,2,16,2304]{3,2,1,0:T(8,128)(2,1)S(1)} %collective-permute-done.12.refs_2_, ...), custom_call_target="tpu_custom_call" | custom-call | flops 1207959552 | bytes 294912 | tf_op jit(solution)/shard_map/down_kernel/pallas_call | solution.py:188
  55.8 2.1 %collective-permute-done.13.refs_2_ = bf16[2,16,2304]{2,1,0:T(8,128)(2,1)S(1)} collective-permute-done((bf16[2,16,2304]{2,1,0:T(8,128)(2,1)S(1)}, bf16[2,16,2304]{2,1,0:T(8,128)(2,1)S(1)}, u32[]{:S(2)}, u32[]{:S(2)}) %collective-permute-start.13) | collective-permute-done | bytes 147488 | tf_op jit(solution)/shard_map/ppermute | solution.py:205
  58.1 1.3 %down_kernel.4.refs_0_.refs_3_ = f32[128,2048]{1,0:T(8,128)S(1)} custom-call(bf16[2,2,16,2304]{3,2,1,0:T(8,128)(2,1)S(1)} %pack_kernel.5.refs_0_.refs_1_, bf16[2,2,16,2048]{3,2,1,0:T(8,128)(2,1)S(1)} %pack_kernel.4.refs_0_.refs_1_, bf16[2,2,16,2048]{3,2,1,0:T(8,128)(2,1)S(1)} %collective-permute-done.14.refs_2_, f32[128,2048]{1,0:T(8,128)S(1)} %down_kernel.3.refs_0_.refs_3_, ...), custom_call_target="tpu_custom_call" | custom-call | flops 1073741824 | bytes 262144 | tf_op jit(solution)/shard_map/down_kernel/pallas_call | solution.py:188
  59.4 0.3 collective-permute-done.15.refs_2_
  59.6 1.4 %down_kernel.5 = (f32[32,2048]{1,0:T(8,128)S(1)}, bf16[32,2048]{1,0:T(8,128)(2,1)S(1)}, bf16[32,2048]{1,0:T(8,128)(2,1)S(1)}, bf16[32,2048]{1,0:T(8,128)(2,1)S(1)}) custom-call(f32[128,2048]{1,0:T(8,128)S(1)} %down_kernel.4.refs_0_.refs_3_, bf16[2,2,16,2304]{3,2,1,0:T(8,128)(2,1)S(1)} %pack_kernel.5.refs_0_.refs_1_, ...), custom_call_target="tpu_custom_call" | custom-call | flops 1207959552 | bytes 294912 | tf_op jit(solution)/shard_map/down_kernel/pallas_call | solution.py:188
  61.0 3.7 %collective-permute-start.16 = (bf16[32,2048]{1,0:T(8,128)(2,1)S(1)}, bf16[32,2048]{1,0:T(8,128)(2,1)S(1)}, u32[]{:S(2)}, u32[]{:S(2)}) collective-permute-start(bf16[32,2048]{1,0:T(8,128)(2,1)S(1)} %get-tuple-element.44), channel_id=1, source_target_pairs={{0,12},{4,8},{8,4},{12,0},{1,13},{5,9},{9,5},{13,1},{2,14},{6,10},... | collective-permute-start | bytes 393224 | tf_op jit(solution)/shard_map/ppermute | solution.py:208
  64.7 0.8 %collective-permute-start.18 = (bf16[32,2048]{1,0:T(8,128)(2,1)S(1)}, bf16[32,2048]{1,0:T(8,128)(2,1)S(1)}, u32[]{:S(2)}, u32[]{:S(2)}) collective-permute-start(bf16[32,2048]{1,0:T(8,128)(2,1)S(1)} %get-tuple-element.46), channel_id=1, source_target_pairs={{0,4},{4,0},{8,12},{12,8},{1,5},{5,1},{9,13},{13,9},{2,6},{6,2},{1... | collective-permute-start | bytes 393224 | tf_op jit(solution)/shard_map/ppermute | solution.py:208
  65.5 3.8 %collective-permute-done.16.refs_2_ = bf16[32,2048]{1,0:T(8,128)(2,1)S(1)} collective-permute-done((bf16[32,2048]{1,0:T(8,128)(2,1)S(1)}, bf16[32,2048]{1,0:T(8,128)(2,1)S(1)}, u32[]{:S(2)}, u32[]{:S(2)}) %collective-permute-start.16) | collective-permute-done | bytes 131104 | tf_op jit(solution)/shard_map/ppermute | solution.py:208
  69.3 6.5 %collective-permute-done.17.refs_3_ = bf16[32,2048]{1,0:T(8,128)(2,1)S(1)} collective-permute-done((bf16[32,2048]{1,0:T(8,128)(2,1)S(1)}, bf16[32,2048]{1,0:T(8,128)(2,1)S(1)}, u32[]{:S(2)}, u32[]{:S(2)}) %collective-permute-start.17) | collective-permute-done | bytes 131104 | tf_op jit(solution)/shard_map/ppermute | solution.py:208
  75.9 0.7 final_kernel.1
  (29 shorter events, 1.0 us)
Async XLA Ops:
  0.0 18.2 %collective-permute-start.2 = (bf16[32,2048]{1,0:T(8,128)(2,1)}, bf16[32,2048]{1,0:T(8,128)(2,1)S(1)}, u32[]{:S(2)}, u32[]{:S(2)}) collective-permute-start(bf16[32,2048]{1,0:T(8,128)(2,1)} %refs_1_.12), channel_id=1, source_target_pairs={{0,12},{4,8},{8,4},{12,0},{1,13},{5,9},{9,5},{13,1},{2,14},{6,10},... | collective-permute-start | bytes 393224 | tf_op jit(solution)/shard_map/ppermute | solution.py:208
  5.0 13.1 %collective-permute-start.1 = (bf16[32,2048]{1,0:T(8,128)(2,1)}, bf16[32,2048]{1,0:T(8,128)(2,1)S(1)}, u32[]{:S(2)}, u32[]{:S(2)}) collective-permute-start(bf16[32,2048]{1,0:T(8,128)(2,1)} %refs_1_.12), channel_id=1, source_target_pairs={{0,8},{4,12},{8,0},{12,4},{1,9},{5,13},{9,1},{13,5},{2,10},{6,14},... | collective-permute-start | bytes 393224 | tf_op jit(solution)/shard_map/ppermute | solution.py:208
  5.1 13.2 %collective-permute-start = (bf16[32,2048]{1,0:T(8,128)(2,1)}, bf16[32,2048]{1,0:T(8,128)(2,1)S(1)}, u32[]{:S(2)}, u32[]{:S(2)}) collective-permute-start(bf16[32,2048]{1,0:T(8,128)(2,1)} %refs_1_.12), channel_id=1, source_target_pairs={{0,4},{4,0},{8,12},{12,8},{1,5},{5,1},{9,13},{13,9},{2,6},{6,2},{1... | collective-permute-start | bytes 393224 | tf_op jit(solution)/shard_map/ppermute | solution.py:208
  12.2 6.0 %copy-start = (bf16[32,2048]{1,0:T(8,128)(2,1)S(1)}, bf16[32,2048]{1,0:T(8,128)(2,1)}, u32[]{:S(2)}) copy-start(bf16[32,2048]{1,0:T(8,128)(2,1)} %refs_1_.12) | copy-start | bytes 393220
  20.9 3.0 %collective-permute-start.3 = (bf16[2,2,32,2304]{3,2,1,0:T(8,128)(2,1)S(1)}, bf16[2,2,32,2304]{3,2,1,0:T(8,128)(2,1)S(1)}, u32[]{:S(2)}, u32[]{:S(2)}) collective-permute-start(bf16[2,2,32,2304]{3,2,1,0:T(8,128)(2,1)S(1)} %get-tuple-element.29.refs_0_), channel_id=1, source_target_pairs={{0,1},{1,0},{2,3},{3,2},{4,5},{5,4},{6,7},{7,6},{8,9},{9,8},{10,11... | collective-permute-start | bytes 1769480 | tf_op jit(solution)/shard_map/ppermute | solution.py:202
  23.3 2.4 %collective-permute-start.4 = (bf16[2,2,32,2048]{3,2,1,0:T(8,128)(2,1)S(1)}, bf16[2,2,32,2048]{3,2,1,0:T(8,128)(2,1)S(1)}, u32[]{:S(2)}, u32[]{:S(2)}) collective-permute-start(bf16[2,2,32,2048]{3,2,1,0:T(8,128)(2,1)S(1)} %get-tuple-element.31.refs_0_), channel_id=1, source_target_pairs={{0,1},{1,0},{2,3},{3,2},{4,5},{5,4},{6,7},{7,6},{8,9},{9,8},{10,11... | collective-permute-start | bytes 1572872 | tf_op jit(solution)/shard_map/ppermute | solution.py:202
  24.0 11.1 %collective-permute-start.5 = (bf16[2,2,16,2304]{3,2,1,0:T(8,128)(2,1)S(1)}, bf16[2,2,16,2304]{3,2,1,0:T(8,128)(2,1)S(1)}, u32[]{:S(2)}, u32[]{:S(2)}) collective-permute-start(bf16[2,2,16,2304]{3,2,1,0:T(8,128)(2,1)S(1)} %get-tuple-element.37), channel_id=1, source_target_pairs={{0,2},{1,3},{2,0},{3,1},{4,6},{5,7},{6,4},{7,5},{8,10},{9,11},{10,... | collective-permute-start | bytes 884744 | tf_op jit(solution)/shard_map/ppermute | solution.py:205
  33.1 2.8 %collective-permute-start.7 = (bf16[1,2,32,2304]{3,2,1,0:T(8,128)(2,1)S(1)}, bf16[1,2,32,2304]{3,2,1,0:T(8,128)(2,1)S(1)}, u32[]{:S(2)}, u32[]{:S(2)}) collective-permute-start(bf16[1,2,32,2304]{3,2,1,0:T(8,128)(2,1)S(1)} %get-tuple-element.39), channel_id=1, source_target_pairs={{0,1},{1,0},{2,3},{3,2},{4,5},{5,4},{6,7},{7,6},{8,9},{9,8},{10,11... | collective-permute-start | bytes 884744 | tf_op jit(solution)/shard_map/ppermute | solution.py:202
  33.2 2.7 %collective-permute-start.6 = (bf16[1,2,32,2304]{3,2,1,0:T(8,128)(2,1)S(1)}, bf16[1,2,32,2304]{3,2,1,0:T(8,128)(2,1)S(1)}, u32[]{:S(2)}, u32[]{:S(2)}) collective-permute-start(bf16[1,2,32,2304]{3,2,1,0:T(8,128)(2,1)S(1)} %get-tuple-element.36.refs_0_), channel_id=1, source_target_pairs={{0,1},{1,0},{2,3},{3,2},{4,5},{5,4},{6,7},{7,6},{8,9},{9,8},{10,11... | collective-permute-start | bytes 884744 | tf_op jit(solution)/shard_map/ppermute | solution.py:202
  33.7 9.2 %collective-permute-start.8 = (bf16[2,2,16,2048]{3,2,1,0:T(8,128)(2,1)S(1)}, bf16[2,2,16,2048]{3,2,1,0:T(8,128)(2,1)S(1)}, u32[]{:S(2)}, u32[]{:S(2)}) collective-permute-start(bf16[2,2,16,2048]{3,2,1,0:T(8,128)(2,1)S(1)} %get-tuple-element.41), channel_id=1, source_target_pairs={{0,2},{1,3},{2,0},{3,1},{4,6},{5,7},{6,4},{7,5},{8,10},{9,11},{10,... | collective-permute-start | bytes 786440 | tf_op jit(solution)/shard_map/ppermute | solution.py:205
  35.2 11.3 %collective-permute-start.9 = (bf16[2,16,2304]{2,1,0:T(8,128)(2,1)S(1)}, bf16[2,16,2304]{2,1,0:T(8,128)(2,1)S(1)}, u32[]{:S(2)}, u32[]{:S(2)}) collective-permute-start(bf16[2,16,2304]{2,1,0:T(8,128)(2,1)S(1)} %hidden_kernel.3.refs_0_.refs_1_), channel_id=1, source_target_pairs={{0,2},{1,3},{2,0},{3,1},{4,6},{5,7},{6,4},{7,5},{8,10},{9,11},{10,... | collective-permute-start | bytes 442376 | tf_op jit(solution)/shard_map/ppermute | solution.py:205
  36.1 16.3 %collective-permute-start.10 = (bf16[2,2,16,2304]{3,2,1,0:T(8,128)(2,1)S(1)}, bf16[2,2,16,2304]{3,2,1,0:T(8,128)(2,1)S(1)}, u32[]{:S(2)}, u32[]{:S(2)}) collective-permute-start(bf16[2,2,16,2304]{3,2,1,0:T(8,128)(2,1)S(1)} %get-tuple-element.42), channel_id=1, source_target_pairs={{0,2},{1,3},{2,0},{3,1},{4,6},{5,7},{6,4},{7,5},{8,10},{9,11},{10,... | collective-permute-start | bytes 884744 | tf_op jit(solution)/shard_map/ppermute | solution.py:205
  46.6 7.9 %collective-permute-start.12 = (bf16[2,2,16,2304]{3,2,1,0:T(8,128)(2,1)S(1)}, bf16[2,2,16,2304]{3,2,1,0:T(8,128)(2,1)S(1)}, u32[]{:S(2)}, u32[]{:S(2)}) collective-permute-start(bf16[2,2,16,2304]{3,2,1,0:T(8,128)(2,1)S(1)} %pack_kernel.3.refs_0_.refs_1_), channel_id=1, source_target_pairs={{0,1},{1,0},{2,3},{3,2},{4,5},{5,4},{6,7},{7,6},{8,9},{9,8},{10,11... | collective-permute-start | bytes 884744 | tf_op jit(solution)/shard_map/ppermute | solution.py:202
  46.6 7.7 %collective-permute-start.11 = (bf16[2,16,2048]{2,1,0:T(8,128)(2,1)S(1)}, bf16[2,16,2048]{2,1,0:T(8,128)(2,1)S(1)}, u32[]{:S(2)}, u32[]{:S(2)}) collective-permute-start(bf16[2,16,2048]{2,1,0:T(8,128)(2,1)S(1)} %hidden_kernel.4.refs_0_.refs_1_), channel_id=1, source_target_pairs={{0,2},{1,3},{2,0},{3,1},{4,6},{5,7},{6,4},{7,5},{8,10},{9,11},{10,... | collective-permute-start | bytes 393224 | tf_op jit(solution)/shard_map/ppermute | solution.py:205
  52.5 5.5 %collective-permute-start.13 = (bf16[2,16,2304]{2,1,0:T(8,128)(2,1)S(1)}, bf16[2,16,2304]{2,1,0:T(8,128)(2,1)S(1)}, u32[]{:S(2)}, u32[]{:S(2)}) collective-permute-start(bf16[2,16,2304]{2,1,0:T(8,128)(2,1)S(1)} %hidden_kernel.5.refs_0_.refs_1_), channel_id=1, source_target_pairs={{0,2},{1,3},{2,0},{3,1},{4,6},{5,7},{6,4},{7,5},{8,10},{9,11},{10,... | collective-permute-start | bytes 442376 | tf_op jit(solution)/shard_map/ppermute | solution.py:205
  54.3 3.7 %collective-permute-start.14 = (bf16[2,2,16,2048]{3,2,1,0:T(8,128)(2,1)S(1)}, bf16[2,2,16,2048]{3,2,1,0:T(8,128)(2,1)S(1)}, u32[]{:S(2)}, u32[]{:S(2)}) collective-permute-start(bf16[2,2,16,2048]{3,2,1,0:T(8,128)(2,1)S(1)} %pack_kernel.4.refs_0_.refs_1_), channel_id=1, source_target_pairs={{0,1},{1,0},{2,3},{3,2},{4,5},{5,4},{6,7},{7,6},{8,9},{9,8},{10,11... | collective-permute-start | bytes 786440 | tf_op jit(solution)/shard_map/ppermute | solution.py:202
  58.0 1.6 %collective-permute-start.15 = (bf16[2,2,16,2304]{3,2,1,0:T(8,128)(2,1)S(1)}, bf16[2,2,16,2304]{3,2,1,0:T(8,128)(2,1)S(1)}, u32[]{:S(2)}, u32[]{:S(2)}) collective-permute-start(bf16[2,2,16,2304]{3,2,1,0:T(8,128)(2,1)S(1)} %pack_kernel.5.refs_0_.refs_1_), channel_id=1, source_target_pairs={{0,1},{1,0},{2,3},{3,2},{4,5},{5,4},{6,7},{7,6},{8,9},{9,8},{10,11... | collective-permute-start | bytes 884744 | tf_op jit(solution)/shard_map/ppermute | solution.py:202
  61.0 8.3 %collective-permute-start.16 = (bf16[32,2048]{1,0:T(8,128)(2,1)S(1)}, bf16[32,2048]{1,0:T(8,128)(2,1)S(1)}, u32[]{:S(2)}, u32[]{:S(2)}) collective-permute-start(bf16[32,2048]{1,0:T(8,128)(2,1)S(1)} %get-tuple-element.44), channel_id=1, source_target_pairs={{0,12},{4,8},{8,4},{12,0},{1,13},{5,9},{9,5},{13,1},{2,14},{6,10},... | collective-permute-start | bytes 393224 | tf_op jit(solution)/shard_map/ppermute | solution.py:208
  64.7 11.1 %collective-permute-start.17 = (bf16[32,2048]{1,0:T(8,128)(2,1)S(1)}, bf16[32,2048]{1,0:T(8,128)(2,1)S(1)}, u32[]{:S(2)}, u32[]{:S(2)}) collective-permute-start(bf16[32,2048]{1,0:T(8,128)(2,1)S(1)} %get-tuple-element.45), channel_id=1, source_target_pairs={{0,8},{4,12},{8,0},{12,4},{1,9},{5,13},{9,1},{13,5},{2,10},{6,14},... | collective-permute-start | bytes 393224 | tf_op jit(solution)/shard_map/ppermute | solution.py:208
  64.7 11.1 %collective-permute-start.18 = (bf16[32,2048]{1,0:T(8,128)(2,1)S(1)}, bf16[32,2048]{1,0:T(8,128)(2,1)S(1)}, u32[]{:S(2)}, u32[]{:S(2)}) collective-permute-start(bf16[32,2048]{1,0:T(8,128)(2,1)S(1)} %get-tuple-element.46), channel_id=1, source_target_pairs={{0,4},{4,0},{8,12},{12,8},{1,5},{5,1},{9,13},{13,9},{2,6},{6,2},{1... | collective-permute-start | bytes 393224 | tf_op jit(solution)/shard_map/ppermute | solution.py:208

commit v3 on v2

--- a/solution.py
+++ b/solution.py
@@ -58,40 +58,55 @@
             left[pl.ds(pl.multiple_of(at, rows), rows), :] = block[...]
 
 
-def put_sums(sums, halves, send_refs, keep_ref):
+def put_sums(sums, halves, send_refs, keep_ref, column):
     for which, value in enumerate(sums):
         quarter = value.shape[0] // (2 * halves)
+        columns = slice(column, column + value.shape[1])
         for h in range(halves):
             at = 2 * h * quarter
-            send_refs[h % len(send_refs)][h // len(send_refs), which] = value[at : at + quarter].astype(BF16)
-            keep_ref[h, which] = value[at + quarter : at + 2 * quarter]
+            send = send_refs[h % len(send_refs)]
+            send[h // len(send_refs), which, :, columns] = value[at : at + quarter].astype(BF16)
+            keep_ref[h, which, :, columns] = value[at + quarter : at + 2 * quarter]
 
 
 def split_parts(refs, halves, blocks):
     return [refs[h * blocks : (h + 1) * blocks] for h in range(halves)], refs[halves * blocks :]
 
 
-def held_gate_up_kernel(halves, blocks, *refs):
-    parts, (gate_ref, up_ref, *send_refs, keep_ref, left) = split_parts(refs, halves, blocks)
+def held_gate_up_kernel(halves, blocks, ahead, *refs):
+    parts, (gate_ref, up_ref, *refs) = split_parts(refs, halves, blocks)
+    copies = []
+    if ahead is not None:
+        sources, refs, sems = refs[:2], refs[2:-1], refs[-1]
+        copies = column_copies(ahead, sources, refs[2:4], sems)
+        refs = refs[:2] + refs[4:]
+    send_ref, keep_ref, left = refs
+    fetch_start(copies)
     order_rows(parts, left)
     sums = [jnp.dot(left[...], w[...], preferred_element_type=F32) for w in (gate_ref, up_ref)]
-    put_sums(sums, halves, send_refs, keep_ref)
-
-
-def gate_up_kernel(start, width, depth, slots, halves, blocks, *refs):
-    parts, (gate_ref, up_ref, *send_refs, keep_ref, left, held, sems) = split_parts(refs, halves, blocks)
+    put_sums(sums, halves, [send_ref], keep_ref, 0)
+    fetch_wait(copies)
+
+
+def gate_up_kernel(start, width, depth, slots, halves, blocks, sends, *refs):
+    parts, refs = split_parts(refs, halves, blocks)
+    held_refs, (gate_ref, up_ref), refs = refs[:2], refs[2:4], refs[4:]
+    send_refs, keep_ref, left, held, sems = refs[:sends], *refs[sends:]
+    before = held_refs[0].shape[1]
     total = 2 * (left.shape[1] // depth)
 
     def copy(i):
         source = (gate_ref, up_ref)[i % 2]
         slot = i % slots
         return pltpu.make_async_copy(
-            source.at[pl.ds(i // 2 * depth, depth), pl.ds(start, width)], held.at[slot], sems.at[slot]
+            source.at[pl.ds(i // 2 * depth, depth), pl.ds(start + before, width - before)], held.at[slot], sems.at[slot]
         )
 
     for i in range(min(slots, total)):
         copy(i).start()
     order_rows(parts, left)
+    sums = [jnp.dot(left[...], w[...], preferred_element_type=F32) for w in held_refs]
+    put_sums(sums, halves, send_refs, keep_ref, 0)
     sums = [None, None]
     for i in range(total):
         copy(i).wait()
@@ -99,7 +114,7 @@
         sums[i % 2] = product if i < 2 else sums[i % 2] + product
         if i + slots < total:
             copy(i + slots).start()
-    put_sums(sums, halves, send_refs, keep_ref)
+    put_sums(sums, halves, send_refs, keep_ref, before)
 
 
 def chip_sum_kernel(chips, halves, keep, *refs):
@@ -154,7 +169,7 @@
                 left[pl.ds(pl.multiple_of(at, rows), rows), :] = ref[j, h]
 
 
-def down_kernel(first, last, near_ref, far_ref, *refs):
+def down_kernel(first, direct, near_ref, far_ref, *refs):
     if not first:
         before_ref, refs = refs[0], refs[1:]
     down_ref, outs, left = refs[0], refs[1:-1], refs[-1]
@@ -162,16 +177,42 @@
     value = jnp.dot(left[...], down_ref[...], preferred_element_type=F32)
     if not first:
         value = value + before_ref[...]
-    rows = outs[0].shape[0]
-    for j, out in enumerate(outs):
-        out[...] = value[j * rows : (j + 1) * rows].astype(out.dtype)
-
-
-def final_kernel(own_ref, *refs):
-    value = own_ref[...]
-    for came in refs[:-1]:
-        value = value + came[...].astype(F32)
-    refs[-1][...] = value.astype(refs[-1].dtype)
+    if direct is None:
+        outs[0][...] = value
+        return
+    own_ref, soon_ref, *late_refs = outs
+    rows, width = own_ref.shape
+    blocks = value.shape[0] // rows
+    straight, held = late_refs[: blocks - 2], late_refs[blocks - 2 :]
+    own_ref[...] = value[:rows]
+    soon_ref[:, :width] = value[rows : 2 * rows].astype(BF16)
+    for j in range(2, blocks):
+        block = value[j * rows : (j + 1) * rows]
+        straight[j - 2][...] = block[:, :direct].astype(BF16)
+        if j % 2 == 0:
+            held[j // 2 - 1][...] = block[:, direct:]
+        else:
+            at = width + (j // 2 - 1) * (width - direct)
+            soon_ref[:, at : at + width - direct] = block[:, direct:].astype(BF16)
+
+
+def pair_sum_kernel(width, soon_ref, *refs):
+    count = len(refs) // 2
+    for held, out in zip(refs[:count], refs[count:]):
+        size = held.shape[1]
+        out[...] = (held[...] + soon_ref[:, width : width + size].astype(F32)).astype(BF16)
+        width += size
+
+
+def final_kernel(direct, count, own_ref, soon_ref, *refs):
+    straight, joined, out_ref = refs[:count], refs[count:-1], refs[-1]
+    width = own_ref.shape[1]
+    value = own_ref[...] + soon_ref[:, :width].astype(F32)
+    for side, arrays in ((slice(0, direct), straight), (slice(direct, width), joined)):
+        part = value[:, side]
+        for came in arrays:
+            part = part + came[...].astype(F32)
+        out_ref[:, side] = part.astype(out_ref.dtype)
 
 
 class Body:
@@ -207,38 +248,53 @@
     def along_z(self, value, j):
         return lax.ppermute(value, "hid", [(z, z ^ j) for z in range(self.groups)])
 
-    def gate_up(self, start, size, halves, weights, sends=1):
+    def gate_up_parts(self):
+        parts = [p for h in self.parts for p in h]
+        return parts, len(parts) * self.part
+
+    def held_gate_up(self, weights, ahead):
+        parts, rows = self.gate_up_parts()
+        size = weights[0].shape[1]
+        outs = [jax.ShapeDtypeStruct((2, 2, rows // 4, size), t) for t in (BF16, F32)]
+        ins, more = [WHOLE] * (len(parts) + 2), ()
+        scratch = [pltpu.VMEM((rows, self.width), BF16)]
+        if ahead is not None:
+            outs += [jax.ShapeDtypeStruct((self.width, ahead[1]), BF16)] * 2
+            ins, more = ins + [FAR] * 2, (self.gate_weight, self.up_weight)
+            scratch.append(pltpu.SemaphoreType.DMA((8,)))
+        got = self.call(
+            functools.partial(held_gate_up_kernel, 2, self.groups // 2, None if ahead is None else ahead[0]),
+            ins,
+            outs,
+            scratch,
+            4 * rows * self.width * size,
+            rows * self.width,
+            6 * MIB,
+            (*parts, *weights, *more),
+        )
+        return (got[1], self.other_core(got[0])), got[2:]
+
+    def gate_up(self, start, size, weights, sends):
+        parts, rows = self.gate_up_parts()
         width = self.width
-        parts = [p for h in halves for p in self.parts[h]]
-        rows = len(parts) * self.part
-        quarter = rows // (2 * len(halves))
-        outs = [jax.ShapeDtypeStruct((len(halves) // sends, 2, quarter, size), BF16)] * sends
-        outs.append(jax.ShapeDtypeStruct((len(halves), 2, quarter, size), F32))
-        left = pltpu.VMEM((rows, width), BF16)
-        count = (len(halves), self.groups // 2)
-        if weights is not None:
-            got = self.call(
-                functools.partial(held_gate_up_kernel, *count),
-                [WHOLE] * (len(parts) + 2),
-                outs,
-                [left],
-                4 * rows * width * size,
-                rows * width,
-                6 * MIB,
-                (*parts, *weights),
-            )
-        else:
-            depth, slots = largest(width, (512, 256)), 4
-            got = self.call(
-                functools.partial(gate_up_kernel, start, size, depth, slots, *count),
-                [WHOLE] * len(parts) + [FAR] * 2,
-                outs,
-                [left, pltpu.VMEM((slots, depth, size), BF16), pltpu.SemaphoreType.DMA((slots,))],
-                4 * rows * width * size,
-                4 * width * size,
-                16 * MIB,
-                (*parts, self.gate_weight, self.up_weight),
-            )
+        outs = [jax.ShapeDtypeStruct((2 // sends, 2, rows // 4, size), BF16)] * sends
+        outs.append(jax.ShapeDtypeStruct((2, 2, rows // 4, size), F32))
+        depth, slots = largest(width, (512, 256)), 8
+        streamed = size - weights[0].shape[1]
+        got = self.call(
+            functools.partial(gate_up_kernel, start, size, depth, slots, 2, self.groups // 2, sends),
+            [WHOLE] * (len(parts) + 2) + [FAR] * 2,
+            outs,
+            [
+                pltpu.VMEM((rows, width), BF16),
+                pltpu.VMEM((slots, depth, streamed), BF16),
+                pltpu.SemaphoreType.DMA((slots,)),
+            ],
+            4 * rows * width * size,
+            4 * width * size,
+            20 * MIB,
+            (*parts, *weights, self.gate_weight, self.up_weight),
+        )
         return got[-1], *(self.other_core(v) for v in got[:-1])
 
     def fetch(self, start, size):
@@ -301,15 +357,18 @@
         )
         return rows
 
-    def down(self, packed, before, weights, last):
+    def down(self, packed, before, weights, direct=None):
         size = weights.shape[0]
-        width, rows = self.width, 2 * self.half
-        if last:
-            outs = [jax.ShapeDtypeStruct((self.part, width), t) for t in [F32] + [BF16] * (self.groups - 1)]
+        width, rows, part = self.width, 2 * self.half, self.part
+        shape = jax.ShapeDtypeStruct
+        if direct is None:
+            outs = [shape((rows, width), F32)]
         else:
-            outs = [jax.ShapeDtypeStruct((rows, width), F32)]
+            pairs, joined = self.groups // 2 - 1, width - direct
+            outs = [shape((part, width), F32), shape((part, width + pairs * joined), BF16)]
+            outs += [shape((part, direct), BF16)] * (2 * pairs) + [shape((part, joined), F32)] * pairs
         return self.call(
-            functools.partial(down_kernel, not before, last),
+            functools.partial(down_kernel, not before, direct),
             [WHOLE] * (3 + len(before)),
             outs,
             [pltpu.VMEM((rows, size), BF16)],
@@ -339,11 +398,11 @@
 
         w0 = self.fetch(s0, n0)
         w1 = self.fetch(s1, n1)
-        a0 = self.gate_up(s0, n0, both, w0)
-        a1 = self.gate_up(s1, n1, both, w1)
+        a0, _ = self.held_gate_up(w0, None)
+        a1, w2 = self.held_gate_up(w1, (s2, count * 4 // 26 * step))
         b0 = self.chip_sum(both, a0)
+        a2 = self.gate_up(s2, n2, w2, 2)
         b1 = self.chip_sum(both, a1)
-        a2 = self.gate_up(s2, n2, both, None, 2)
         h0 = self.hidden(b0)
         b2 = self.chip_sum(both, a2)
         d0 = self.fetch_rows(s0, n0)
@@ -352,21 +411,36 @@
         p0 = self.pack(h0)
         d2 = self.fetch_rows(s2, n2)
         h2 = self.hidden(b2)
+        value = self.down(p0, [], d0)
         p1 = self.pack(h1)
-        value = self.down(p0, [], d0, False)
         p2 = self.pack(h2)
-        value = self.down(p1, value, d1, False)
-        own, *late = self.down(p2, value, d2, True)
-        arrived = [self.along_z(late[j - 1], j) for j in range(groups - 1, 0, -1)]
+        value = self.down(p1, value, d1)
+        direct = self.width // 128 * 10 // 16 * 128
+        own, soon, *late = self.down(p2, value, d2, direct)
+        straight, held = late[: groups - 2], late[groups - 2 :]
+        soon = self.along_z(soon, 1)
+        straight = [self.along_z(v, 2 + j) for j, v in enumerate(straight)]
+        size = self.width - direct
+        joined = self.call(
+            functools.partial(pair_sum_kernel, self.width),
+            [WHOLE] * (1 + len(held)),
+            [jax.ShapeDtypeStruct((self.part, size), BF16)] * len(held),
+            [],
+            256,
+            1024,
+            4 * MIB,
+            (soon, *held),
+        )
+        joined = [self.along_z(v, 2 + 2 * j) for j, v in enumerate(joined)]
         (mixed,) = self.call(
-            final_kernel,
-            [WHOLE] * groups,
+            functools.partial(final_kernel, direct, groups - 2),
+            [WHOLE] * (2 + len(straight) + len(joined)),
             [jax.ShapeDtypeStruct((self.part, self.width), BF16)],
             [],
-            groups * self.part * self.width,
-            4 * groups * self.part * self.width,
+            256,
+            1024,
             4 * MIB,
-            (own, *arrived),
+            (own, soon, *straight, *joined),
         )
         return mixed
 

time: 76.7 us -> 75.4 us (0.983)
  waiting for transfers between devices: 15.3 us -> 13.9 us
    ppermute x6 -> x7, waiting for transfers between devices: 10.4 us -> 6.13 us  [along_z(): return lax.ppermute(value, 'hid', [(z, z ^ j) for z in range(self.groups)])]
    ppermute x6 -> x7, starting transfers between devices: 10.1 us -> 13.6 us  [along_z(): return lax.ppermute(value, 'hid', [(z, z ^ j) for z in range(self.groups)])]
    ppermute x6, starting transfers between devices: 8.09 us -> 5.12 us  [along_x(): lax.ppermute(value, 'wid', [(w, (w // 2 + j) % self.chips * 2 + w % 2) fo...]
    ppermute x6, waiting for transfers between devices: 4.66 us -> 7.45 us  [along_x(): lax.ppermute(value, 'wid', [(w, (w // 2 + j) % self.chips * 2 + w % 2) fo...]
    pallas_call x21 -> x22, Pallas kernels: 41.5 us -> 41 us  [call(): pl.pallas_call(run, name=kernel.func.__name__ if isinstance(kernel, funct...]
  transfers between devices with their start and end apart: 19 -> 20, of which waited for: 7 -> 9; matrix products, arithmetic and copies ran while one was open for 0% -> 0% of each run, Pallas kernels for 48% -> 48%
where the time goes in v3:
time: 75.4 us; the launch traced here: 75.2 us
  Pallas kernels  41 us (54%)
  starting transfers between devices  20.1 us (27%)
  waiting for transfers between devices  13.9 us (18%)
    pallas_call x22, Pallas kernels, call(): pl.pallas_call(run, name=kernel.func.__name__ if isinstance(kernel, funct...  41 us
    ppermute x7, starting transfers between devices, along_z(): return lax.ppermute(value, 'hid', [(z, z ^ j) for z in range(self.groups)])  13.6 us
    ppermute x6, waiting for transfers between devices, along_x(): lax.ppermute(value, 'wid', [(w, (w // 2 + j) % self.chips * 2 + w % 2) fo...  7.45 us
    ppermute x7, waiting for transfers between devices, along_z(): return lax.ppermute(value, 'hid', [(z, z ^ j) for z in range(self.groups)])  6.13 us
    ppermute x6, starting transfers between devices, along_x(): lax.ppermute(value, 'wid', [(w, (w // 2 + j) % self.chips * 2 + w % 2) fo...  5.12 us
  transfers between devices with their start and end apart: 20, of which 9 were waited for; matrix products, arithmetic and copies ran while one was open for 0% of the time, Pallas kernels for 48%

profile of v3, /device:TPU:0, one launch (start us, length us, event | category | flops | bytes accessed | tf_op | source)
XLA Modules:
  0.0 75.2 jit_solution(8827922780049020795)
XLA Ops:
  0.0 5.0 %collective-permute-start.2 = (bf16[32,2048]{1,0:T(8,128)(2,1)}, bf16[32,2048]{1,0:T(8,128)(2,1)S(1)}, u32[]{:S(2)}, u32[]{:S(2)}) collective-permute-start(bf16[32,2048]{1,0:T(8,128)(2,1)} %refs_1_.12), channel_id=1, source_target_pairs={{0,12},{4,8},{8,4},{12,0},{1,13},{5,9},{9,5},{13,1},{2,14},{6,10},... | collective-permute-start | bytes 393224 | tf_op jit(solution)/shard_map/ppermute | solution.py:249
  5.1 0.6 collective-permute-start
  5.6 6.6 %fetch_kernel.2 = (bf16[2048,2304]{1,0:T(8,128)(2,1)S(1)}, bf16[2048,2304]{1,0:T(8,128)(2,1)S(1)}) custom-call(bf16[2048,6656]{1,0:T(8,128)(2,1)} %refs_7_.3, bf16[2048,6656]{1,0:T(8,128)(2,1)} %refs_8_.3), custom_call_target="tpu_custom_call" | custom-call | bytes 18874368 | tf_op jit(solution)/shard_map/fetch_kernel/pallas_call | solution.py:229
  12.2 6.0 %fetch_kernel.3 = (bf16[2048,2048]{1,0:T(8,128)(2,1)S(1)}, bf16[2048,2048]{1,0:T(8,128)(2,1)S(1)}) custom-call(bf16[2048,2304]{1,0:T(8,128)(2,1)S(1)} %get-tuple-element.29.refs_0_.refs_5_, bf16[2048,6656]{1,0:T(8,128)(2,1)} %refs_7_.3, bf16[2048,6656]{1,0:T(8,128)(2,1)} %refs_8_.3), custom_call_target="tpu_custom_call" | custom-call | bytes 16777216 | tf_op jit(solution)/shard_map/fetch_kernel/pallas_call | solution.py:229
  18.2 2.6 %held_gate_up_kernel.2 = (bf16[2,2,32,2304]{3,2,1,0:T(8,128)(2,1)S(1)}, f32[2,2,32,2304]{3,2,1,0:T(8,128)S(1)}) custom-call(bf16[2048,2048]{1,0:T(8,128)(2,1)S(1)} %get-tuple-element.30.refs_0_.refs_5_, bf16[32,2048]{1,0:T(8,128)(2,1)S(1)} %copy-done, bf16[32,2048]{1,0:T(8,128)(2,1)S(1)} %collective-permute-done.refs_2_, ...), custom_call_target="tpu_custom_call" | custom-call | flops 2415919104 | bytes 262144 | tf_op jit(solution)/shard_map/held_gate_up_kernel/pallas_call | solution.py:229
  20.9 3.6 %held_gate_up_kernel.3 = (bf16[2,2,32,2048]{3,2,1,0:T(8,128)(2,1)S(1)}, f32[2,2,32,2048]{3,2,1,0:T(8,128)S(1)}, bf16[2048,1024]{1,0:T(8,128)(2,1)S(1)}, bf16[2048,1024]{1,0:T(8,128)(2,1)S(1)}) custom-call(bf16[2,2,32,2304]{3,2,1,0:T(8,128)(2,1)S(1)} %get-tuple-element.32.refs_0_, bf16[32,2048]{1,0:T(8,128)(2,1)S(1)} %copy-done, ...), custom_call_target="tpu_custom_call" | custom-call | flops 2147483648 | bytes 262144 | tf_op jit(solution)/shard_map/held_gate_up_kernel/pallas_call | solution.py:229
  24.5 0.6 collective-permute-start.4
  25.2 1.8 %collective-permute-start.5 = (bf16[2,2,16,2304]{3,2,1,0:T(8,128)(2,1)S(1)}, bf16[2,2,16,2304]{3,2,1,0:T(8,128)(2,1)S(1)}, u32[]{:S(2)}, u32[]{:S(2)}) collective-permute-start(bf16[2,2,16,2304]{3,2,1,0:T(8,128)(2,1)S(1)} %get-tuple-element.42), channel_id=1, source_target_pairs={{0,2},{1,3},{2,0},{3,1},{4,6},{5,7},{6,4},{7,5},{8,10},{9,11},{10,... | collective-permute-start | bytes 884744 | tf_op jit(solution)/shard_map/ppermute | solution.py:246
  27.0 5.6 %gate_up_kernel.1 = (bf16[1,2,32,2304]{3,2,1,0:T(8,128)(2,1)S(1)}, bf16[1,2,32,2304]{3,2,1,0:T(8,128)(2,1)S(1)}, f32[2,2,32,2304]{3,2,1,0:T(8,128)S(1)}) custom-call(f32[2,2,16,2304]{3,2,1,0:T(8,128)S(1)} %get-tuple-element.36.refs_0_.refs_1_, bf16[32,2048]{1,0:T(8,128)(2,1)S(1)} %copy-done, bf16[32,2048]{1,0:T(8,128)(2,1)S(1)} %collective-permute-done.refs_2_, ...), custom_call_target="tpu_custom_call" | custom-call | flops 2415919104 | bytes 18874368 | tf_op jit(solution)/shard_map/gate_up_kernel/pallas_call | solution.py:229
  32.7 0.5 collective-permute-start.6
  33.3 0.4 collective-permute-start.8
  33.7 0.5 collective-permute-done.5.refs_2_
  34.3 1.8 %collective-permute-start.9 = (bf16[2,16,2304]{2,1,0:T(8,128)(2,1)S(1)}, bf16[2,16,2304]{2,1,0:T(8,128)(2,1)S(1)}, u32[]{:S(2)}, u32[]{:S(2)}) collective-permute-start(bf16[2,16,2304]{2,1,0:T(8,128)(2,1)S(1)} %hidden_kernel.3.refs_0_.refs_1_), channel_id=1, source_target_pairs={{0,2},{1,3},{2,0},{3,1},{4,6},{5,7},{6,4},{7,5},{8,10},{9,11},{10,... | collective-permute-start | bytes 442376 | tf_op jit(solution)/shard_map/ppermute | solution.py:246
  36.2 0.4 collective-permute-start.10
  36.6 3.8 %fetch_rows_kernel.3.refs_0_.refs_3_ = bf16[2304,2048]{1,0:T(8,128)(2,1)S(1)} custom-call(f32[2,2,16,2304]{3,2,1,0:T(8,128)S(1)} %get-tuple-element.45.refs_0_.refs_1_, bf16[6656,2048]{1,0:T(8,128)(2,1)} %refs_1_.15), custom_call_target="tpu_custom_call" | custom-call | bytes 9437184 | tf_op jit(solution)/shard_map/fetch_rows_kernel/pallas_call | solution.py:229
  40.4 2.1 %collective-permute-done.8.refs_2_ = bf16[2,2,16,2048]{3,2,1,0:T(8,128)(2,1)S(1)} collective-permute-done((bf16[2,2,16,2048]{3,2,1,0:T(8,128)(2,1)S(1)}, bf16[2,2,16,2048]{3,2,1,0:T(8,128)(2,1)S(1)}, u32[]{:S(2)}, u32[]{:S(2)}) %collective-permute-start.8) | collective-permute-done | bytes 262176 | tf_op jit(solution)/shard_map/ppermute | solution.py:246
  42.6 3.5 %fetch_rows_kernel.4.refs_0_.refs_4_ = bf16[2048,2048]{1,0:T(8,128)(2,1)S(1)} custom-call(bf16[2,16,2048]{2,1,0:T(8,128)(2,1)S(1)} %hidden_kernel.4.refs_0_.refs_1_, bf16[6656,2048]{1,0:T(8,128)(2,1)} %refs_1_.15), custom_call_target="tpu_custom_call" | custom-call | bytes 8388608 | tf_op jit(solution)/shard_map/fetch_rows_kernel/pallas_call | solution.py:229
  46.2 0.4 collective-permute-start.12
  46.6 3.8 %fetch_rows_kernel.5.refs_0_.refs_4_ = bf16[2304,2048]{1,0:T(8,128)(2,1)S(1)} custom-call(bf16[2,2,16,2304]{3,2,1,0:T(8,128)(2,1)S(1)} %pack_kernel.3.refs_0_.refs_1_, bf16[6656,2048]{1,0:T(8,128)(2,1)} %refs_1_.15), custom_call_target="tpu_custom_call" | custom-call | bytes 9437184 | tf_op jit(solution)/shard_map/fetch_rows_kernel/pallas_call | solution.py:229
  50.5 1.5 %collective-permute-done.10.refs_2_ = bf16[2,2,16,2304]{3,2,1,0:T(8,128)(2,1)S(1)} collective-permute-done((bf16[2,2,16,2304]{3,2,1,0:T(8,128)(2,1)S(1)}, bf16[2,2,16,2304]{3,2,1,0:T(8,128)(2,1)S(1)}, u32[]{:S(2)}, u32[]{:S(2)}) %collective-permute-start.10) | collective-permute-done | bytes 294944 | tf_op jit(solution)/shard_map/ppermute | solution.py:246
  52.1 0.4 collective-permute-start.13
  52.5 1.4 %down_kernel.3.refs_0_.refs_3_ = f32[128,2048]{1,0:T(8,128)S(1)} custom-call(bf16[2,16,2304]{2,1,0:T(8,128)(2,1)S(1)} %hidden_kernel.5.refs_0_.refs_1_, bf16[2,2,16,2304]{3,2,1,0:T(8,128)(2,1)S(1)} %pack_kernel.3.refs_0_.refs_1_, bf16[2,2,16,2304]{3,2,1,0:T(8,128)(2,1)S(1)} %collective-permute-done.11.refs_2_, ...), custom_call_target="tpu_custom_call" | custom-call | flops 1207959552 | bytes 294912 | tf_op jit(solution)/shard_map/down_kernel/pallas_call | solution.py:229
  53.9 0.4 collective-permute-done.12.refs_2_
  54.4 2.9 %collective-permute-done.13.refs_2_ = bf16[2,16,2304]{2,1,0:T(8,128)(2,1)S(1)} collective-permute-done((bf16[2,16,2304]{2,1,0:T(8,128)(2,1)S(1)}, bf16[2,16,2304]{2,1,0:T(8,128)(2,1)S(1)}, u32[]{:S(2)}, u32[]{:S(2)}) %collective-permute-start.13) | collective-permute-done | bytes 147488 | tf_op jit(solution)/shard_map/ppermute | solution.py:246
  57.4 1.3 %down_kernel.4.refs_0_.refs_3_ = f32[128,2048]{1,0:T(8,128)S(1)} custom-call(bf16[2,2,16,2304]{3,2,1,0:T(8,128)(2,1)S(1)} %pack_kernel.5.refs_0_.refs_1_, bf16[2,2,16,2048]{3,2,1,0:T(8,128)(2,1)S(1)} %pack_kernel.4.refs_0_.refs_1_, bf16[2,2,16,2048]{3,2,1,0:T(8,128)(2,1)S(1)} %collective-permute-done.14.refs_2_, f32[128,2048]{1,0:T(8,128)S(1)} %down_kernel.3.refs_0_.refs_3_, ...), custom_call_target="tpu_custom_call" | custom-call | flops 1073741824 | bytes 262144 | tf_op jit(solution)/shard_map/down_kernel/pallas_call | solution.py:229
  59.0 1.4 %down_kernel.5 = (f32[32,2048]{1,0:T(8,128)S(1)}, bf16[32,2816]{1,0:T(8,128)(2,1)S(1)}, bf16[32,1280]{1,0:T(8,128)(2,1)S(1)}, bf16[32,1280]{1,0:T(8,128)(2,1)S(1)}, f32[32,768]{1,0:T(8,128)S(1)}) custom-call(f32[128,2048]{1,0:T(8,128)S(1)} %down_kernel.4.refs_0_.refs_3_, bf16[2,2,16,2304]{3,2,1,0:T(8,128)(2,1)S(1)} %pack_kernel.5.refs_0_.refs_1_, ...), custom_call_target="tpu_custom_call" | custom-call | flops 1207959552 | bytes 294912 | tf_op jit(solution)/shard_map/down_kernel/pallas_call | solution.py:229
  60.4 1.3 %collective-permute-start.16 = (bf16[32,2816]{1,0:T(8,128)(2,1)S(1)}, bf16[32,2816]{1,0:T(8,128)(2,1)S(1)}, u32[]{:S(2)}, u32[]{:S(2)}) collective-permute-start(bf16[32,2816]{1,0:T(8,128)(2,1)S(1)} %get-tuple-element.49), channel_id=1, source_target_pairs={{0,4},{4,0},{8,12},{12,8},{1,5},{5,1},{9,13},{13,9},{2,6},{6,2},{1... | collective-permute-start | bytes 540680 | tf_op jit(solution)/shard_map/ppermute | solution.py:249
  61.7 2.9 %collective-permute-start.17 = (bf16[32,1280]{1,0:T(8,128)(2,1)S(1)}, bf16[32,1280]{1,0:T(8,128)(2,1)S(1)}, u32[]{:S(2)}, u32[]{:S(2)}) collective-permute-start(bf16[32,1280]{1,0:T(8,128)(2,1)S(1)} %get-tuple-element.51), channel_id=1, source_target_pairs={{0,8},{4,12},{8,0},{12,4},{1,9},{5,13},{9,1},{13,5},{2,10},{6,14},... | collective-permute-start | bytes 245768 | tf_op jit(solution)/shard_map/ppermute | solution.py:249
  64.8 4.1 %collective-permute-done.16.refs_1_.refs_2_ = bf16[32,2816]{1,0:T(8,128)(2,1)S(1)} collective-permute-done((bf16[32,2816]{1,0:T(8,128)(2,1)S(1)}, bf16[32,2816]{1,0:T(8,128)(2,1)S(1)}, u32[]{:S(2)}, u32[]{:S(2)}) %collective-permute-start.16) | collective-permute-done | bytes 180256 | tf_op jit(solution)/shard_map/ppermute | solution.py:249
  68.9 3.5 %collective-permute-start.19 = (bf16[32,768]{1,0:T(8,128)(2,1)S(1)}, bf16[32,768]{1,0:T(8,128)(2,1)S(1)}, u32[]{:S(2)}, u32[]{:S(2)}) collective-permute-start(bf16[32,768]{1,0:T(8,128)(2,1)S(1)} %pair_sum_kernel.1.refs_0_), channel_id=1, source_target_pairs={{0,8},{4,12},{8,0},{12,4},{1,9},{5,13},{9,1},{13,5},{2,10},{6,14},... | collective-permute-start | bytes 147464 | tf_op jit(solution)/shard_map/ppermute | solution.py:249
  72.6 1.9 %collective-permute-done.19.refs_5_ = bf16[32,768]{1,0:T(8,128)(2,1)S(1)} collective-permute-done((bf16[32,768]{1,0:T(8,128)(2,1)S(1)}, bf16[32,768]{1,0:T(8,128)(2,1)S(1)}, u32[]{:S(2)}, u32[]{:S(2)}) %collective-permute-start.19) | collective-permute-done | bytes 49184 | tf_op jit(solution)/shard_map/ppermute | solution.py:249
  74.5 0.7 final_kernel.1
  (32 shorter events, 1.8 us)
Async XLA Ops:
  0.0 18.2 %collective-permute-start.2 = (bf16[32,2048]{1,0:T(8,128)(2,1)}, bf16[32,2048]{1,0:T(8,128)(2,1)S(1)}, u32[]{:S(2)}, u32[]{:S(2)}) collective-permute-start(bf16[32,2048]{1,0:T(8,128)(2,1)} %refs_1_.12), channel_id=1, source_target_pairs={{0,12},{4,8},{8,4},{12,0},{1,13},{5,9},{9,5},{13,1},{2,14},{6,10},... | collective-permute-start | bytes 393224 | tf_op jit(solution)/shard_map/ppermute | solution.py:249
  5.0 13.1 %collective-permute-start.1 = (bf16[32,2048]{1,0:T(8,128)(2,1)}, bf16[32,2048]{1,0:T(8,128)(2,1)S(1)}, u32[]{:S(2)}, u32[]{:S(2)}) collective-permute-start(bf16[32,2048]{1,0:T(8,128)(2,1)} %refs_1_.12), channel_id=1, source_target_pairs={{0,8},{4,12},{8,0},{12,4},{1,9},{5,13},{9,1},{13,5},{2,10},{6,14},... | collective-permute-start | bytes 393224 | tf_op jit(solution)/shard_map/ppermute | solution.py:249
  5.1 13.2 %collective-permute-start = (bf16[32,2048]{1,0:T(8,128)(2,1)}, bf16[32,2048]{1,0:T(8,128)(2,1)S(1)}, u32[]{:S(2)}, u32[]{:S(2)}) collective-permute-start(bf16[32,2048]{1,0:T(8,128)(2,1)} %refs_1_.12), channel_id=1, source_target_pairs={{0,4},{4,0},{8,12},{12,8},{1,5},{5,1},{9,13},{13,9},{2,6},{6,2},{1... | collective-permute-start | bytes 393224 | tf_op jit(solution)/shard_map/ppermute | solution.py:249
  12.2 6.0 %copy-start = (bf16[32,2048]{1,0:T(8,128)(2,1)S(1)}, bf16[32,2048]{1,0:T(8,128)(2,1)}, u32[]{:S(2)}) copy-start(bf16[32,2048]{1,0:T(8,128)(2,1)} %refs_1_.12) | copy-start | bytes 393220
  20.9 4.2 %collective-permute-start.3 = (bf16[2,2,32,2304]{3,2,1,0:T(8,128)(2,1)S(1)}, bf16[2,2,32,2304]{3,2,1,0:T(8,128)(2,1)S(1)}, u32[]{:S(2)}, u32[]{:S(2)}) collective-permute-start(bf16[2,2,32,2304]{3,2,1,0:T(8,128)(2,1)S(1)} %get-tuple-element.32.refs_0_), channel_id=1, source_target_pairs={{0,1},{1,0},{2,3},{3,2},{4,5},{5,4},{6,7},{7,6},{8,9},{9,8},{10,11... | collective-permute-start | bytes 1769480 | tf_op jit(solution)/shard_map/ppermute | solution.py:243
  24.5 8.7 %collective-permute-start.4 = (bf16[2,2,32,2048]{3,2,1,0:T(8,128)(2,1)S(1)}, bf16[2,2,32,2048]{3,2,1,0:T(8,128)(2,1)S(1)}, u32[]{:S(2)}, u32[]{:S(2)}) collective-permute-start(bf16[2,2,32,2048]{3,2,1,0:T(8,128)(2,1)S(1)} %get-tuple-element.34.refs_0_), channel_id=1, source_target_pairs={{0,1},{1,0},{2,3},{3,2},{4,5},{5,4},{6,7},{7,6},{8,9},{9,8},{10,11... | collective-permute-start | bytes 1572872 | tf_op jit(solution)/shard_map/ppermute | solution.py:243
  25.2 9.0 %collective-permute-start.5 = (bf16[2,2,16,2304]{3,2,1,0:T(8,128)(2,1)S(1)}, bf16[2,2,16,2304]{3,2,1,0:T(8,128)(2,1)S(1)}, u32[]{:S(2)}, u32[]{:S(2)}) collective-permute-start(bf16[2,2,16,2304]{3,2,1,0:T(8,128)(2,1)S(1)} %get-tuple-element.42), channel_id=1, source_target_pairs={{0,2},{1,3},{2,0},{3,1},{4,6},{5,7},{6,4},{7,5},{8,10},{9,11},{10,... | collective-permute-start | bytes 884744 | tf_op jit(solution)/shard_map/ppermute | solution.py:246
  32.6 3.5 %collective-permute-start.7 = (bf16[1,2,32,2304]{3,2,1,0:T(8,128)(2,1)S(1)}, bf16[1,2,32,2304]{3,2,1,0:T(8,128)(2,1)S(1)}, u32[]{:S(2)}, u32[]{:S(2)}) collective-permute-start(bf16[1,2,32,2304]{3,2,1,0:T(8,128)(2,1)S(1)} %get-tuple-element.44), channel_id=1, source_target_pairs={{0,1},{1,0},{2,3},{3,2},{4,5},{5,4},{6,7},{7,6},{8,9},{9,8},{10,11... | collective-permute-start | bytes 884744 | tf_op jit(solution)/shard_map/ppermute | solution.py:243
  32.7 3.4 %collective-permute-start.6 = (bf16[1,2,32,2304]{3,2,1,0:T(8,128)(2,1)S(1)}, bf16[1,2,32,2304]{3,2,1,0:T(8,128)(2,1)S(1)}, u32[]{:S(2)}, u32[]{:S(2)}) collective-permute-start(bf16[1,2,32,2304]{3,2,1,0:T(8,128)(2,1)S(1)} %get-tuple-element.39.refs_0_), channel_id=1, source_target_pairs={{0,1},{1,0},{2,3},{3,2},{4,5},{5,4},{6,7},{7,6},{8,9},{9,8},{10,11... | collective-permute-start | bytes 884744 | tf_op jit(solution)/shard_map/ppermute | solution.py:243
  33.3 9.2 %collective-permute-start.8 = (bf16[2,2,16,2048]{3,2,1,0:T(8,128)(2,1)S(1)}, bf16[2,2,16,2048]{3,2,1,0:T(8,128)(2,1)S(1)}, u32[]{:S(2)}, u32[]{:S(2)}) collective-permute-start(bf16[2,2,16,2048]{3,2,1,0:T(8,128)(2,1)S(1)} %get-tuple-element.46), channel_id=1, source_target_pairs={{0,2},{1,3},{2,0},{3,1},{4,6},{5,7},{6,4},{7,5},{8,10},{9,11},{10,... | collective-permute-start | bytes 786440 | tf_op jit(solution)/shard_map/ppermute | solution.py:246
  34.3 11.8 %collective-permute-start.9 = (bf16[2,16,2304]{2,1,0:T(8,128)(2,1)S(1)}, bf16[2,16,2304]{2,1,0:T(8,128)(2,1)S(1)}, u32[]{:S(2)}, u32[]{:S(2)}) collective-permute-start(bf16[2,16,2304]{2,1,0:T(8,128)(2,1)S(1)} %hidden_kernel.3.refs_0_.refs_1_), channel_id=1, source_target_pairs={{0,2},{1,3},{2,0},{3,1},{4,6},{5,7},{6,4},{7,5},{8,10},{9,11},{10,... | collective-permute-start | bytes 442376 | tf_op jit(solution)/shard_map/ppermute | solution.py:246
  36.2 15.7 %collective-permute-start.10 = (bf16[2,2,16,2304]{3,2,1,0:T(8,128)(2,1)S(1)}, bf16[2,2,16,2304]{3,2,1,0:T(8,128)(2,1)S(1)}, u32[]{:S(2)}, u32[]{:S(2)}) collective-permute-start(bf16[2,2,16,2304]{3,2,1,0:T(8,128)(2,1)S(1)} %get-tuple-element.47), channel_id=1, source_target_pairs={{0,2},{1,3},{2,0},{3,1},{4,6},{5,7},{6,4},{7,5},{8,10},{9,11},{10,... | collective-permute-start | bytes 884744 | tf_op jit(solution)/shard_map/ppermute | solution.py:246
  46.2 6.3 %collective-permute-start.11 = (bf16[2,2,16,2304]{3,2,1,0:T(8,128)(2,1)S(1)}, bf16[2,2,16,2304]{3,2,1,0:T(8,128)(2,1)S(1)}, u32[]{:S(2)}, u32[]{:S(2)}) collective-permute-start(bf16[2,2,16,2304]{3,2,1,0:T(8,128)(2,1)S(1)} %pack_kernel.3.refs_0_.refs_1_), channel_id=1, source_target_pairs={{0,1},{1,0},{2,3},{3,2},{4,5},{5,4},{6,7},{7,6},{8,9},{9,8},{10,11... | collective-permute-start | bytes 884744 | tf_op jit(solution)/shard_map/ppermute | solution.py:243
  46.2 8.1 %collective-permute-start.12 = (bf16[2,16,2048]{2,1,0:T(8,128)(2,1)S(1)}, bf16[2,16,2048]{2,1,0:T(8,128)(2,1)S(1)}, u32[]{:S(2)}, u32[]{:S(2)}) collective-permute-start(bf16[2,16,2048]{2,1,0:T(8,128)(2,1)S(1)} %hidden_kernel.4.refs_0_.refs_1_), channel_id=1, source_target_pairs={{0,2},{1,3},{2,0},{3,1},{4,6},{5,7},{6,4},{7,5},{8,10},{9,11},{10,... | collective-permute-start | bytes 393224 | tf_op jit(solution)/shard_map/ppermute | solution.py:246
  52.1 5.2 %collective-permute-start.13 = (bf16[2,16,2304]{2,1,0:T(8,128)(2,1)S(1)}, bf16[2,16,2304]{2,1,0:T(8,128)(2,1)S(1)}, u32[]{:S(2)}, u32[]{:S(2)}) collective-permute-start(bf16[2,16,2304]{2,1,0:T(8,128)(2,1)S(1)} %hidden_kernel.5.refs_0_.refs_1_), channel_id=1, source_target_pairs={{0,2},{1,3},{2,0},{3,1},{4,6},{5,7},{6,4},{7,5},{8,10},{9,11},{10,... | collective-permute-start | bytes 442376 | tf_op jit(solution)/shard_map/ppermute | solution.py:246
  54.4 3.1 %collective-permute-start.14 = (bf16[2,2,16,2048]{3,2,1,0:T(8,128)(2,1)S(1)}, bf16[2,2,16,2048]{3,2,1,0:T(8,128)(2,1)S(1)}, u32[]{:S(2)}, u32[]{:S(2)}) collective-permute-start(bf16[2,2,16,2048]{3,2,1,0:T(8,128)(2,1)S(1)} %pack_kernel.4.refs_0_.refs_1_), channel_id=1, source_target_pairs={{0,1},{1,0},{2,3},{3,2},{4,5},{5,4},{6,7},{7,6},{8,9},{9,8},{10,11... | collective-permute-start | bytes 786440 | tf_op jit(solution)/shard_map/ppermute | solution.py:243
  57.3 1.6 %collective-permute-start.15 = (bf16[2,2,16,2304]{3,2,1,0:T(8,128)(2,1)S(1)}, bf16[2,2,16,2304]{3,2,1,0:T(8,128)(2,1)S(1)}, u32[]{:S(2)}, u32[]{:S(2)}) collective-permute-start(bf16[2,2,16,2304]{3,2,1,0:T(8,128)(2,1)S(1)} %pack_kernel.5.refs_0_.refs_1_), channel_id=1, source_target_pairs={{0,1},{1,0},{2,3},{3,2},{4,5},{5,4},{6,7},{7,6},{8,9},{9,8},{10,11... | collective-permute-start | bytes 884744 | tf_op jit(solution)/shard_map/ppermute | solution.py:243
  60.4 8.5 %collective-permute-start.16 = (bf16[32,2816]{1,0:T(8,128)(2,1)S(1)}, bf16[32,2816]{1,0:T(8,128)(2,1)S(1)}, u32[]{:S(2)}, u32[]{:S(2)}) collective-permute-start(bf16[32,2816]{1,0:T(8,128)(2,1)S(1)} %get-tuple-element.49), channel_id=1, source_target_pairs={{0,4},{4,0},{8,12},{12,8},{1,5},{5,1},{9,13},{13,9},{2,6},{6,2},{1... | collective-permute-start | bytes 540680 | tf_op jit(solution)/shard_map/ppermute | solution.py:249
  61.7 10.8 %collective-permute-start.17 = (bf16[32,1280]{1,0:T(8,128)(2,1)S(1)}, bf16[32,1280]{1,0:T(8,128)(2,1)S(1)}, u32[]{:S(2)}, u32[]{:S(2)}) collective-permute-start(bf16[32,1280]{1,0:T(8,128)(2,1)S(1)} %get-tuple-element.51), channel_id=1, source_target_pairs={{0,8},{4,12},{8,0},{12,4},{1,9},{5,13},{9,1},{13,5},{2,10},{6,14},... | collective-permute-start | bytes 245768 | tf_op jit(solution)/shard_map/ppermute | solution.py:249
  64.6 8.0 %collective-permute-start.18 = (bf16[32,1280]{1,0:T(8,128)(2,1)S(1)}, bf16[32,1280]{1,0:T(8,128)(2,1)S(1)}, u32[]{:S(2)}, u32[]{:S(2)}) collective-permute-start(bf16[32,1280]{1,0:T(8,128)(2,1)S(1)} %get-tuple-element.52), channel_id=1, source_target_pairs={{0,12},{4,8},{8,4},{12,0},{1,13},{5,9},{9,5},{13,1},{2,14},{6,10},... | collective-permute-start | bytes 245768 | tf_op jit(solution)/shard_map/ppermute | solution.py:249
  68.9 5.6 %collective-permute-start.19 = (bf16[32,768]{1,0:T(8,128)(2,1)S(1)}, bf16[32,768]{1,0:T(8,128)(2,1)S(1)}, u32[]{:S(2)}, u32[]{:S(2)}) collective-permute-start(bf16[32,768]{1,0:T(8,128)(2,1)S(1)} %pair_sum_kernel.1.refs_0_), channel_id=1, source_target_pairs={{0,8},{4,12},{8,0},{12,4},{1,9},{5,13},{9,1},{13,5},{2,10},{6,14},... | collective-permute-start | bytes 147464 | tf_op jit(solution)/shard_map/ppermute | solution.py:249

commit v4 on v3

--- a/solution.py
+++ b/solution.py
@@ -73,8 +73,9 @@
     return [refs[h * blocks : (h + 1) * blocks] for h in range(halves)], refs[halves * blocks :]
 
 
-def held_gate_up_kernel(halves, blocks, ahead, *refs):
-    parts, (gate_ref, up_ref, *refs) = split_parts(refs, halves, blocks)
+def held_gate_up_kernel(halves, blocks, pieces, ahead, *refs):
+    parts, refs = split_parts(refs, halves, blocks)
+    pairs, refs = [refs[2 * p : 2 * p + 2] for p in range(pieces)], refs[2 * pieces :]
     copies = []
     if ahead is not None:
         sources, refs, sems = refs[:2], refs[2:-1], refs[-1]
@@ -83,8 +84,11 @@
     send_ref, keep_ref, left = refs
     fetch_start(copies)
     order_rows(parts, left)
-    sums = [jnp.dot(left[...], w[...], preferred_element_type=F32) for w in (gate_ref, up_ref)]
-    put_sums(sums, halves, [send_ref], keep_ref, 0)
+    column = 0
+    for pair in pairs:
+        sums = [jnp.dot(left[...], w[...], preferred_element_type=F32) for w in pair]
+        put_sums(sums, halves, [send_ref], keep_ref, column)
+        column += pair[0].shape[1]
     fetch_wait(copies)
 
 
@@ -252,18 +256,19 @@
         parts = [p for h in self.parts for p in h]
         return parts, len(parts) * self.part
 
-    def held_gate_up(self, weights, ahead):
+    def held_gate_up(self, pairs, ahead):
+        weights = [w for pair in pairs for w in pair]
         parts, rows = self.gate_up_parts()
-        size = weights[0].shape[1]
+        size = sum(w.shape[1] for w in weights) // 2
         outs = [jax.ShapeDtypeStruct((2, 2, rows // 4, size), t) for t in (BF16, F32)]
-        ins, more = [WHOLE] * (len(parts) + 2), ()
+        ins, more = [WHOLE] * (len(parts) + len(weights)), ()
         scratch = [pltpu.VMEM((rows, self.width), BF16)]
         if ahead is not None:
             outs += [jax.ShapeDtypeStruct((self.width, ahead[1]), BF16)] * 2
             ins, more = ins + [FAR] * 2, (self.gate_weight, self.up_weight)
-            scratch.append(pltpu.SemaphoreType.DMA((8,)))
+            scratch.append(pltpu.SemaphoreType.DMA((2,)))
         got = self.call(
-            functools.partial(held_gate_up_kernel, 2, self.groups // 2, None if ahead is None else ahead[0]),
+            functools.partial(held_gate_up_kernel, 2, self.groups // 2, len(pairs), None if ahead is None else ahead[0]),
             ins,
             outs,
             scratch,
@@ -292,7 +297,7 @@
             ],
             4 * rows * width * size,
             4 * width * size,
-            20 * MIB,
+            26 * MIB,
             (*parts, *weights, self.gate_weight, self.up_weight),
         )
         return got[-1], *(self.other_core(v) for v in got[:-1])
@@ -302,7 +307,7 @@
             functools.partial(fetch_kernel, start),
             [FAR] * 2,
             [jax.ShapeDtypeStruct((self.width, size), BF16)] * 2,
-            [pltpu.SemaphoreType.DMA((8,))],
+            [pltpu.SemaphoreType.DMA((2,))],
             0,
             4 * self.width * size,
             2 * MIB,
@@ -349,7 +354,7 @@
             functools.partial(fetch_rows_kernel, start),
             [FAR],
             [jax.ShapeDtypeStruct((size, self.width), BF16)],
-            [pltpu.SemaphoreType.DMA((4,))],
+            [pltpu.SemaphoreType.DMA((1,))],
             0,
             2 * self.width * size,
             2 * MIB,
@@ -396,10 +401,11 @@
         blocks = [tokens] + [self.along_z(tokens, j) for j in range(1, groups)]
         self.parts = (blocks[: groups // 2], blocks[groups // 2 :])
 
+        part = count * 6 // 26 * step
         w0 = self.fetch(s0, n0)
-        w1 = self.fetch(s1, n1)
-        a0, _ = self.held_gate_up(w0, None)
-        a1, w2 = self.held_gate_up(w1, (s2, count * 4 // 26 * step))
+        w1 = self.fetch(s1, part)
+        a0, rest = self.held_gate_up([w0], (s1 + part, n1 - part))
+        a1, w2 = self.held_gate_up([w1, rest], (s2, count * 2 // 26 * step))
         b0 = self.chip_sum(both, a0)
         a2 = self.gate_up(s2, n2, w2, 2)
         b1 = self.chip_sum(both, a1)

time: 75.4 us -> 74.2 us (0.984)
  Pallas kernels: 41 us -> 39.4 us
    pallas_call x22, Pallas kernels: 41 us -> 39.4 us  [call(): pl.pallas_call(run, name=kernel.func.__name__ if isinstance(kernel, funct...]
  transfers between devices with their start and end apart: 20 -> 20, of which waited for: 9 -> 8; matrix products, arithmetic and copies ran while one was open for 0% -> 0% of each run, Pallas kernels for 48% -> 46%
where the time goes in v4:
time: 74.2 us; the launch traced here: 73.9 us
  Pallas kernels  39.4 us (53%)
  starting transfers between devices  20.1 us (27%)
  waiting for transfers between devices  14.2 us (19%)
    pallas_call x22, Pallas kernels, call(): pl.pallas_call(run, name=kernel.func.__name__ if isinstance(kernel, funct...  39.4 us
    ppermute x7, starting transfers between devices, along_z(): return lax.ppermute(value, 'hid', [(z, z ^ j) for z in range(self.groups)])  13.6 us
    ppermute x6, waiting for transfers between devices, along_x(): lax.ppermute(value, 'wid', [(w, (w // 2 + j) % self.chips * 2 + w % 2) fo...  7.84 us
    ppermute x7, waiting for transfers between devices, along_z(): return lax.ppermute(value, 'hid', [(z, z ^ j) for z in range(self.groups)])  6.13 us
    ppermute x6, starting transfers between devices, along_x(): lax.ppermute(value, 'wid', [(w, (w // 2 + j) % self.chips * 2 + w % 2) fo...  5.07 us
  transfers between devices with their start and end apart: 20, of which 8 were waited for; matrix products, arithmetic and copies ran while one was open for 0% of the time, Pallas kernels for 46%

profile of v4, /device:TPU:0, one launch (start us, length us, event | category | flops | bytes accessed | tf_op | source)
XLA Modules:
  0.0 73.9 jit_solution(6106517380064195384)
XLA Ops:
  0.0 5.0 %collective-permute-start.2 = (bf16[32,2048]{1,0:T(8,128)(2,1)}, bf16[32,2048]{1,0:T(8,128)(2,1)S(1)}, u32[]{:S(2)}, u32[]{:S(2)}) collective-permute-start(bf16[32,2048]{1,0:T(8,128)(2,1)} %refs_1_.12), channel_id=1, source_target_pairs={{0,12},{4,8},{8,4},{12,0},{1,13},{5,9},{9,5},{13,1},{2,14},{6,10},... | collective-permute-start | bytes 393224 | tf_op jit(solution)/shard_map/ppermute | solution.py:253
  5.1 0.6 collective-permute-start
  5.6 6.5 %fetch_kernel.2 = (bf16[2048,2304]{1,0:T(8,128)(2,1)S(1)}, bf16[2048,2304]{1,0:T(8,128)(2,1)S(1)}) custom-call(bf16[2048,6656]{1,0:T(8,128)(2,1)} %refs_7_.3, bf16[2048,6656]{1,0:T(8,128)(2,1)} %refs_8_.3), custom_call_target="tpu_custom_call" | custom-call | bytes 18874368 | tf_op jit(solution)/shard_map/fetch_kernel/pallas_call | solution.py:233
  12.1 4.7 %fetch_kernel.3 = (bf16[2048,1536]{1,0:T(8,128)(2,1)S(1)}, bf16[2048,1536]{1,0:T(8,128)(2,1)S(1)}) custom-call(bf16[2048,2304]{1,0:T(8,128)(2,1)S(1)} %get-tuple-element.31.refs_0_.refs_5_, bf16[2048,6656]{1,0:T(8,128)(2,1)} %refs_7_.3, bf16[2048,6656]{1,0:T(8,128)(2,1)} %refs_8_.3), custom_call_target="tpu_custom_call" | custom-call | bytes 12582912 | tf_op jit(solution)/shard_map/fetch_kernel/pallas_call | solution.py:233
  16.9 3.1 %held_gate_up_kernel.2 = (bf16[2,2,32,2304]{3,2,1,0:T(8,128)(2,1)S(1)}, f32[2,2,32,2304]{3,2,1,0:T(8,128)S(1)}, bf16[2048,512]{1,0:T(8,128)(2,1)S(1)}, bf16[2048,512]{1,0:T(8,128)(2,1)S(1)}) custom-call(bf16[2048,1536]{1,0:T(8,128)(2,1)S(1)} %get-tuple-element.32.refs_0_.refs_5_, bf16[32,2048]{1,0:T(8,128)(2,1)S(1)} %copy-done, ...), custom_call_target="tpu_custom_call" | custom-call | flops 2415919104 | bytes 262144 | tf_op jit(solution)/shard_map/held_gate_up_kernel/pallas_call | solution.py:233
  20.0 2.4 %held_gate_up_kernel.3 = (bf16[2,2,32,2048]{3,2,1,0:T(8,128)(2,1)S(1)}, f32[2,2,32,2048]{3,2,1,0:T(8,128)S(1)}, bf16[2048,512]{1,0:T(8,128)(2,1)S(1)}, bf16[2048,512]{1,0:T(8,128)(2,1)S(1)}) custom-call(bf16[2,2,32,2304]{3,2,1,0:T(8,128)(2,1)S(1)} %get-tuple-element.34.refs_0_, bf16[32,2048]{1,0:T(8,128)(2,1)S(1)} %copy-done, ...), custom_call_target="tpu_custom_call" | custom-call | flops 2147483648 | bytes 262144 | tf_op jit(solution)/shard_map/held_gate_up_kernel/pallas_call | solution.py:233
  22.4 0.5 collective-permute-start.4
  23.1 1.8 %collective-permute-start.5 = (bf16[2,2,16,2304]{3,2,1,0:T(8,128)(2,1)S(1)}, bf16[2,2,16,2304]{3,2,1,0:T(8,128)(2,1)S(1)}, u32[]{:S(2)}, u32[]{:S(2)}) collective-permute-start(bf16[2,2,16,2304]{3,2,1,0:T(8,128)(2,1)S(1)} %get-tuple-element.46), channel_id=1, source_target_pairs={{0,2},{1,3},{2,0},{3,1},{4,6},{5,7},{6,4},{7,5},{8,10},{9,11},{10,... | collective-permute-start | bytes 884744 | tf_op jit(solution)/shard_map/ppermute | solution.py:250
  24.9 6.4 %gate_up_kernel.1 = (bf16[1,2,32,2304]{3,2,1,0:T(8,128)(2,1)S(1)}, bf16[1,2,32,2304]{3,2,1,0:T(8,128)(2,1)S(1)}, f32[2,2,32,2304]{3,2,1,0:T(8,128)S(1)}) custom-call(f32[2,2,16,2304]{3,2,1,0:T(8,128)S(1)} %get-tuple-element.40.refs_0_.refs_1_, bf16[32,2048]{1,0:T(8,128)(2,1)S(1)} %copy-done, bf16[32,2048]{1,0:T(8,128)(2,1)S(1)} %collective-permute-done.refs_2_, ...), custom_call_target="tpu_custom_call" | custom-call | flops 2415919104 | bytes 18874368 | tf_op jit(solution)/shard_map/gate_up_kernel/pallas_call | solution.py:233
  31.4 0.5 collective-permute-start.6
  32.0 0.4 collective-permute-start.8
  32.5 1.8 %collective-permute-start.9 = (bf16[2,16,2304]{2,1,0:T(8,128)(2,1)S(1)}, bf16[2,16,2304]{2,1,0:T(8,128)(2,1)S(1)}, u32[]{:S(2)}, u32[]{:S(2)}) collective-permute-start(bf16[2,16,2304]{2,1,0:T(8,128)(2,1)S(1)} %hidden_kernel.3.refs_0_.refs_1_), channel_id=1, source_target_pairs={{0,2},{1,3},{2,0},{3,1},{4,6},{5,7},{6,4},{7,5},{8,10},{9,11},{10,... | collective-permute-start | bytes 442376 | tf_op jit(solution)/shard_map/ppermute | solution.py:250
  34.4 0.4 collective-permute-start.10
  34.8 3.7 %fetch_rows_kernel.3.refs_0_.refs_3_ = bf16[2304,2048]{1,0:T(8,128)(2,1)S(1)} custom-call(f32[2,2,16,2304]{3,2,1,0:T(8,128)S(1)} %get-tuple-element.49.refs_0_.refs_1_, bf16[6656,2048]{1,0:T(8,128)(2,1)} %refs_1_.15), custom_call_target="tpu_custom_call" | custom-call | bytes 9437184 | tf_op jit(solution)/shard_map/fetch_rows_kernel/pallas_call | solution.py:233
  38.5 2.7 %collective-permute-done.8.refs_2_ = bf16[2,2,16,2048]{3,2,1,0:T(8,128)(2,1)S(1)} collective-permute-done((bf16[2,2,16,2048]{3,2,1,0:T(8,128)(2,1)S(1)}, bf16[2,2,16,2048]{3,2,1,0:T(8,128)(2,1)S(1)}, u32[]{:S(2)}, u32[]{:S(2)}) %collective-permute-start.8) | collective-permute-done | bytes 262176 | tf_op jit(solution)/shard_map/ppermute | solution.py:250
  41.3 3.4 %fetch_rows_kernel.4.refs_0_.refs_4_ = bf16[2048,2048]{1,0:T(8,128)(2,1)S(1)} custom-call(bf16[2,16,2048]{2,1,0:T(8,128)(2,1)S(1)} %hidden_kernel.4.refs_0_.refs_1_, bf16[6656,2048]{1,0:T(8,128)(2,1)} %refs_1_.15), custom_call_target="tpu_custom_call" | custom-call | bytes 8388608 | tf_op jit(solution)/shard_map/fetch_rows_kernel/pallas_call | solution.py:233
  44.9 0.4 collective-permute-start.12
  45.2 3.7 %fetch_rows_kernel.5.refs_0_.refs_4_ = bf16[2304,2048]{1,0:T(8,128)(2,1)S(1)} custom-call(bf16[2,2,16,2304]{3,2,1,0:T(8,128)(2,1)S(1)} %pack_kernel.3.refs_0_.refs_1_, bf16[6656,2048]{1,0:T(8,128)(2,1)} %refs_1_.15), custom_call_target="tpu_custom_call" | custom-call | bytes 9437184 | tf_op jit(solution)/shard_map/fetch_rows_kernel/pallas_call | solution.py:233
  48.9 1.8 %collective-permute-done.10.refs_2_ = bf16[2,2,16,2304]{3,2,1,0:T(8,128)(2,1)S(1)} collective-permute-done((bf16[2,2,16,2304]{3,2,1,0:T(8,128)(2,1)S(1)}, bf16[2,2,16,2304]{3,2,1,0:T(8,128)(2,1)S(1)}, u32[]{:S(2)}, u32[]{:S(2)}) %collective-permute-start.10) | collective-permute-done | bytes 294944 | tf_op jit(solution)/shard_map/ppermute | solution.py:250
  50.8 0.4 collective-permute-start.13
  51.2 1.4 %down_kernel.3.refs_0_.refs_3_ = f32[128,2048]{1,0:T(8,128)S(1)} custom-call(bf16[2,16,2304]{2,1,0:T(8,128)(2,1)S(1)} %hidden_kernel.5.refs_0_.refs_1_, bf16[2,2,16,2304]{3,2,1,0:T(8,128)(2,1)S(1)} %pack_kernel.3.refs_0_.refs_1_, bf16[2,2,16,2304]{3,2,1,0:T(8,128)(2,1)S(1)} %collective-permute-done.11.refs_2_, ...), custom_call_target="tpu_custom_call" | custom-call | flops 1207959552 | bytes 294912 | tf_op jit(solution)/shard_map/down_kernel/pallas_call | solution.py:233
  52.6 0.7 collective-permute-done.12.refs_2_
  53.4 2.6 %collective-permute-done.13.refs_2_ = bf16[2,16,2304]{2,1,0:T(8,128)(2,1)S(1)} collective-permute-done((bf16[2,16,2304]{2,1,0:T(8,128)(2,1)S(1)}, bf16[2,16,2304]{2,1,0:T(8,128)(2,1)S(1)}, u32[]{:S(2)}, u32[]{:S(2)}) %collective-permute-start.13) | collective-permute-done | bytes 147488 | tf_op jit(solution)/shard_map/ppermute | solution.py:250
  56.2 1.3 %down_kernel.4.refs_0_.refs_3_ = f32[128,2048]{1,0:T(8,128)S(1)} custom-call(bf16[2,2,16,2304]{3,2,1,0:T(8,128)(2,1)S(1)} %pack_kernel.5.refs_0_.refs_1_, bf16[2,2,16,2048]{3,2,1,0:T(8,128)(2,1)S(1)} %pack_kernel.4.refs_0_.refs_1_, bf16[2,2,16,2048]{3,2,1,0:T(8,128)(2,1)S(1)} %collective-permute-done.14.refs_2_, f32[128,2048]{1,0:T(8,128)S(1)} %down_kernel.3.refs_0_.refs_3_, ...), custom_call_target="tpu_custom_call" | custom-call | flops 1073741824 | bytes 262144 | tf_op jit(solution)/shard_map/down_kernel/pallas_call | solution.py:233
  57.5 0.3 collective-permute-done.15.refs_2_
  57.7 1.4 %down_kernel.5 = (f32[32,2048]{1,0:T(8,128)S(1)}, bf16[32,2816]{1,0:T(8,128)(2,1)S(1)}, bf16[32,1280]{1,0:T(8,128)(2,1)S(1)}, bf16[32,1280]{1,0:T(8,128)(2,1)S(1)}, f32[32,768]{1,0:T(8,128)S(1)}) custom-call(f32[128,2048]{1,0:T(8,128)S(1)} %down_kernel.4.refs_0_.refs_3_, bf16[2,2,16,2304]{3,2,1,0:T(8,128)(2,1)S(1)} %pack_kernel.5.refs_0_.refs_1_, ...), custom_call_target="tpu_custom_call" | custom-call | flops 1207959552 | bytes 294912 | tf_op jit(solution)/shard_map/down_kernel/pallas_call | solution.py:233
  59.1 1.3 %collective-permute-start.16 = (bf16[32,2816]{1,0:T(8,128)(2,1)S(1)}, bf16[32,2816]{1,0:T(8,128)(2,1)S(1)}, u32[]{:S(2)}, u32[]{:S(2)}) collective-permute-start(bf16[32,2816]{1,0:T(8,128)(2,1)S(1)} %get-tuple-element.53), channel_id=1, source_target_pairs={{0,4},{4,0},{8,12},{12,8},{1,5},{5,1},{9,13},{13,9},{2,6},{6,2},{1... | collective-permute-start | bytes 540680 | tf_op jit(solution)/shard_map/ppermute | solution.py:253
  60.4 2.9 %collective-permute-start.17 = (bf16[32,1280]{1,0:T(8,128)(2,1)S(1)}, bf16[32,1280]{1,0:T(8,128)(2,1)S(1)}, u32[]{:S(2)}, u32[]{:S(2)}) collective-permute-start(bf16[32,1280]{1,0:T(8,128)(2,1)S(1)} %get-tuple-element.55), channel_id=1, source_target_pairs={{0,8},{4,12},{8,0},{12,4},{1,9},{5,13},{9,1},{13,5},{2,10},{6,14},... | collective-permute-start | bytes 245768 | tf_op jit(solution)/shard_map/ppermute | solution.py:253
  63.6 4.1 %collective-permute-done.16.refs_1_.refs_2_ = bf16[32,2816]{1,0:T(8,128)(2,1)S(1)} collective-permute-done((bf16[32,2816]{1,0:T(8,128)(2,1)S(1)}, bf16[32,2816]{1,0:T(8,128)(2,1)S(1)}, u32[]{:S(2)}, u32[]{:S(2)}) %collective-permute-start.16) | collective-permute-done | bytes 180256 | tf_op jit(solution)/shard_map/ppermute | solution.py:253
  67.6 3.5 %collective-permute-start.19 = (bf16[32,768]{1,0:T(8,128)(2,1)S(1)}, bf16[32,768]{1,0:T(8,128)(2,1)S(1)}, u32[]{:S(2)}, u32[]{:S(2)}) collective-permute-start(bf16[32,768]{1,0:T(8,128)(2,1)S(1)} %pair_sum_kernel.1.refs_0_), channel_id=1, source_target_pairs={{0,8},{4,12},{8,0},{12,4},{1,9},{5,13},{9,1},{13,5},{2,10},{6,14},... | collective-permute-start | bytes 147464 | tf_op jit(solution)/shard_map/ppermute | solution.py:253
  71.3 1.9 %collective-permute-done.19.refs_5_ = bf16[32,768]{1,0:T(8,128)(2,1)S(1)} collective-permute-done((bf16[32,768]{1,0:T(8,128)(2,1)S(1)}, bf16[32,768]{1,0:T(8,128)(2,1)S(1)}, u32[]{:S(2)}, u32[]{:S(2)}) %collective-permute-start.19) | collective-permute-done | bytes 49184 | tf_op jit(solution)/shard_map/ppermute | solution.py:253
  73.2 0.7 final_kernel.1
  (32 shorter events, 1.5 us)
Async XLA Ops:
  0.0 16.8 %collective-permute-start.2 = (bf16[32,2048]{1,0:T(8,128)(2,1)}, bf16[32,2048]{1,0:T(8,128)(2,1)S(1)}, u32[]{:S(2)}, u32[]{:S(2)}) collective-permute-start(bf16[32,2048]{1,0:T(8,128)(2,1)} %refs_1_.12), channel_id=1, source_target_pairs={{0,12},{4,8},{8,4},{12,0},{1,13},{5,9},{9,5},{13,1},{2,14},{6,10},... | collective-permute-start | bytes 393224 | tf_op jit(solution)/shard_map/ppermute | solution.py:253
  5.0 11.8 %collective-permute-start.1 = (bf16[32,2048]{1,0:T(8,128)(2,1)}, bf16[32,2048]{1,0:T(8,128)(2,1)S(1)}, u32[]{:S(2)}, u32[]{:S(2)}) collective-permute-start(bf16[32,2048]{1,0:T(8,128)(2,1)} %refs_1_.12), channel_id=1, source_target_pairs={{0,8},{4,12},{8,0},{12,4},{1,9},{5,13},{9,1},{13,5},{2,10},{6,14},... | collective-permute-start | bytes 393224 | tf_op jit(solution)/shard_map/ppermute | solution.py:253
  5.1 11.8 %collective-permute-start = (bf16[32,2048]{1,0:T(8,128)(2,1)}, bf16[32,2048]{1,0:T(8,128)(2,1)S(1)}, u32[]{:S(2)}, u32[]{:S(2)}) collective-permute-start(bf16[32,2048]{1,0:T(8,128)(2,1)} %refs_1_.12), channel_id=1, source_target_pairs={{0,4},{4,0},{8,12},{12,8},{1,5},{5,1},{9,13},{13,9},{2,6},{6,2},{1... | collective-permute-start | bytes 393224 | tf_op jit(solution)/shard_map/ppermute | solution.py:253
  12.1 4.7 %copy-start = (bf16[32,2048]{1,0:T(8,128)(2,1)S(1)}, bf16[32,2048]{1,0:T(8,128)(2,1)}, u32[]{:S(2)}) copy-start(bf16[32,2048]{1,0:T(8,128)(2,1)} %refs_1_.12) | copy-start | bytes 393220
  19.9 3.0 %collective-permute-start.3 = (bf16[2,2,32,2304]{3,2,1,0:T(8,128)(2,1)S(1)}, bf16[2,2,32,2304]{3,2,1,0:T(8,128)(2,1)S(1)}, u32[]{:S(2)}, u32[]{:S(2)}) collective-permute-start(bf16[2,2,32,2304]{3,2,1,0:T(8,128)(2,1)S(1)} %get-tuple-element.34.refs_0_), channel_id=1, source_target_pairs={{0,1},{1,0},{2,3},{3,2},{4,5},{5,4},{6,7},{7,6},{8,9},{9,8},{10,11... | collective-permute-start | bytes 1769480 | tf_op jit(solution)/shard_map/ppermute | solution.py:247
  22.4 9.5 %collective-permute-start.4 = (bf16[2,2,32,2048]{3,2,1,0:T(8,128)(2,1)S(1)}, bf16[2,2,32,2048]{3,2,1,0:T(8,128)(2,1)S(1)}, u32[]{:S(2)}, u32[]{:S(2)}) collective-permute-start(bf16[2,2,32,2048]{3,2,1,0:T(8,128)(2,1)S(1)} %get-tuple-element.38.refs_0_), channel_id=1, source_target_pairs={{0,1},{1,0},{2,3},{3,2},{4,5},{5,4},{6,7},{7,6},{8,9},{9,8},{10,11... | collective-permute-start | bytes 1572872 | tf_op jit(solution)/shard_map/ppermute | solution.py:247
  23.1 9.3 %collective-permute-start.5 = (bf16[2,2,16,2304]{3,2,1,0:T(8,128)(2,1)S(1)}, bf16[2,2,16,2304]{3,2,1,0:T(8,128)(2,1)S(1)}, u32[]{:S(2)}, u32[]{:S(2)}) collective-permute-start(bf16[2,2,16,2304]{3,2,1,0:T(8,128)(2,1)S(1)} %get-tuple-element.46), channel_id=1, source_target_pairs={{0,2},{1,3},{2,0},{3,1},{4,6},{5,7},{6,4},{7,5},{8,10},{9,11},{10,... | collective-permute-start | bytes 884744 | tf_op jit(solution)/shard_map/ppermute | solution.py:250
  31.3 3.0 %collective-permute-start.7 = (bf16[1,2,32,2304]{3,2,1,0:T(8,128)(2,1)S(1)}, bf16[1,2,32,2304]{3,2,1,0:T(8,128)(2,1)S(1)}, u32[]{:S(2)}, u32[]{:S(2)}) collective-permute-start(bf16[1,2,32,2304]{3,2,1,0:T(8,128)(2,1)S(1)} %get-tuple-element.48), channel_id=1, source_target_pairs={{0,1},{1,0},{2,3},{3,2},{4,5},{5,4},{6,7},{7,6},{8,9},{9,8},{10,11... | collective-permute-start | bytes 884744 | tf_op jit(solution)/shard_map/ppermute | solution.py:247
  31.4 2.9 %collective-permute-start.6 = (bf16[1,2,32,2304]{3,2,1,0:T(8,128)(2,1)S(1)}, bf16[1,2,32,2304]{3,2,1,0:T(8,128)(2,1)S(1)}, u32[]{:S(2)}, u32[]{:S(2)}) collective-permute-start(bf16[1,2,32,2304]{3,2,1,0:T(8,128)(2,1)S(1)} %get-tuple-element.43.refs_0_), channel_id=1, source_target_pairs={{0,1},{1,0},{2,3},{3,2},{4,5},{5,4},{6,7},{7,6},{8,9},{9,8},{10,11... | collective-permute-start | bytes 884744 | tf_op jit(solution)/shard_map/ppermute | solution.py:247
  32.0 9.2 %collective-permute-start.8 = (bf16[2,2,16,2048]{3,2,1,0:T(8,128)(2,1)S(1)}, bf16[2,2,16,2048]{3,2,1,0:T(8,128)(2,1)S(1)}, u32[]{:S(2)}, u32[]{:S(2)}) collective-permute-start(bf16[2,2,16,2048]{3,2,1,0:T(8,128)(2,1)S(1)} %get-tuple-element.50), channel_id=1, source_target_pairs={{0,2},{1,3},{2,0},{3,1},{4,6},{5,7},{6,4},{7,5},{8,10},{9,11},{10,... | collective-permute-start | bytes 786440 | tf_op jit(solution)/shard_map/ppermute | solution.py:250
  32.5 12.2 %collective-permute-start.9 = (bf16[2,16,2304]{2,1,0:T(8,128)(2,1)S(1)}, bf16[2,16,2304]{2,1,0:T(8,128)(2,1)S(1)}, u32[]{:S(2)}, u32[]{:S(2)}) collective-permute-start(bf16[2,16,2304]{2,1,0:T(8,128)(2,1)S(1)} %hidden_kernel.3.refs_0_.refs_1_), channel_id=1, source_target_pairs={{0,2},{1,3},{2,0},{3,1},{4,6},{5,7},{6,4},{7,5},{8,10},{9,11},{10,... | collective-permute-start | bytes 442376 | tf_op jit(solution)/shard_map/ppermute | solution.py:250
  34.4 16.3 %collective-permute-start.10 = (bf16[2,2,16,2304]{3,2,1,0:T(8,128)(2,1)S(1)}, bf16[2,2,16,2304]{3,2,1,0:T(8,128)(2,1)S(1)}, u32[]{:S(2)}, u32[]{:S(2)}) collective-permute-start(bf16[2,2,16,2304]{3,2,1,0:T(8,128)(2,1)S(1)} %get-tuple-element.51), channel_id=1, source_target_pairs={{0,2},{1,3},{2,0},{3,1},{4,6},{5,7},{6,4},{7,5},{8,10},{9,11},{10,... | collective-permute-start | bytes 884744 | tf_op jit(solution)/shard_map/ppermute | solution.py:250
  44.8 6.4 %collective-permute-start.11 = (bf16[2,2,16,2304]{3,2,1,0:T(8,128)(2,1)S(1)}, bf16[2,2,16,2304]{3,2,1,0:T(8,128)(2,1)S(1)}, u32[]{:S(2)}, u32[]{:S(2)}) collective-permute-start(bf16[2,2,16,2304]{3,2,1,0:T(8,128)(2,1)S(1)} %pack_kernel.3.refs_0_.refs_1_), channel_id=1, source_target_pairs={{0,1},{1,0},{2,3},{3,2},{4,5},{5,4},{6,7},{7,6},{8,9},{9,8},{10,11... | collective-permute-start | bytes 884744 | tf_op jit(solution)/shard_map/ppermute | solution.py:247
  44.9 8.5 %collective-permute-start.12 = (bf16[2,16,2048]{2,1,0:T(8,128)(2,1)S(1)}, bf16[2,16,2048]{2,1,0:T(8,128)(2,1)S(1)}, u32[]{:S(2)}, u32[]{:S(2)}) collective-permute-start(bf16[2,16,2048]{2,1,0:T(8,128)(2,1)S(1)} %hidden_kernel.4.refs_0_.refs_1_), channel_id=1, source_target_pairs={{0,2},{1,3},{2,0},{3,1},{4,6},{5,7},{6,4},{7,5},{8,10},{9,11},{10,... | collective-permute-start | bytes 393224 | tf_op jit(solution)/shard_map/ppermute | solution.py:250
  50.8 5.2 %collective-permute-start.13 = (bf16[2,16,2304]{2,1,0:T(8,128)(2,1)S(1)}, bf16[2,16,2304]{2,1,0:T(8,128)(2,1)S(1)}, u32[]{:S(2)}, u32[]{:S(2)}) collective-permute-start(bf16[2,16,2304]{2,1,0:T(8,128)(2,1)S(1)} %hidden_kernel.5.refs_0_.refs_1_), channel_id=1, source_target_pairs={{0,2},{1,3},{2,0},{3,1},{4,6},{5,7},{6,4},{7,5},{8,10},{9,11},{10,... | collective-permute-start | bytes 442376 | tf_op jit(solution)/shard_map/ppermute | solution.py:250
  53.3 2.8 %collective-permute-start.14 = (bf16[2,2,16,2048]{3,2,1,0:T(8,128)(2,1)S(1)}, bf16[2,2,16,2048]{3,2,1,0:T(8,128)(2,1)S(1)}, u32[]{:S(2)}, u32[]{:S(2)}) collective-permute-start(bf16[2,2,16,2048]{3,2,1,0:T(8,128)(2,1)S(1)} %pack_kernel.4.refs_0_.refs_1_), channel_id=1, source_target_pairs={{0,1},{1,0},{2,3},{3,2},{4,5},{5,4},{6,7},{7,6},{8,9},{9,8},{10,11... | collective-permute-start | bytes 786440 | tf_op jit(solution)/shard_map/ppermute | solution.py:247
  56.1 1.6 %collective-permute-start.15 = (bf16[2,2,16,2304]{3,2,1,0:T(8,128)(2,1)S(1)}, bf16[2,2,16,2304]{3,2,1,0:T(8,128)(2,1)S(1)}, u32[]{:S(2)}, u32[]{:S(2)}) collective-permute-start(bf16[2,2,16,2304]{3,2,1,0:T(8,128)(2,1)S(1)} %pack_kernel.5.refs_0_.refs_1_), channel_id=1, source_target_pairs={{0,1},{1,0},{2,3},{3,2},{4,5},{5,4},{6,7},{7,6},{8,9},{9,8},{10,11... | collective-permute-start | bytes 884744 | tf_op jit(solution)/shard_map/ppermute | solution.py:247
  59.1 8.5 %collective-permute-start.16 = (bf16[32,2816]{1,0:T(8,128)(2,1)S(1)}, bf16[32,2816]{1,0:T(8,128)(2,1)S(1)}, u32[]{:S(2)}, u32[]{:S(2)}) collective-permute-start(bf16[32,2816]{1,0:T(8,128)(2,1)S(1)} %get-tuple-element.53), channel_id=1, source_target_pairs={{0,4},{4,0},{8,12},{12,8},{1,5},{5,1},{9,13},{13,9},{2,6},{6,2},{1... | collective-permute-start | bytes 540680 | tf_op jit(solution)/shard_map/ppermute | solution.py:253
  60.4 10.8 %collective-permute-start.17 = (bf16[32,1280]{1,0:T(8,128)(2,1)S(1)}, bf16[32,1280]{1,0:T(8,128)(2,1)S(1)}, u32[]{:S(2)}, u32[]{:S(2)}) collective-permute-start(bf16[32,1280]{1,0:T(8,128)(2,1)S(1)} %get-tuple-element.55), channel_id=1, source_target_pairs={{0,8},{4,12},{8,0},{12,4},{1,9},{5,13},{9,1},{13,5},{2,10},{6,14},... | collective-permute-start | bytes 245768 | tf_op jit(solution)/shard_map/ppermute | solution.py:253
  63.3 8.0 %collective-permute-start.18 = (bf16[32,1280]{1,0:T(8,128)(2,1)S(1)}, bf16[32,1280]{1,0:T(8,128)(2,1)S(1)}, u32[]{:S(2)}, u32[]{:S(2)}) collective-permute-start(bf16[32,1280]{1,0:T(8,128)(2,1)S(1)} %get-tuple-element.56), channel_id=1, source_target_pairs={{0,12},{4,8},{8,4},{12,0},{1,13},{5,9},{9,5},{13,1},{2,14},{6,10},... | collective-permute-start | bytes 245768 | tf_op jit(solution)/shard_map/ppermute | solution.py:253
  67.6 5.6 %collective-permute-start.19 = (bf16[32,768]{1,0:T(8,128)(2,1)S(1)}, bf16[32,768]{1,0:T(8,128)(2,1)S(1)}, u32[]{:S(2)}, u32[]{:S(2)}) collective-permute-start(bf16[32,768]{1,0:T(8,128)(2,1)S(1)} %pair_sum_kernel.1.refs_0_), channel_id=1, source_target_pairs={{0,8},{4,12},{8,0},{12,4},{1,9},{5,13},{9,1},{13,5},{2,10},{6,14},... | collective-permute-start | bytes 147464 | tf_op jit(solution)/shard_map/ppermute | solution.py:253

commit v5 on v4

--- a/solution.py
+++ b/solution.py
@@ -284,7 +284,7 @@
         width = self.width
         outs = [jax.ShapeDtypeStruct((2 // sends, 2, rows // 4, size), BF16)] * sends
         outs.append(jax.ShapeDtypeStruct((2, 2, rows // 4, size), F32))
-        depth, slots = largest(width, (512, 256)), 8
+        depth, slots = largest(width, (256, 128)), 16
         streamed = size - weights[0].shape[1]
         got = self.call(
             functools.partial(gate_up_kernel, start, size, depth, slots, 2, self.groups // 2, sends),

time: 74.2 us -> 74.1 us (level)
  no operation moved by 1% of the time
where the time goes in v5:
time: 74.1 us; the launch traced here: 73.9 us
  Pallas kernels  39.3 us (53%)
  starting transfers between devices  20.1 us (27%)
  waiting for transfers between devices  14.3 us (19%)
    pallas_call x22, Pallas kernels, call(): pl.pallas_call(run, name=kernel.func.__name__ if isinstance(kernel, funct...  39.3 us
    ppermute x7, starting transfers between devices, along_z(): return lax.ppermute(value, 'hid', [(z, z ^ j) for z in range(self.groups)])  13.6 us
    ppermute x6, waiting for transfers between devices, along_x(): lax.ppermute(value, 'wid', [(w, (w // 2 + j) % self.chips * 2 + w % 2) fo...  7.85 us
    ppermute x7, waiting for transfers between devices, along_z(): return lax.ppermute(value, 'hid', [(z, z ^ j) for z in range(self.groups)])  6.13 us
    ppermute x6, starting transfers between devices, along_x(): lax.ppermute(value, 'wid', [(w, (w // 2 + j) % self.chips * 2 + w % 2) fo...  5.06 us
  transfers between devices with their start and end apart: 20, of which 8 were waited for; matrix products, arithmetic and copies ran while one was open for 0% of the time, Pallas kernels for 46%

profile of v5, /device:TPU:0, one launch (start us, length us, event | category | flops | bytes accessed | tf_op | source)
XLA Modules:
  0.0 73.9 jit_solution(12669493263206484973)
XLA Ops:
  0.0 5.0 %collective-permute-start.2 = (bf16[32,2048]{1,0:T(8,128)(2,1)}, bf16[32,2048]{1,0:T(8,128)(2,1)S(1)}, u32[]{:S(2)}, u32[]{:S(2)}) collective-permute-start(bf16[32,2048]{1,0:T(8,128)(2,1)} %refs_1_.12), channel_id=1, source_target_pairs={{0,12},{4,8},{8,4},{12,0},{1,13},{5,9},{9,5},{13,1},{2,14},{6,10},... | collective-permute-start | bytes 393224 | tf_op jit(solution)/shard_map/ppermute | solution.py:253
  5.1 0.6 collective-permute-start
  5.6 6.5 %fetch_kernel.2 = (bf16[2048,2304]{1,0:T(8,128)(2,1)S(1)}, bf16[2048,2304]{1,0:T(8,128)(2,1)S(1)}) custom-call(bf16[2048,6656]{1,0:T(8,128)(2,1)} %refs_7_.3, bf16[2048,6656]{1,0:T(8,128)(2,1)} %refs_8_.3), custom_call_target="tpu_custom_call" | custom-call | bytes 18874368 | tf_op jit(solution)/shard_map/fetch_kernel/pallas_call | solution.py:233
  12.1 4.7 %fetch_kernel.3 = (bf16[2048,1536]{1,0:T(8,128)(2,1)S(1)}, bf16[2048,1536]{1,0:T(8,128)(2,1)S(1)}) custom-call(bf16[2048,2304]{1,0:T(8,128)(2,1)S(1)} %get-tuple-element.31.refs_0_.refs_5_, bf16[2048,6656]{1,0:T(8,128)(2,1)} %refs_7_.3, bf16[2048,6656]{1,0:T(8,128)(2,1)} %refs_8_.3), custom_call_target="tpu_custom_call" | custom-call | bytes 12582912 | tf_op jit(solution)/shard_map/fetch_kernel/pallas_call | solution.py:233
  16.9 3.1 %held_gate_up_kernel.2 = (bf16[2,2,32,2304]{3,2,1,0:T(8,128)(2,1)S(1)}, f32[2,2,32,2304]{3,2,1,0:T(8,128)S(1)}, bf16[2048,512]{1,0:T(8,128)(2,1)S(1)}, bf16[2048,512]{1,0:T(8,128)(2,1)S(1)}) custom-call(bf16[2048,1536]{1,0:T(8,128)(2,1)S(1)} %get-tuple-element.32.refs_0_.refs_5_, bf16[32,2048]{1,0:T(8,128)(2,1)S(1)} %copy-done, ...), custom_call_target="tpu_custom_call" | custom-call | flops 2415919104 | bytes 262144 | tf_op jit(solution)/shard_map/held_gate_up_kernel/pallas_call | solution.py:233
  20.0 2.4 %held_gate_up_kernel.3 = (bf16[2,2,32,2048]{3,2,1,0:T(8,128)(2,1)S(1)}, f32[2,2,32,2048]{3,2,1,0:T(8,128)S(1)}, bf16[2048,512]{1,0:T(8,128)(2,1)S(1)}, bf16[2048,512]{1,0:T(8,128)(2,1)S(1)}) custom-call(bf16[2,2,32,2304]{3,2,1,0:T(8,128)(2,1)S(1)} %get-tuple-element.34.refs_0_, bf16[32,2048]{1,0:T(8,128)(2,1)S(1)} %copy-done, ...), custom_call_target="tpu_custom_call" | custom-call | flops 2147483648 | bytes 262144 | tf_op jit(solution)/shard_map/held_gate_up_kernel/pallas_call | solution.py:233
  22.4 0.5 collective-permute-start.4
  23.1 1.8 %collective-permute-start.5 = (bf16[2,2,16,2304]{3,2,1,0:T(8,128)(2,1)S(1)}, bf16[2,2,16,2304]{3,2,1,0:T(8,128)(2,1)S(1)}, u32[]{:S(2)}, u32[]{:S(2)}) collective-permute-start(bf16[2,2,16,2304]{3,2,1,0:T(8,128)(2,1)S(1)} %get-tuple-element.46), channel_id=1, source_target_pairs={{0,2},{1,3},{2,0},{3,1},{4,6},{5,7},{6,4},{7,5},{8,10},{9,11},{10,... | collective-permute-start | bytes 884744 | tf_op jit(solution)/shard_map/ppermute | solution.py:250
  24.9 6.4 %gate_up_kernel.1 = (bf16[1,2,32,2304]{3,2,1,0:T(8,128)(2,1)S(1)}, bf16[1,2,32,2304]{3,2,1,0:T(8,128)(2,1)S(1)}, f32[2,2,32,2304]{3,2,1,0:T(8,128)S(1)}) custom-call(f32[2,2,16,2304]{3,2,1,0:T(8,128)S(1)} %get-tuple-element.40.refs_0_.refs_1_, bf16[32,2048]{1,0:T(8,128)(2,1)S(1)} %copy-done, bf16[32,2048]{1,0:T(8,128)(2,1)S(1)} %collective-permute-done.refs_2_, ...), custom_call_target="tpu_custom_call" | custom-call | flops 2415919104 | bytes 18874368 | tf_op jit(solution)/shard_map/gate_up_kernel/pallas_call | solution.py:233
  31.4 0.5 collective-permute-start.6
  31.9 0.4 collective-permute-start.8
  32.5 1.8 %collective-permute-start.9 = (bf16[2,16,2304]{2,1,0:T(8,128)(2,1)S(1)}, bf16[2,16,2304]{2,1,0:T(8,128)(2,1)S(1)}, u32[]{:S(2)}, u32[]{:S(2)}) collective-permute-start(bf16[2,16,2304]{2,1,0:T(8,128)(2,1)S(1)} %hidden_kernel.3.refs_0_.refs_1_), channel_id=1, source_target_pairs={{0,2},{1,3},{2,0},{3,1},{4,6},{5,7},{6,4},{7,5},{8,10},{9,11},{10,... | collective-permute-start | bytes 442376 | tf_op jit(solution)/shard_map/ppermute | solution.py:250
  34.4 0.4 collective-permute-start.10
  34.7 3.7 %fetch_rows_kernel.3.refs_0_.refs_3_ = bf16[2304,2048]{1,0:T(8,128)(2,1)S(1)} custom-call(f32[2,2,16,2304]{3,2,1,0:T(8,128)S(1)} %get-tuple-element.49.refs_0_.refs_1_, bf16[6656,2048]{1,0:T(8,128)(2,1)} %refs_1_.15), custom_call_target="tpu_custom_call" | custom-call | bytes 9437184 | tf_op jit(solution)/shard_map/fetch_rows_kernel/pallas_call | solution.py:233
  38.4 2.7 %collective-permute-done.8.refs_2_ = bf16[2,2,16,2048]{3,2,1,0:T(8,128)(2,1)S(1)} collective-permute-done((bf16[2,2,16,2048]{3,2,1,0:T(8,128)(2,1)S(1)}, bf16[2,2,16,2048]{3,2,1,0:T(8,128)(2,1)S(1)}, u32[]{:S(2)}, u32[]{:S(2)}) %collective-permute-start.8) | collective-permute-done | bytes 262176 | tf_op jit(solution)/shard_map/ppermute | solution.py:250
  41.3 3.4 %fetch_rows_kernel.4.refs_0_.refs_4_ = bf16[2048,2048]{1,0:T(8,128)(2,1)S(1)} custom-call(bf16[2,16,2048]{2,1,0:T(8,128)(2,1)S(1)} %hidden_kernel.4.refs_0_.refs_1_, bf16[6656,2048]{1,0:T(8,128)(2,1)} %refs_1_.15), custom_call_target="tpu_custom_call" | custom-call | bytes 8388608 | tf_op jit(solution)/shard_map/fetch_rows_kernel/pallas_call | solution.py:233
  44.8 0.4 collective-permute-start.12
  45.2 3.7 %fetch_rows_kernel.5.refs_0_.refs_4_ = bf16[2304,2048]{1,0:T(8,128)(2,1)S(1)} custom-call(bf16[2,2,16,2304]{3,2,1,0:T(8,128)(2,1)S(1)} %pack_kernel.3.refs_0_.refs_1_, bf16[6656,2048]{1,0:T(8,128)(2,1)} %refs_1_.15), custom_call_target="tpu_custom_call" | custom-call | bytes 9437184 | tf_op jit(solution)/shard_map/fetch_rows_kernel/pallas_call | solution.py:233
  48.9 1.8 %collective-permute-done.10.refs_2_ = bf16[2,2,16,2304]{3,2,1,0:T(8,128)(2,1)S(1)} collective-permute-done((bf16[2,2,16,2304]{3,2,1,0:T(8,128)(2,1)S(1)}, bf16[2,2,16,2304]{3,2,1,0:T(8,128)(2,1)S(1)}, u32[]{:S(2)}, u32[]{:S(2)}) %collective-permute-start.10) | collective-permute-done | bytes 294944 | tf_op jit(solution)/shard_map/ppermute | solution.py:250
  50.8 0.4 collective-permute-start.13
  51.2 1.4 %down_kernel.3.refs_0_.refs_3_ = f32[128,2048]{1,0:T(8,128)S(1)} custom-call(bf16[2,16,2304]{2,1,0:T(8,128)(2,1)S(1)} %hidden_kernel.5.refs_0_.refs_1_, bf16[2,2,16,2304]{3,2,1,0:T(8,128)(2,1)S(1)} %pack_kernel.3.refs_0_.refs_1_, bf16[2,2,16,2304]{3,2,1,0:T(8,128)(2,1)S(1)} %collective-permute-done.11.refs_2_, ...), custom_call_target="tpu_custom_call" | custom-call | flops 1207959552 | bytes 294912 | tf_op jit(solution)/shard_map/down_kernel/pallas_call | solution.py:233
  52.6 0.7 collective-permute-done.12.refs_2_
  53.4 2.6 %collective-permute-done.13.refs_2_ = bf16[2,16,2304]{2,1,0:T(8,128)(2,1)S(1)} collective-permute-done((bf16[2,16,2304]{2,1,0:T(8,128)(2,1)S(1)}, bf16[2,16,2304]{2,1,0:T(8,128)(2,1)S(1)}, u32[]{:S(2)}, u32[]{:S(2)}) %collective-permute-start.13) | collective-permute-done | bytes 147488 | tf_op jit(solution)/shard_map/ppermute | solution.py:250
  56.1 1.3 %down_kernel.4.refs_0_.refs_3_ = f32[128,2048]{1,0:T(8,128)S(1)} custom-call(bf16[2,2,16,2304]{3,2,1,0:T(8,128)(2,1)S(1)} %pack_kernel.5.refs_0_.refs_1_, bf16[2,2,16,2048]{3,2,1,0:T(8,128)(2,1)S(1)} %pack_kernel.4.refs_0_.refs_1_, bf16[2,2,16,2048]{3,2,1,0:T(8,128)(2,1)S(1)} %collective-permute-done.14.refs_2_, f32[128,2048]{1,0:T(8,128)S(1)} %down_kernel.3.refs_0_.refs_3_, ...), custom_call_target="tpu_custom_call" | custom-call | flops 1073741824 | bytes 262144 | tf_op jit(solution)/shard_map/down_kernel/pallas_call | solution.py:233
  57.4 0.3 collective-permute-done.15.refs_2_
  57.7 1.4 %down_kernel.5 = (f32[32,2048]{1,0:T(8,128)S(1)}, bf16[32,2816]{1,0:T(8,128)(2,1)S(1)}, bf16[32,1280]{1,0:T(8,128)(2,1)S(1)}, bf16[32,1280]{1,0:T(8,128)(2,1)S(1)}, f32[32,768]{1,0:T(8,128)S(1)}) custom-call(f32[128,2048]{1,0:T(8,128)S(1)} %down_kernel.4.refs_0_.refs_3_, bf16[2,2,16,2304]{3,2,1,0:T(8,128)(2,1)S(1)} %pack_kernel.5.refs_0_.refs_1_, ...), custom_call_target="tpu_custom_call" | custom-call | flops 1207959552 | bytes 294912 | tf_op jit(solution)/shard_map/down_kernel/pallas_call | solution.py:233
  59.1 1.3 %collective-permute-start.16 = (bf16[32,2816]{1,0:T(8,128)(2,1)S(1)}, bf16[32,2816]{1,0:T(8,128)(2,1)S(1)}, u32[]{:S(2)}, u32[]{:S(2)}) collective-permute-start(bf16[32,2816]{1,0:T(8,128)(2,1)S(1)} %get-tuple-element.53), channel_id=1, source_target_pairs={{0,4},{4,0},{8,12},{12,8},{1,5},{5,1},{9,13},{13,9},{2,6},{6,2},{1... | collective-permute-start | bytes 540680 | tf_op jit(solution)/shard_map/ppermute | solution.py:253
  60.4 2.9 %collective-permute-start.17 = (bf16[32,1280]{1,0:T(8,128)(2,1)S(1)}, bf16[32,1280]{1,0:T(8,128)(2,1)S(1)}, u32[]{:S(2)}, u32[]{:S(2)}) collective-permute-start(bf16[32,1280]{1,0:T(8,128)(2,1)S(1)} %get-tuple-element.55), channel_id=1, source_target_pairs={{0,8},{4,12},{8,0},{12,4},{1,9},{5,13},{9,1},{13,5},{2,10},{6,14},... | collective-permute-start | bytes 245768 | tf_op jit(solution)/shard_map/ppermute | solution.py:253
  63.5 4.1 %collective-permute-done.16.refs_1_.refs_2_ = bf16[32,2816]{1,0:T(8,128)(2,1)S(1)} collective-permute-done((bf16[32,2816]{1,0:T(8,128)(2,1)S(1)}, bf16[32,2816]{1,0:T(8,128)(2,1)S(1)}, u32[]{:S(2)}, u32[]{:S(2)}) %collective-permute-start.16) | collective-permute-done | bytes 180256 | tf_op jit(solution)/shard_map/ppermute | solution.py:253
  67.6 3.5 %collective-permute-start.19 = (bf16[32,768]{1,0:T(8,128)(2,1)S(1)}, bf16[32,768]{1,0:T(8,128)(2,1)S(1)}, u32[]{:S(2)}, u32[]{:S(2)}) collective-permute-start(bf16[32,768]{1,0:T(8,128)(2,1)S(1)} %pair_sum_kernel.1.refs_0_), channel_id=1, source_target_pairs={{0,8},{4,12},{8,0},{12,4},{1,9},{5,13},{9,1},{13,5},{2,10},{6,14},... | collective-permute-start | bytes 147464 | tf_op jit(solution)/shard_map/ppermute | solution.py:253
  71.2 1.9 %collective-permute-done.19.refs_5_ = bf16[32,768]{1,0:T(8,128)(2,1)S(1)} collective-permute-done((bf16[32,768]{1,0:T(8,128)(2,1)S(1)}, bf16[32,768]{1,0:T(8,128)(2,1)S(1)}, u32[]{:S(2)}, u32[]{:S(2)}) %collective-permute-start.19) | collective-permute-done | bytes 49184 | tf_op jit(solution)/shard_map/ppermute | solution.py:253
  73.2 0.7 final_kernel.1
  (32 shorter events, 1.5 us)
Async XLA Ops:
  0.0 16.8 %collective-permute-start.2 = (bf16[32,2048]{1,0:T(8,128)(2,1)}, bf16[32,2048]{1,0:T(8,128)(2,1)S(1)}, u32[]{:S(2)}, u32[]{:S(2)}) collective-permute-start(bf16[32,2048]{1,0:T(8,128)(2,1)} %refs_1_.12), channel_id=1, source_target_pairs={{0,12},{4,8},{8,4},{12,0},{1,13},{5,9},{9,5},{13,1},{2,14},{6,10},... | collective-permute-start | bytes 393224 | tf_op jit(solution)/shard_map/ppermute | solution.py:253
  5.0 11.8 %collective-permute-start.1 = (bf16[32,2048]{1,0:T(8,128)(2,1)}, bf16[32,2048]{1,0:T(8,128)(2,1)S(1)}, u32[]{:S(2)}, u32[]{:S(2)}) collective-permute-start(bf16[32,2048]{1,0:T(8,128)(2,1)} %refs_1_.12), channel_id=1, source_target_pairs={{0,8},{4,12},{8,0},{12,4},{1,9},{5,13},{9,1},{13,5},{2,10},{6,14},... | collective-permute-start | bytes 393224 | tf_op jit(solution)/shard_map/ppermute | solution.py:253
  5.1 11.8 %collective-permute-start = (bf16[32,2048]{1,0:T(8,128)(2,1)}, bf16[32,2048]{1,0:T(8,128)(2,1)S(1)}, u32[]{:S(2)}, u32[]{:S(2)}) collective-permute-start(bf16[32,2048]{1,0:T(8,128)(2,1)} %refs_1_.12), channel_id=1, source_target_pairs={{0,4},{4,0},{8,12},{12,8},{1,5},{5,1},{9,13},{13,9},{2,6},{6,2},{1... | collective-permute-start | bytes 393224 | tf_op jit(solution)/shard_map/ppermute | solution.py:253
  12.1 4.7 %copy-start = (bf16[32,2048]{1,0:T(8,128)(2,1)S(1)}, bf16[32,2048]{1,0:T(8,128)(2,1)}, u32[]{:S(2)}) copy-start(bf16[32,2048]{1,0:T(8,128)(2,1)} %refs_1_.12) | copy-start | bytes 393220
  19.9 3.0 %collective-permute-start.3 = (bf16[2,2,32,2304]{3,2,1,0:T(8,128)(2,1)S(1)}, bf16[2,2,32,2304]{3,2,1,0:T(8,128)(2,1)S(1)}, u32[]{:S(2)}, u32[]{:S(2)}) collective-permute-start(bf16[2,2,32,2304]{3,2,1,0:T(8,128)(2,1)S(1)} %get-tuple-element.34.refs_0_), channel_id=1, source_target_pairs={{0,1},{1,0},{2,3},{3,2},{4,5},{5,4},{6,7},{7,6},{8,9},{9,8},{10,11... | collective-permute-start | bytes 1769480 | tf_op jit(solution)/shard_map/ppermute | solution.py:247
  22.4 9.4 %collective-permute-start.4 = (bf16[2,2,32,2048]{3,2,1,0:T(8,128)(2,1)S(1)}, bf16[2,2,32,2048]{3,2,1,0:T(8,128)(2,1)S(1)}, u32[]{:S(2)}, u32[]{:S(2)}) collective-permute-start(bf16[2,2,32,2048]{3,2,1,0:T(8,128)(2,1)S(1)} %get-tuple-element.38.refs_0_), channel_id=1, source_target_pairs={{0,1},{1,0},{2,3},{3,2},{4,5},{5,4},{6,7},{7,6},{8,9},{9,8},{10,11... | collective-permute-start | bytes 1572872 | tf_op jit(solution)/shard_map/ppermute | solution.py:247
  23.1 9.2 %collective-permute-start.5 = (bf16[2,2,16,2304]{3,2,1,0:T(8,128)(2,1)S(1)}, bf16[2,2,16,2304]{3,2,1,0:T(8,128)(2,1)S(1)}, u32[]{:S(2)}, u32[]{:S(2)}) collective-permute-start(bf16[2,2,16,2304]{3,2,1,0:T(8,128)(2,1)S(1)} %get-tuple-element.46), channel_id=1, source_target_pairs={{0,2},{1,3},{2,0},{3,1},{4,6},{5,7},{6,4},{7,5},{8,10},{9,11},{10,... | collective-permute-start | bytes 884744 | tf_op jit(solution)/shard_map/ppermute | solution.py:250
  31.3 3.0 %collective-permute-start.7 = (bf16[1,2,32,2304]{3,2,1,0:T(8,128)(2,1)S(1)}, bf16[1,2,32,2304]{3,2,1,0:T(8,128)(2,1)S(1)}, u32[]{:S(2)}, u32[]{:S(2)}) collective-permute-start(bf16[1,2,32,2304]{3,2,1,0:T(8,128)(2,1)S(1)} %get-tuple-element.48), channel_id=1, source_target_pairs={{0,1},{1,0},{2,3},{3,2},{4,5},{5,4},{6,7},{7,6},{8,9},{9,8},{10,11... | collective-permute-start | bytes 884744 | tf_op jit(solution)/shard_map/ppermute | solution.py:247
  31.4 2.9 %collective-permute-start.6 = (bf16[1,2,32,2304]{3,2,1,0:T(8,128)(2,1)S(1)}, bf16[1,2,32,2304]{3,2,1,0:T(8,128)(2,1)S(1)}, u32[]{:S(2)}, u32[]{:S(2)}) collective-permute-start(bf16[1,2,32,2304]{3,2,1,0:T(8,128)(2,1)S(1)} %get-tuple-element.43.refs_0_), channel_id=1, source_target_pairs={{0,1},{1,0},{2,3},{3,2},{4,5},{5,4},{6,7},{7,6},{8,9},{9,8},{10,11... | collective-permute-start | bytes 884744 | tf_op jit(solution)/shard_map/ppermute | solution.py:247
  31.9 9.2 %collective-permute-start.8 = (bf16[2,2,16,2048]{3,2,1,0:T(8,128)(2,1)S(1)}, bf16[2,2,16,2048]{3,2,1,0:T(8,128)(2,1)S(1)}, u32[]{:S(2)}, u32[]{:S(2)}) collective-permute-start(bf16[2,2,16,2048]{3,2,1,0:T(8,128)(2,1)S(1)} %get-tuple-element.50), channel_id=1, source_target_pairs={{0,2},{1,3},{2,0},{3,1},{4,6},{5,7},{6,4},{7,5},{8,10},{9,11},{10,... | collective-permute-start | bytes 786440 | tf_op jit(solution)/shard_map/ppermute | solution.py:250
  32.5 12.2 %collective-permute-start.9 = (bf16[2,16,2304]{2,1,0:T(8,128)(2,1)S(1)}, bf16[2,16,2304]{2,1,0:T(8,128)(2,1)S(1)}, u32[]{:S(2)}, u32[]{:S(2)}) collective-permute-start(bf16[2,16,2304]{2,1,0:T(8,128)(2,1)S(1)} %hidden_kernel.3.refs_0_.refs_1_), channel_id=1, source_target_pairs={{0,2},{1,3},{2,0},{3,1},{4,6},{5,7},{6,4},{7,5},{8,10},{9,11},{10,... | collective-permute-start | bytes 442376 | tf_op jit(solution)/shard_map/ppermute | solution.py:250
  34.4 16.3 %collective-permute-start.10 = (bf16[2,2,16,2304]{3,2,1,0:T(8,128)(2,1)S(1)}, bf16[2,2,16,2304]{3,2,1,0:T(8,128)(2,1)S(1)}, u32[]{:S(2)}, u32[]{:S(2)}) collective-permute-start(bf16[2,2,16,2304]{3,2,1,0:T(8,128)(2,1)S(1)} %get-tuple-element.51), channel_id=1, source_target_pairs={{0,2},{1,3},{2,0},{3,1},{4,6},{5,7},{6,4},{7,5},{8,10},{9,11},{10,... | collective-permute-start | bytes 884744 | tf_op jit(solution)/shard_map/ppermute | solution.py:250
  44.7 6.4 %collective-permute-start.11 = (bf16[2,2,16,2304]{3,2,1,0:T(8,128)(2,1)S(1)}, bf16[2,2,16,2304]{3,2,1,0:T(8,128)(2,1)S(1)}, u32[]{:S(2)}, u32[]{:S(2)}) collective-permute-start(bf16[2,2,16,2304]{3,2,1,0:T(8,128)(2,1)S(1)} %pack_kernel.3.refs_0_.refs_1_), channel_id=1, source_target_pairs={{0,1},{1,0},{2,3},{3,2},{4,5},{5,4},{6,7},{7,6},{8,9},{9,8},{10,11... | collective-permute-start | bytes 884744 | tf_op jit(solution)/shard_map/ppermute | solution.py:247
  44.8 8.5 %collective-permute-start.12 = (bf16[2,16,2048]{2,1,0:T(8,128)(2,1)S(1)}, bf16[2,16,2048]{2,1,0:T(8,128)(2,1)S(1)}, u32[]{:S(2)}, u32[]{:S(2)}) collective-permute-start(bf16[2,16,2048]{2,1,0:T(8,128)(2,1)S(1)} %hidden_kernel.4.refs_0_.refs_1_), channel_id=1, source_target_pairs={{0,2},{1,3},{2,0},{3,1},{4,6},{5,7},{6,4},{7,5},{8,10},{9,11},{10,... | collective-permute-start | bytes 393224 | tf_op jit(solution)/shard_map/ppermute | solution.py:250
  50.8 5.2 %collective-permute-start.13 = (bf16[2,16,2304]{2,1,0:T(8,128)(2,1)S(1)}, bf16[2,16,2304]{2,1,0:T(8,128)(2,1)S(1)}, u32[]{:S(2)}, u32[]{:S(2)}) collective-permute-start(bf16[2,16,2304]{2,1,0:T(8,128)(2,1)S(1)} %hidden_kernel.5.refs_0_.refs_1_), channel_id=1, source_target_pairs={{0,2},{1,3},{2,0},{3,1},{4,6},{5,7},{6,4},{7,5},{8,10},{9,11},{10,... | collective-permute-start | bytes 442376 | tf_op jit(solution)/shard_map/ppermute | solution.py:250
  53.3 2.8 %collective-permute-start.14 = (bf16[2,2,16,2048]{3,2,1,0:T(8,128)(2,1)S(1)}, bf16[2,2,16,2048]{3,2,1,0:T(8,128)(2,1)S(1)}, u32[]{:S(2)}, u32[]{:S(2)}) collective-permute-start(bf16[2,2,16,2048]{3,2,1,0:T(8,128)(2,1)S(1)} %pack_kernel.4.refs_0_.refs_1_), channel_id=1, source_target_pairs={{0,1},{1,0},{2,3},{3,2},{4,5},{5,4},{6,7},{7,6},{8,9},{9,8},{10,11... | collective-permute-start | bytes 786440 | tf_op jit(solution)/shard_map/ppermute | solution.py:247
  56.0 1.6 %collective-permute-start.15 = (bf16[2,2,16,2304]{3,2,1,0:T(8,128)(2,1)S(1)}, bf16[2,2,16,2304]{3,2,1,0:T(8,128)(2,1)S(1)}, u32[]{:S(2)}, u32[]{:S(2)}) collective-permute-start(bf16[2,2,16,2304]{3,2,1,0:T(8,128)(2,1)S(1)} %pack_kernel.5.refs_0_.refs_1_), channel_id=1, source_target_pairs={{0,1},{1,0},{2,3},{3,2},{4,5},{5,4},{6,7},{7,6},{8,9},{9,8},{10,11... | collective-permute-start | bytes 884744 | tf_op jit(solution)/shard_map/ppermute | solution.py:247
  59.1 8.5 %collective-permute-start.16 = (bf16[32,2816]{1,0:T(8,128)(2,1)S(1)}, bf16[32,2816]{1,0:T(8,128)(2,1)S(1)}, u32[]{:S(2)}, u32[]{:S(2)}) collective-permute-start(bf16[32,2816]{1,0:T(8,128)(2,1)S(1)} %get-tuple-element.53), channel_id=1, source_target_pairs={{0,4},{4,0},{8,12},{12,8},{1,5},{5,1},{9,13},{13,9},{2,6},{6,2},{1... | collective-permute-start | bytes 540680 | tf_op jit(solution)/shard_map/ppermute | solution.py:253
  60.4 10.8 %collective-permute-start.17 = (bf16[32,1280]{1,0:T(8,128)(2,1)S(1)}, bf16[32,1280]{1,0:T(8,128)(2,1)S(1)}, u32[]{:S(2)}, u32[]{:S(2)}) collective-permute-start(bf16[32,1280]{1,0:T(8,128)(2,1)S(1)} %get-tuple-element.55), channel_id=1, source_target_pairs={{0,8},{4,12},{8,0},{12,4},{1,9},{5,13},{9,1},{13,5},{2,10},{6,14},... | collective-permute-start | bytes 245768 | tf_op jit(solution)/shard_map/ppermute | solution.py:253
  63.3 8.0 %collective-permute-start.18 = (bf16[32,1280]{1,0:T(8,128)(2,1)S(1)}, bf16[32,1280]{1,0:T(8,128)(2,1)S(1)}, u32[]{:S(2)}, u32[]{:S(2)}) collective-permute-start(bf16[32,1280]{1,0:T(8,128)(2,1)S(1)} %get-tuple-element.56), channel_id=1, source_target_pairs={{0,12},{4,8},{8,4},{12,0},{1,13},{5,9},{9,5},{13,1},{2,14},{6,10},... | collective-permute-start | bytes 245768 | tf_op jit(solution)/shard_map/ppermute | solution.py:253
  67.6 5.6 %collective-permute-start.19 = (bf16[32,768]{1,0:T(8,128)(2,1)S(1)}, bf16[32,768]{1,0:T(8,128)(2,1)S(1)}, u32[]{:S(2)}, u32[]{:S(2)}) collective-permute-start(bf16[32,768]{1,0:T(8,128)(2,1)S(1)} %pair_sum_kernel.1.refs_0_), channel_id=1, source_target_pairs={{0,8},{4,12},{8,0},{12,4},{1,9},{5,13},{9,1},{13,5},{2,10},{6,14},... | collective-permute-start | bytes 147464 | tf_op jit(solution)/shard_map/ppermute | solution.py:253

commit v6 on v5

--- a/solution.py
+++ b/solution.py
@@ -405,7 +405,7 @@
         w0 = self.fetch(s0, n0)
         w1 = self.fetch(s1, part)
         a0, rest = self.held_gate_up([w0], (s1 + part, n1 - part))
-        a1, w2 = self.held_gate_up([w1, rest], (s2, count * 2 // 26 * step))
+        a1, w2 = self.held_gate_up([w1, rest], (s2, count * 3 // 26 * step))
         b0 = self.chip_sum(both, a0)
         a2 = self.gate_up(s2, n2, w2, 2)
         b1 = self.chip_sum(both, a1)

time: 74.1 us -> 74.4 us (level)
  transfers between devices with their start and end apart: 20 -> 20, of which waited for: 8 -> 9; matrix products, arithmetic and copies ran while one was open for 0% -> 0% of each run, Pallas kernels for 46% -> 46%
where the time goes in v6:
time: 74.4 us; the launch traced here: 74.2 us
  Pallas kernels  39.6 us (53%)
  starting transfers between devices  20.1 us (27%)
  waiting for transfers between devices  14.2 us (19%)
    pallas_call x22, Pallas kernels, call(): pl.pallas_call(run, name=kernel.func.__name__ if isinstance(kernel, funct...  39.6 us
    ppermute x7, starting transfers between devices, along_z(): return lax.ppermute(value, 'hid', [(z, z ^ j) for z in range(self.groups)])  13.6 us
    ppermute x6, waiting for transfers between devices, along_x(): lax.ppermute(value, 'wid', [(w, (w // 2 + j) % self.chips * 2 + w % 2) fo...  7.81 us
    ppermute x7, waiting for transfers between devices, along_z(): return lax.ppermute(value, 'hid', [(z, z ^ j) for z in range(self.groups)])  6.14 us
    ppermute x6, starting transfers between devices, along_x(): lax.ppermute(value, 'wid', [(w, (w // 2 + j) % self.chips * 2 + w % 2) fo...  5.09 us
  transfers between devices with their start and end apart: 20, of which 9 were waited for; matrix products, arithmetic and copies ran while one was open for 0% of the time, Pallas kernels for 46%

profile of v6, /device:TPU:0, one launch (start us, length us, event | category | flops | bytes accessed | tf_op | source)
XLA Modules:
  0.0 74.2 jit_solution(5765826319699836982)
XLA Ops:
  0.0 5.0 %collective-permute-start.2 = (bf16[32,2048]{1,0:T(8,128)(2,1)}, bf16[32,2048]{1,0:T(8,128)(2,1)S(1)}, u32[]{:S(2)}, u32[]{:S(2)}) collective-permute-start(bf16[32,2048]{1,0:T(8,128)(2,1)} %refs_1_.12), channel_id=1, source_target_pairs={{0,12},{4,8},{8,4},{12,0},{1,13},{5,9},{9,5},{13,1},{2,14},{6,10},... | collective-permute-start | bytes 393224 | tf_op jit(solution)/shard_map/ppermute | solution.py:253
  5.1 0.6 collective-permute-start
  5.6 6.5 %fetch_kernel.2 = (bf16[2048,2304]{1,0:T(8,128)(2,1)S(1)}, bf16[2048,2304]{1,0:T(8,128)(2,1)S(1)}) custom-call(bf16[2048,6656]{1,0:T(8,128)(2,1)} %refs_7_.3, bf16[2048,6656]{1,0:T(8,128)(2,1)} %refs_8_.3), custom_call_target="tpu_custom_call" | custom-call | bytes 18874368 | tf_op jit(solution)/shard_map/fetch_kernel/pallas_call | solution.py:233
  12.1 4.7 %fetch_kernel.3 = (bf16[2048,1536]{1,0:T(8,128)(2,1)S(1)}, bf16[2048,1536]{1,0:T(8,128)(2,1)S(1)}) custom-call(bf16[2048,2304]{1,0:T(8,128)(2,1)S(1)} %get-tuple-element.31.refs_0_.refs_5_, bf16[2048,6656]{1,0:T(8,128)(2,1)} %refs_7_.3, bf16[2048,6656]{1,0:T(8,128)(2,1)} %refs_8_.3), custom_call_target="tpu_custom_call" | custom-call | bytes 12582912 | tf_op jit(solution)/shard_map/fetch_kernel/pallas_call | solution.py:233
  16.9 3.1 %held_gate_up_kernel.2 = (bf16[2,2,32,2304]{3,2,1,0:T(8,128)(2,1)S(1)}, f32[2,2,32,2304]{3,2,1,0:T(8,128)S(1)}, bf16[2048,512]{1,0:T(8,128)(2,1)S(1)}, bf16[2048,512]{1,0:T(8,128)(2,1)S(1)}) custom-call(bf16[2048,1536]{1,0:T(8,128)(2,1)S(1)} %get-tuple-element.32.refs_0_.refs_5_, bf16[32,2048]{1,0:T(8,128)(2,1)S(1)} %copy-done, ...), custom_call_target="tpu_custom_call" | custom-call | flops 2415919104 | bytes 262144 | tf_op jit(solution)/shard_map/held_gate_up_kernel/pallas_call | solution.py:233
  20.0 2.9 %held_gate_up_kernel.3 = (bf16[2,2,32,2048]{3,2,1,0:T(8,128)(2,1)S(1)}, f32[2,2,32,2048]{3,2,1,0:T(8,128)S(1)}, bf16[2048,768]{1,0:T(8,128)(2,1)S(1)}, bf16[2048,768]{1,0:T(8,128)(2,1)S(1)}) custom-call(bf16[2,2,32,2304]{3,2,1,0:T(8,128)(2,1)S(1)} %get-tuple-element.34.refs_0_, bf16[32,2048]{1,0:T(8,128)(2,1)S(1)} %copy-done, ...), custom_call_target="tpu_custom_call" | custom-call | flops 2147483648 | bytes 262144 | tf_op jit(solution)/shard_map/held_gate_up_kernel/pallas_call | solution.py:233
  23.0 0.6 collective-permute-start.4
  23.6 1.8 %collective-permute-start.5 = (bf16[2,2,16,2304]{3,2,1,0:T(8,128)(2,1)S(1)}, bf16[2,2,16,2304]{3,2,1,0:T(8,128)(2,1)S(1)}, u32[]{:S(2)}, u32[]{:S(2)}) collective-permute-start(bf16[2,2,16,2304]{3,2,1,0:T(8,128)(2,1)S(1)} %get-tuple-element.46), channel_id=1, source_target_pairs={{0,2},{1,3},{2,0},{3,1},{4,6},{5,7},{6,4},{7,5},{8,10},{9,11},{10,... | collective-permute-start | bytes 884744 | tf_op jit(solution)/shard_map/ppermute | solution.py:250
  25.4 6.1 %gate_up_kernel.1 = (bf16[1,2,32,2304]{3,2,1,0:T(8,128)(2,1)S(1)}, bf16[1,2,32,2304]{3,2,1,0:T(8,128)(2,1)S(1)}, f32[2,2,32,2304]{3,2,1,0:T(8,128)S(1)}) custom-call(f32[2,2,16,2304]{3,2,1,0:T(8,128)S(1)} %get-tuple-element.40.refs_0_.refs_1_, bf16[32,2048]{1,0:T(8,128)(2,1)S(1)} %copy-done, bf16[32,2048]{1,0:T(8,128)(2,1)S(1)} %collective-permute-done.refs_2_, ...), custom_call_target="tpu_custom_call" | custom-call | flops 2415919104 | bytes 18874368 | tf_op jit(solution)/shard_map/gate_up_kernel/pallas_call | solution.py:233
  31.6 0.5 collective-permute-start.6
  32.2 0.4 collective-permute-start.8
  32.8 1.8 %collective-permute-start.9 = (bf16[2,16,2304]{2,1,0:T(8,128)(2,1)S(1)}, bf16[2,16,2304]{2,1,0:T(8,128)(2,1)S(1)}, u32[]{:S(2)}, u32[]{:S(2)}) collective-permute-start(bf16[2,16,2304]{2,1,0:T(8,128)(2,1)S(1)} %hidden_kernel.3.refs_0_.refs_1_), channel_id=1, source_target_pairs={{0,2},{1,3},{2,0},{3,1},{4,6},{5,7},{6,4},{7,5},{8,10},{9,11},{10,... | collective-permute-start | bytes 442376 | tf_op jit(solution)/shard_map/ppermute | solution.py:250
  34.7 0.4 collective-permute-start.10
  35.1 3.7 %fetch_rows_kernel.3.refs_0_.refs_3_ = bf16[2304,2048]{1,0:T(8,128)(2,1)S(1)} custom-call(f32[2,2,16,2304]{3,2,1,0:T(8,128)S(1)} %get-tuple-element.49.refs_0_.refs_1_, bf16[6656,2048]{1,0:T(8,128)(2,1)} %refs_1_.15), custom_call_target="tpu_custom_call" | custom-call | bytes 9437184 | tf_op jit(solution)/shard_map/fetch_rows_kernel/pallas_call | solution.py:233
  38.8 2.7 %collective-permute-done.8.refs_2_ = bf16[2,2,16,2048]{3,2,1,0:T(8,128)(2,1)S(1)} collective-permute-done((bf16[2,2,16,2048]{3,2,1,0:T(8,128)(2,1)S(1)}, bf16[2,2,16,2048]{3,2,1,0:T(8,128)(2,1)S(1)}, u32[]{:S(2)}, u32[]{:S(2)}) %collective-permute-start.8) | collective-permute-done | bytes 262176 | tf_op jit(solution)/shard_map/ppermute | solution.py:250
  41.5 3.4 %fetch_rows_kernel.4.refs_0_.refs_4_ = bf16[2048,2048]{1,0:T(8,128)(2,1)S(1)} custom-call(bf16[2,16,2048]{2,1,0:T(8,128)(2,1)S(1)} %hidden_kernel.4.refs_0_.refs_1_, bf16[6656,2048]{1,0:T(8,128)(2,1)} %refs_1_.15), custom_call_target="tpu_custom_call" | custom-call | bytes 8388608 | tf_op jit(solution)/shard_map/fetch_rows_kernel/pallas_call | solution.py:233
  45.1 0.4 collective-permute-start.12
  45.5 3.7 %fetch_rows_kernel.5.refs_0_.refs_4_ = bf16[2304,2048]{1,0:T(8,128)(2,1)S(1)} custom-call(bf16[2,2,16,2304]{3,2,1,0:T(8,128)(2,1)S(1)} %pack_kernel.3.refs_0_.refs_1_, bf16[6656,2048]{1,0:T(8,128)(2,1)} %refs_1_.15), custom_call_target="tpu_custom_call" | custom-call | bytes 9437184 | tf_op jit(solution)/shard_map/fetch_rows_kernel/pallas_call | solution.py:233
  49.2 1.8 %collective-permute-done.10.refs_2_ = bf16[2,2,16,2304]{3,2,1,0:T(8,128)(2,1)S(1)} collective-permute-done((bf16[2,2,16,2304]{3,2,1,0:T(8,128)(2,1)S(1)}, bf16[2,2,16,2304]{3,2,1,0:T(8,128)(2,1)S(1)}, u32[]{:S(2)}, u32[]{:S(2)}) %collective-permute-start.10) | collective-permute-done | bytes 294944 | tf_op jit(solution)/shard_map/ppermute | solution.py:250
  51.0 0.4 collective-permute-start.13
  51.4 1.4 %down_kernel.3.refs_0_.refs_3_ = f32[128,2048]{1,0:T(8,128)S(1)} custom-call(bf16[2,16,2304]{2,1,0:T(8,128)(2,1)S(1)} %hidden_kernel.5.refs_0_.refs_1_, bf16[2,2,16,2304]{3,2,1,0:T(8,128)(2,1)S(1)} %pack_kernel.3.refs_0_.refs_1_, bf16[2,2,16,2304]{3,2,1,0:T(8,128)(2,1)S(1)} %collective-permute-done.11.refs_2_, ...), custom_call_target="tpu_custom_call" | custom-call | flops 1207959552 | bytes 294912 | tf_op jit(solution)/shard_map/down_kernel/pallas_call | solution.py:233
  52.8 0.7 collective-permute-done.12.refs_2_
  53.6 2.6 %collective-permute-done.13.refs_2_ = bf16[2,16,2304]{2,1,0:T(8,128)(2,1)S(1)} collective-permute-done((bf16[2,16,2304]{2,1,0:T(8,128)(2,1)S(1)}, bf16[2,16,2304]{2,1,0:T(8,128)(2,1)S(1)}, u32[]{:S(2)}, u32[]{:S(2)}) %collective-permute-start.13) | collective-permute-done | bytes 147488 | tf_op jit(solution)/shard_map/ppermute | solution.py:250
  56.4 1.3 %down_kernel.4.refs_0_.refs_3_ = f32[128,2048]{1,0:T(8,128)S(1)} custom-call(bf16[2,2,16,2304]{3,2,1,0:T(8,128)(2,1)S(1)} %pack_kernel.5.refs_0_.refs_1_, bf16[2,2,16,2048]{3,2,1,0:T(8,128)(2,1)S(1)} %pack_kernel.4.refs_0_.refs_1_, bf16[2,2,16,2048]{3,2,1,0:T(8,128)(2,1)S(1)} %collective-permute-done.14.refs_2_, f32[128,2048]{1,0:T(8,128)S(1)} %down_kernel.3.refs_0_.refs_3_, ...), custom_call_target="tpu_custom_call" | custom-call | flops 1073741824 | bytes 262144 | tf_op jit(solution)/shard_map/down_kernel/pallas_call | solution.py:233
  57.7 0.3 collective-permute-done.15.refs_2_
  57.9 1.4 %down_kernel.5 = (f32[32,2048]{1,0:T(8,128)S(1)}, bf16[32,2816]{1,0:T(8,128)(2,1)S(1)}, bf16[32,1280]{1,0:T(8,128)(2,1)S(1)}, bf16[32,1280]{1,0:T(8,128)(2,1)S(1)}, f32[32,768]{1,0:T(8,128)S(1)}) custom-call(f32[128,2048]{1,0:T(8,128)S(1)} %down_kernel.4.refs_0_.refs_3_, bf16[2,2,16,2304]{3,2,1,0:T(8,128)(2,1)S(1)} %pack_kernel.5.refs_0_.refs_1_, ...), custom_call_target="tpu_custom_call" | custom-call | flops 1207959552 | bytes 294912 | tf_op jit(solution)/shard_map/down_kernel/pallas_call | solution.py:233
  59.3 1.3 %collective-permute-start.16 = (bf16[32,2816]{1,0:T(8,128)(2,1)S(1)}, bf16[32,2816]{1,0:T(8,128)(2,1)S(1)}, u32[]{:S(2)}, u32[]{:S(2)}) collective-permute-start(bf16[32,2816]{1,0:T(8,128)(2,1)S(1)} %get-tuple-element.53), channel_id=1, source_target_pairs={{0,4},{4,0},{8,12},{12,8},{1,5},{5,1},{9,13},{13,9},{2,6},{6,2},{1... | collective-permute-start | bytes 540680 | tf_op jit(solution)/shard_map/ppermute | solution.py:253
  60.6 2.9 %collective-permute-start.17 = (bf16[32,1280]{1,0:T(8,128)(2,1)S(1)}, bf16[32,1280]{1,0:T(8,128)(2,1)S(1)}, u32[]{:S(2)}, u32[]{:S(2)}) collective-permute-start(bf16[32,1280]{1,0:T(8,128)(2,1)S(1)} %get-tuple-element.55), channel_id=1, source_target_pairs={{0,8},{4,12},{8,0},{12,4},{1,9},{5,13},{9,1},{13,5},{2,10},{6,14},... | collective-permute-start | bytes 245768 | tf_op jit(solution)/shard_map/ppermute | solution.py:253
  63.8 4.1 %collective-permute-done.16.refs_1_.refs_2_ = bf16[32,2816]{1,0:T(8,128)(2,1)S(1)} collective-permute-done((bf16[32,2816]{1,0:T(8,128)(2,1)S(1)}, bf16[32,2816]{1,0:T(8,128)(2,1)S(1)}, u32[]{:S(2)}, u32[]{:S(2)}) %collective-permute-start.16) | collective-permute-done | bytes 180256 | tf_op jit(solution)/shard_map/ppermute | solution.py:253
  67.9 3.5 %collective-permute-start.19 = (bf16[32,768]{1,0:T(8,128)(2,1)S(1)}, bf16[32,768]{1,0:T(8,128)(2,1)S(1)}, u32[]{:S(2)}, u32[]{:S(2)}) collective-permute-start(bf16[32,768]{1,0:T(8,128)(2,1)S(1)} %pair_sum_kernel.1.refs_0_), channel_id=1, source_target_pairs={{0,8},{4,12},{8,0},{12,4},{1,9},{5,13},{9,1},{13,5},{2,10},{6,14},... | collective-permute-start | bytes 147464 | tf_op jit(solution)/shard_map/ppermute | solution.py:253
  71.5 1.9 %collective-permute-done.19.refs_5_ = bf16[32,768]{1,0:T(8,128)(2,1)S(1)} collective-permute-done((bf16[32,768]{1,0:T(8,128)(2,1)S(1)}, bf16[32,768]{1,0:T(8,128)(2,1)S(1)}, u32[]{:S(2)}, u32[]{:S(2)}) %collective-permute-start.19) | collective-permute-done | bytes 49184 | tf_op jit(solution)/shard_map/ppermute | solution.py:253
  73.5 0.7 final_kernel.1
  (32 shorter events, 1.6 us)
Async XLA Ops:
  0.0 16.8 %collective-permute-start.2 = (bf16[32,2048]{1,0:T(8,128)(2,1)}, bf16[32,2048]{1,0:T(8,128)(2,1)S(1)}, u32[]{:S(2)}, u32[]{:S(2)}) collective-permute-start(bf16[32,2048]{1,0:T(8,128)(2,1)} %refs_1_.12), channel_id=1, source_target_pairs={{0,12},{4,8},{8,4},{12,0},{1,13},{5,9},{9,5},{13,1},{2,14},{6,10},... | collective-permute-start | bytes 393224 | tf_op jit(solution)/shard_map/ppermute | solution.py:253
  5.0 11.8 %collective-permute-start.1 = (bf16[32,2048]{1,0:T(8,128)(2,1)}, bf16[32,2048]{1,0:T(8,128)(2,1)S(1)}, u32[]{:S(2)}, u32[]{:S(2)}) collective-permute-start(bf16[32,2048]{1,0:T(8,128)(2,1)} %refs_1_.12), channel_id=1, source_target_pairs={{0,8},{4,12},{8,0},{12,4},{1,9},{5,13},{9,1},{13,5},{2,10},{6,14},... | collective-permute-start | bytes 393224 | tf_op jit(solution)/shard_map/ppermute | solution.py:253
  5.1 11.8 %collective-permute-start = (bf16[32,2048]{1,0:T(8,128)(2,1)}, bf16[32,2048]{1,0:T(8,128)(2,1)S(1)}, u32[]{:S(2)}, u32[]{:S(2)}) collective-permute-start(bf16[32,2048]{1,0:T(8,128)(2,1)} %refs_1_.12), channel_id=1, source_target_pairs={{0,4},{4,0},{8,12},{12,8},{1,5},{5,1},{9,13},{13,9},{2,6},{6,2},{1... | collective-permute-start | bytes 393224 | tf_op jit(solution)/shard_map/ppermute | solution.py:253
  12.1 4.7 %copy-start = (bf16[32,2048]{1,0:T(8,128)(2,1)S(1)}, bf16[32,2048]{1,0:T(8,128)(2,1)}, u32[]{:S(2)}) copy-start(bf16[32,2048]{1,0:T(8,128)(2,1)} %refs_1_.12) | copy-start | bytes 393220
  19.9 3.6 %collective-permute-start.3 = (bf16[2,2,32,2304]{3,2,1,0:T(8,128)(2,1)S(1)}, bf16[2,2,32,2304]{3,2,1,0:T(8,128)(2,1)S(1)}, u32[]{:S(2)}, u32[]{:S(2)}) collective-permute-start(bf16[2,2,32,2304]{3,2,1,0:T(8,128)(2,1)S(1)} %get-tuple-element.34.refs_0_), channel_id=1, source_target_pairs={{0,1},{1,0},{2,3},{3,2},{4,5},{5,4},{6,7},{7,6},{8,9},{9,8},{10,11... | collective-permute-start | bytes 1769480 | tf_op jit(solution)/shard_map/ppermute | solution.py:247
  23.0 9.2 %collective-permute-start.4 = (bf16[2,2,32,2048]{3,2,1,0:T(8,128)(2,1)S(1)}, bf16[2,2,32,2048]{3,2,1,0:T(8,128)(2,1)S(1)}, u32[]{:S(2)}, u32[]{:S(2)}) collective-permute-start(bf16[2,2,32,2048]{3,2,1,0:T(8,128)(2,1)S(1)} %get-tuple-element.38.refs_0_), channel_id=1, source_target_pairs={{0,1},{1,0},{2,3},{3,2},{4,5},{5,4},{6,7},{7,6},{8,9},{9,8},{10,11... | collective-permute-start | bytes 1572872 | tf_op jit(solution)/shard_map/ppermute | solution.py:247
  23.6 9.0 %collective-permute-start.5 = (bf16[2,2,16,2304]{3,2,1,0:T(8,128)(2,1)S(1)}, bf16[2,2,16,2304]{3,2,1,0:T(8,128)(2,1)S(1)}, u32[]{:S(2)}, u32[]{:S(2)}) collective-permute-start(bf16[2,2,16,2304]{3,2,1,0:T(8,128)(2,1)S(1)} %get-tuple-element.46), channel_id=1, source_target_pairs={{0,2},{1,3},{2,0},{3,1},{4,6},{5,7},{6,4},{7,5},{8,10},{9,11},{10,... | collective-permute-start | bytes 884744 | tf_op jit(solution)/shard_map/ppermute | solution.py:250
  31.5 3.0 %collective-permute-start.7 = (bf16[1,2,32,2304]{3,2,1,0:T(8,128)(2,1)S(1)}, bf16[1,2,32,2304]{3,2,1,0:T(8,128)(2,1)S(1)}, u32[]{:S(2)}, u32[]{:S(2)}) collective-permute-start(bf16[1,2,32,2304]{3,2,1,0:T(8,128)(2,1)S(1)} %get-tuple-element.48), channel_id=1, source_target_pairs={{0,1},{1,0},{2,3},{3,2},{4,5},{5,4},{6,7},{7,6},{8,9},{9,8},{10,11... | collective-permute-start | bytes 884744 | tf_op jit(solution)/shard_map/ppermute | solution.py:247
  31.6 2.9 %collective-permute-start.6 = (bf16[1,2,32,2304]{3,2,1,0:T(8,128)(2,1)S(1)}, bf16[1,2,32,2304]{3,2,1,0:T(8,128)(2,1)S(1)}, u32[]{:S(2)}, u32[]{:S(2)}) collective-permute-start(bf16[1,2,32,2304]{3,2,1,0:T(8,128)(2,1)S(1)} %get-tuple-element.43.refs_0_), channel_id=1, source_target_pairs={{0,1},{1,0},{2,3},{3,2},{4,5},{5,4},{6,7},{7,6},{8,9},{9,8},{10,11... | collective-permute-start | bytes 884744 | tf_op jit(solution)/shard_map/ppermute | solution.py:247
  32.2 9.2 %collective-permute-start.8 = (bf16[2,2,16,2048]{3,2,1,0:T(8,128)(2,1)S(1)}, bf16[2,2,16,2048]{3,2,1,0:T(8,128)(2,1)S(1)}, u32[]{:S(2)}, u32[]{:S(2)}) collective-permute-start(bf16[2,2,16,2048]{3,2,1,0:T(8,128)(2,1)S(1)} %get-tuple-element.50), channel_id=1, source_target_pairs={{0,2},{1,3},{2,0},{3,1},{4,6},{5,7},{6,4},{7,5},{8,10},{9,11},{10,... | collective-permute-start | bytes 786440 | tf_op jit(solution)/shard_map/ppermute | solution.py:250
  32.8 12.2 %collective-permute-start.9 = (bf16[2,16,2304]{2,1,0:T(8,128)(2,1)S(1)}, bf16[2,16,2304]{2,1,0:T(8,128)(2,1)S(1)}, u32[]{:S(2)}, u32[]{:S(2)}) collective-permute-start(bf16[2,16,2304]{2,1,0:T(8,128)(2,1)S(1)} %hidden_kernel.3.refs_0_.refs_1_), channel_id=1, source_target_pairs={{0,2},{1,3},{2,0},{3,1},{4,6},{5,7},{6,4},{7,5},{8,10},{9,11},{10,... | collective-permute-start | bytes 442376 | tf_op jit(solution)/shard_map/ppermute | solution.py:250
  34.7 16.2 %collective-permute-start.10 = (bf16[2,2,16,2304]{3,2,1,0:T(8,128)(2,1)S(1)}, bf16[2,2,16,2304]{3,2,1,0:T(8,128)(2,1)S(1)}, u32[]{:S(2)}, u32[]{:S(2)}) collective-permute-start(bf16[2,2,16,2304]{3,2,1,0:T(8,128)(2,1)S(1)} %get-tuple-element.51), channel_id=1, source_target_pairs={{0,2},{1,3},{2,0},{3,1},{4,6},{5,7},{6,4},{7,5},{8,10},{9,11},{10,... | collective-permute-start | bytes 884744 | tf_op jit(solution)/shard_map/ppermute | solution.py:250
  45.0 6.4 %collective-permute-start.11 = (bf16[2,2,16,2304]{3,2,1,0:T(8,128)(2,1)S(1)}, bf16[2,2,16,2304]{3,2,1,0:T(8,128)(2,1)S(1)}, u32[]{:S(2)}, u32[]{:S(2)}) collective-permute-start(bf16[2,2,16,2304]{3,2,1,0:T(8,128)(2,1)S(1)} %pack_kernel.3.refs_0_.refs_1_), channel_id=1, source_target_pairs={{0,1},{1,0},{2,3},{3,2},{4,5},{5,4},{6,7},{7,6},{8,9},{9,8},{10,11... | collective-permute-start | bytes 884744 | tf_op jit(solution)/shard_map/ppermute | solution.py:247
  45.1 8.4 %collective-permute-start.12 = (bf16[2,16,2048]{2,1,0:T(8,128)(2,1)S(1)}, bf16[2,16,2048]{2,1,0:T(8,128)(2,1)S(1)}, u32[]{:S(2)}, u32[]{:S(2)}) collective-permute-start(bf16[2,16,2048]{2,1,0:T(8,128)(2,1)S(1)} %hidden_kernel.4.refs_0_.refs_1_), channel_id=1, source_target_pairs={{0,2},{1,3},{2,0},{3,1},{4,6},{5,7},{6,4},{7,5},{8,10},{9,11},{10,... | collective-permute-start | bytes 393224 | tf_op jit(solution)/shard_map/ppermute | solution.py:250
  51.0 5.2 %collective-permute-start.13 = (bf16[2,16,2304]{2,1,0:T(8,128)(2,1)S(1)}, bf16[2,16,2304]{2,1,0:T(8,128)(2,1)S(1)}, u32[]{:S(2)}, u32[]{:S(2)}) collective-permute-start(bf16[2,16,2304]{2,1,0:T(8,128)(2,1)S(1)} %hidden_kernel.5.refs_0_.refs_1_), channel_id=1, source_target_pairs={{0,2},{1,3},{2,0},{3,1},{4,6},{5,7},{6,4},{7,5},{8,10},{9,11},{10,... | collective-permute-start | bytes 442376 | tf_op jit(solution)/shard_map/ppermute | solution.py:250
  53.5 2.8 %collective-permute-start.14 = (bf16[2,2,16,2048]{3,2,1,0:T(8,128)(2,1)S(1)}, bf16[2,2,16,2048]{3,2,1,0:T(8,128)(2,1)S(1)}, u32[]{:S(2)}, u32[]{:S(2)}) collective-permute-start(bf16[2,2,16,2048]{3,2,1,0:T(8,128)(2,1)S(1)} %pack_kernel.4.refs_0_.refs_1_), channel_id=1, source_target_pairs={{0,1},{1,0},{2,3},{3,2},{4,5},{5,4},{6,7},{7,6},{8,9},{9,8},{10,11... | collective-permute-start | bytes 786440 | tf_op jit(solution)/shard_map/ppermute | solution.py:247
  56.3 1.6 %collective-permute-start.15 = (bf16[2,2,16,2304]{3,2,1,0:T(8,128)(2,1)S(1)}, bf16[2,2,16,2304]{3,2,1,0:T(8,128)(2,1)S(1)}, u32[]{:S(2)}, u32[]{:S(2)}) collective-permute-start(bf16[2,2,16,2304]{3,2,1,0:T(8,128)(2,1)S(1)} %pack_kernel.5.refs_0_.refs_1_), channel_id=1, source_target_pairs={{0,1},{1,0},{2,3},{3,2},{4,5},{5,4},{6,7},{7,6},{8,9},{9,8},{10,11... | collective-permute-start | bytes 884744 | tf_op jit(solution)/shard_map/ppermute | solution.py:247
  59.3 8.5 %collective-permute-start.16 = (bf16[32,2816]{1,0:T(8,128)(2,1)S(1)}, bf16[32,2816]{1,0:T(8,128)(2,1)S(1)}, u32[]{:S(2)}, u32[]{:S(2)}) collective-permute-start(bf16[32,2816]{1,0:T(8,128)(2,1)S(1)} %get-tuple-element.53), channel_id=1, source_target_pairs={{0,4},{4,0},{8,12},{12,8},{1,5},{5,1},{9,13},{13,9},{2,6},{6,2},{1... | collective-permute-start | bytes 540680 | tf_op jit(solution)/shard_map/ppermute | solution.py:253
  60.6 10.8 %collective-permute-start.17 = (bf16[32,1280]{1,0:T(8,128)(2,1)S(1)}, bf16[32,1280]{1,0:T(8,128)(2,1)S(1)}, u32[]{:S(2)}, u32[]{:S(2)}) collective-permute-start(bf16[32,1280]{1,0:T(8,128)(2,1)S(1)} %get-tuple-element.55), channel_id=1, source_target_pairs={{0,8},{4,12},{8,0},{12,4},{1,9},{5,13},{9,1},{13,5},{2,10},{6,14},... | collective-permute-start | bytes 245768 | tf_op jit(solution)/shard_map/ppermute | solution.py:253
  63.5 8.0 %collective-permute-start.18 = (bf16[32,1280]{1,0:T(8,128)(2,1)S(1)}, bf16[32,1280]{1,0:T(8,128)(2,1)S(1)}, u32[]{:S(2)}, u32[]{:S(2)}) collective-permute-start(bf16[32,1280]{1,0:T(8,128)(2,1)S(1)} %get-tuple-element.56), channel_id=1, source_target_pairs={{0,12},{4,8},{8,4},{12,0},{1,13},{5,9},{9,5},{13,1},{2,14},{6,10},... | collective-permute-start | bytes 245768 | tf_op jit(solution)/shard_map/ppermute | solution.py:253
  67.9 5.6 %collective-permute-start.19 = (bf16[32,768]{1,0:T(8,128)(2,1)S(1)}, bf16[32,768]{1,0:T(8,128)(2,1)S(1)}, u32[]{:S(2)}, u32[]{:S(2)}) collective-permute-start(bf16[32,768]{1,0:T(8,128)(2,1)S(1)} %pair_sum_kernel.1.refs_0_), channel_id=1, source_target_pairs={{0,8},{4,12},{8,0},{12,4},{1,9},{5,13},{9,1},{13,5},{2,10},{6,14},... | collective-permute-start | bytes 147464 | tf_op jit(solution)/shard_map/ppermute | solution.py:253
